TPU v7x, 1024 devices: a whole 4x4x32 slice. The times are simulated.
1024 devices in a mesh: ctx: 16 (over z_lo), exp: 64 (over x, z_hi, y, core).
Axes of the slice: x: 4, y: 4, z: 32 (z_hi: 2, z_lo: 16; z = z_hi * 16 + z_lo), core: 2. Of those that a mesh axis runs over, the one named last changes fastest.
Arguments:
- queries: bfloat16 [2048, 8192], P('ctx', 'exp'), may hold values from -8 to 8
- keys_values: bfloat16 [2048, 1024], P('ctx'), may hold values from -8 to 8
- residual: bfloat16 [2048, 4096], P(('ctx', 'exp')), may hold values from -1.1953125 to 1.1953125
- norm_gain: float32 [4096], replicated, may hold values from 0.5 to 1.5
- out_weight: bfloat16 [8192, 4096], P('exp'), may hold values from -0.0625 to 0.0625
- expert_ids: int32 [2048, 8], P('exp'), may hold values from 0 to 63, all different within a row; in each aligned block of 32 rows (0 to 31, 32 to 63, ...) at most 5 rows name the same one
- gate_values: float32 [2048, 8], P('exp'), may hold values from 0.1 to 1
- gate_up_weight: bfloat16 [64, 4096, 3072], P('exp', 'ctx'), may hold values from -0.09375 to 0.09375
- down_weight: bfloat16 [64, 1536, 4096], P('exp', None, 'ctx'), may hold values from -0.15625 to 0.15625
Outputs:
- layer_out: bfloat16 [2048, 4096], P('exp', 'ctx')
Inputs may be any that keep to these rules, and one draw needn't show every extreme that they name: `expert_ids`: in the 32 rows of one routing group no expert is chosen more than 5 times.
All inputs are finite; a program needn't handle non-finite values.
Results may differ from a plain program's by a relative error of at most 0.033.
Values may be sent and summed in bfloat16 or wider, within the bound.
No kernel may reach another device: no remote copies, remote signals or barrier semaphores. Data moves between devices by JAX's collectives and lax.ppermute only.
A program may use at most 32 MiB of HBM per device.

v0:
```python
import jax
import jax.numpy as jnp
from jax import lax
from jax.sharding import PartitionSpec as P

HEADS = 64
KV_HEADS = 4
HD = 128
FFE = 1536
TOPK = 8
EXPERTS = 64


masked_score = -1e30


def shards(
    queries,
    keys_values,
    residual,
    norm_gain,
    out_weight,
    expert_ids,
    gate_values,
    gate_up_weight,
    down_weight,
):
    exp_index = lax.axis_index("exp")
    ctx_index = lax.axis_index("ctx")
    row_count = queries.shape[0]
    local_heads = queries.shape[1] // HD
    group_size = HEADS // KV_HEADS
    kv_index = exp_index * local_heads // group_size
    key_block = lax.dynamic_slice_in_dim(keys_values, kv_index * HD, HD, 1)
    value_block = lax.dynamic_slice_in_dim(keys_values, KV_HEADS * HD + kv_index * HD, HD, 1)
    key_value = jnp.concatenate([key_block, value_block], axis=1)
    query_heads = queries.reshape(row_count, local_heads, HD).transpose(1, 0, 2)
    query_pos = ctx_index * row_count + jnp.arange(row_count, dtype=jnp.int32)
    scaling = HD ** (-0.5)
    segment = lax.all_gather(key_value, "ctx", axis=0, tiled=True)
    running_max = jnp.full((local_heads, row_count), masked_score, jnp.float32)
    key_part = segment[:, :HD]
    value_part = segment[:, HD:]
    scores = (
        jnp.einsum("hqd,kd->hqk", query_heads, key_part, preferred_element_type=jnp.float32)
        * scaling
    )
    key_pos = jnp.arange(segment.shape[0], dtype=jnp.int32)
    allowed = key_pos[None, :] <= query_pos[:, None]
    scores = jnp.where(allowed[None], scores, masked_score)
    new_max = jnp.maximum(running_max, jnp.max(scores, axis=-1))
    weights = jnp.where(allowed[None], jnp.exp(scores - new_max[:, :, None]), 0.0)
    new_sum = jnp.sum(weights, axis=-1)
    update = jnp.einsum(
        "hqk,kd->hqd", weights.astype(jnp.bfloat16), value_part, preferred_element_type=jnp.float32
    )
    attended = (update / new_sum[:, :, None]).astype(jnp.bfloat16)
    attended = attended.transpose(1, 0, 2).reshape(row_count, local_heads * HD)
    attn_rows = lax.psum_scatter(
        jnp.dot(attended, out_weight, preferred_element_type=jnp.float32),
        "exp",
        scatter_dimension=0,
        tiled=True,
    )
    hidden_state = (residual.astype(jnp.float32) + attn_rows).astype(jnp.bfloat16)
    widened = hidden_state.astype(jnp.float32)
    mean_square = jnp.mean(widened * widened, axis=-1, keepdims=True)
    normed = (widened * lax.rsqrt(mean_square + 1e-06) * norm_gain).astype(jnp.bfloat16)
    hidden_cols, normed_cols = (
        lax.all_to_all(hidden_state, "ctx", split_axis=1, concat_axis=0, tiled=True),
        lax.all_to_all(normed, "ctx", split_axis=1, concat_axis=0, tiled=True),
    )
    token_count = normed_cols.shape[0]
    capacity = min(token_count, token_count * TOPK * 5 // (4 * EXPERTS))
    picked = expert_ids[:, :, None] == jnp.arange(EXPERTS, dtype=jnp.int32)[None, None, :]
    chosen = jnp.sum(picked.astype(jnp.int32), axis=1)
    slot_index = jnp.cumsum(chosen, axis=0, dtype=jnp.int32) - chosen
    gate_table = jnp.sum(jnp.where(picked, gate_values[:, :, None], 0.0), axis=1)
    placed = (chosen[:, :, None] > 0) & (
        slot_index[:, :, None] == jnp.arange(capacity, dtype=jnp.int32)[None, None, :]
    )
    placed_flat = placed.reshape(token_count, EXPERTS * capacity)
    buckets = jnp.einsum(
        "ts,td->sd",
        placed_flat.astype(jnp.bfloat16),
        normed_cols,
        preferred_element_type=jnp.float32,
    )
    buckets = buckets.astype(jnp.bfloat16).reshape(EXPERTS, capacity, normed_cols.shape[1])
    arrived = lax.all_to_all(buckets, "exp", split_axis=0, concat_axis=1, tiled=True)
    local_experts, slot_total, feature_count = arrived.shape
    partial_gate = jnp.einsum(
        "esd,edf->esf", arrived, gate_up_weight, preferred_element_type=jnp.float32
    )
    flat_terms = partial_gate.reshape(local_experts * slot_total, 2 * FFE)
    summed = lax.psum_scatter(
        flat_terms.astype(jnp.bfloat16), "ctx", scatter_dimension=0, tiled=True
    ).astype(jnp.float32)
    activated = (jax.nn.silu(summed[:, :FFE]) * summed[:, FFE:]).astype(jnp.bfloat16)
    activated = lax.all_gather(activated, "ctx", axis=0, tiled=True).reshape(
        local_experts, slot_total, FFE
    )
    expert_out = jnp.einsum(
        "esf,efd->esd", activated, down_weight, preferred_element_type=jnp.float32
    ).astype(jnp.bfloat16)
    returned = lax.all_to_all(expert_out, "exp", split_axis=1, concat_axis=0, tiled=True)
    combine = (gate_table[:, :, None] * placed.astype(jnp.float32)).reshape(
        token_count, EXPERTS * capacity
    )
    mixed_rows = jnp.dot(
        combine,
        returned.reshape(EXPERTS * capacity, feature_count).astype(jnp.float32),
        precision=lax.Precision.HIGHEST,
    )
    return (hidden_cols.astype(jnp.float32) + mixed_rows).astype(jnp.bfloat16)


def solution(mesh):
    in_specs = (
        P("ctx", "exp"),
        P("ctx", None),
        P(("ctx", "exp"), None),
        P(),
        P("exp", None),
        P("exp", None),
        P("exp", None),
        P("exp", "ctx", None),
        P("exp", None, "ctx"),
    )
    out_specs = P("exp", "ctx")
    return jax.shard_map(shards, mesh=mesh, in_specs=in_specs, out_specs=out_specs, check_vma=False)
```

profile of v0, /device:TPU:1, one launch (start us, length us, event | category | flops | bytes accessed | tf_op | source)
XLA Modules:
  0.0 2266.8 jit_solution(8046548486949522861)
XLA Ops:
  6.5 0.9 constant_dynamic-slice_fusion.1
  7.4 0.6 pad_maximum_fusion
  8.2 184.1 %all-gather.3.cloned.1.call-done = bf16[2048,256]{1,0:T(8,128)(2,1)} async-done(((bf16[128,256]{1,0:T(8,128)(2,1)}), bf16[2048,256]{1,0:T(8,128)(2,1)}) %all-gather.3.cloned.1.call-update) | async-done | bytes 1048592 | tf_op jit(solution)/shard_map/all_gather | solution.py:40
  192.2 1.5 fusion.35
  194.0 3.5 fusion.6
  197.6 0.6 copy-done.9
  198.7 1.3 dynamic-slice
  200.6 1680.0 %all-reduce.5.cloned.1.call-done = f32[128,4096]{1,0:T(8,128)} async-done(((f32[128,4096]{1,0:T(8,128)}), f32[128,4096]{1,0:T(8,128)}) %all-reduce.5.cloned.1.call-update) | async-done | bytes 2097168
  1880.6 1.1 fusion.27
  1881.7 0.7 fusion.29
  1882.4 3.5 all-to-all-start.1
  1886.1 18.6 all-to-all-done.1
  1905.0 54.7 %all_to_all.50 = bf16[64,5,256]{2,1,0:T(8,128)(2,1)S(1)} all-to-all(bf16[64,5,256]{2,1,0:T(8,128)(2,1)S(1)} %reshape.175), channel_id=1, replica_groups=mesh['ctx'=16,'exp'=64] {'exp'}, dimensions={0} | all-to-all | bytes 327680 | tf_op jit(solution)/shard_map/all_to_all | solution.py:90
  1959.7 0.7 reshape.176
  1960.4 1.6 convolution_convert_fusion
  1962.0 119.3 %fusion = bf16[24,3072]{1,0:T(8,128)(2,1)} fusion(bf16[320,3072]{1,0:T(8,128)(2,1)S(1)} %convolution_convert_fusion), kind=kCustom, calls=%all-reduce-scatter | all-reduce-scatter fusion | flops 1179649 | bytes 2117632
  2081.4 1.3 collective-permute-start
  2082.7 1.3 collective-permute-start.1
  2084.0 0.9 slice.20
  2084.9 1.3 collective-permute-start.2
  2086.2 1.3 dynamic-slice.6
  2088.2 4.2 all-to-all-start
  2092.4 2.5 concatenate.4
  2094.9 109.0 %all-gather = bf16[16,20,1536]{2,1,0:T(8,128)(2,1)S(1)} all-gather(bf16[1,20,1536]{2,1,0:T(8,128)(2,1)S(1)} %fusion.26), channel_id=1, replica_groups=mesh['ctx'=16,'exp'=64] {'ctx'}, dimensions={0}, use_global_device_ids=true | all-gather | bytes 1044480 | tf_op jit(solution)/shard_map/all_gather | solution.py:100
  2204.0 1.1 reshape.182
  2205.1 1.7 fusion.4
  2207.6 1.6 reduce.4
  2209.2 0.8 reshape.185
  2209.9 21.8 all-to-all-start.3
  2232.2 0.7 convert_bitcast_fusion
  2233.0 26.0 %all-to-all-done.3 = bf16[64,2,640]{2,1,0:T(2,128)(2,1)S(1)} async-done(((bf16[64,2,640]{2,1,0:T(2,128)(2,1)}), bf16[64,2,640]{2,1,0:T(2,128)(2,1)S(1)}, u32[]{:S(2)}, u32[]{:S(2)}) %all-to-all-start.3) | async-done | bytes 163872 | tf_op jit(solution)/shard_map/all_to_all | solution.py:106
  2259.0 0.9 fusion.7
  (56 shorter events, 2.7 us)
Async XLA Ops:
  6.5 1953.9 %copy-start = (bf16[1,256,3072]{2,1,0:T(8,128)(2,1)S(1)}, bf16[1,256,3072]{2,1,0:T(8,128)(2,1)}, u32[]{:S(2)}) copy-start(bf16[1,256,3072]{2,1,0:T(8,128)(2,1)} %param.16) | copy-start | bytes 4718596
  6.5 185.7 %all-gather.3.cloned.1.call-start = ((), (), s32[]{:S(2)}) async-start(), calls=%async_computation.4 | async-start | bytes 1114112 | tf_op jit(solution)/shard_map/all_gather | solution.py:40
  8.1 1872.6 %all-reduce.5.cloned.1.call-start = ((), (), s32[]{:S(2)}) async-start(), calls=%async_computation.5 | async-start | bytes 4194304
  197.5 0.7 copy-start.9
  197.5 1683.1 %copy-start.8 = (bf16[2,4096]{1,0:T(2,128)(2,1)S(1)}, bf16[2,4096]{1,0:T(2,128)(2,1)}, u32[]{:S(2)}) copy-start(bf16[2,4096]{1,0:T(2,128)(2,1)} %param.11) | copy-start | bytes 49156
  197.5 1684.2 %copy-start.7 = (f32[4096]{0:T(1024)S(1)}, f32[4096]{0:T(1024)}, u32[]{:S(2)}) copy-start(f32[4096]{0:T(1024)} %param.12) | copy-start | bytes 49156
  198.5 1706.2 %copy-start.2 = (s32[32,64]{0,1:T(8,128)}, s32[32,64]{0,1:T(8,128)S(1)}, u32[]{:S(2)}) copy-start(s32[32,64]{0,1:T(8,128)S(1)} %copy.36) | copy-start | bytes 24580
  198.7 1687.2 %copy-start.5 = (pred[32,64]{0,1:T(8,128)(4,1)}, pred[32,64]{0,1:T(8,128)(4,1)S(1)}, u32[]{:S(2)}) copy-start(pred[32,64]{0,1:T(8,128)(4,1)S(1)} %copy.35) | copy-start | bytes 6148
  1881.7 0.7 copy-start.4
  1882.4 22.3 all-to-all-start.1
  2081.4 11.0 collective-permute-start
  2082.7 9.7 collective-permute-start.1
  2084.9 7.4 collective-permute-start.2
  2088.2 121.8 %all-to-all-start = ((bf16[2,16,256]{2,0,1:T(2,128)(2,1)}), bf16[2,16,256]{2,0,1:T(2,128)(2,1)}, u32[]{:S(2)}, u32[]{:S(2)}) async-start(bf16[2,16,256]{2,0,1:T(2,128)(2,1)} %bitcast.43), calls=%async_computation | async-start | bytes 32768 | tf_op jit(solution)/shard_map/all_to_all | solution.py:70
  2094.9 110.2 %copy-start.1 = (bf16[1,1536,256]{2,1,0:T(8,128)(2,1)S(1)}, bf16[1,1536,256]{2,1,0:T(8,128)(2,1)}, u32[]{:S(2)}) copy-start(bf16[1,1536,256]{2,1,0:T(8,128)(2,1)} %param.17) | copy-start | bytes 2359300
  2205.1 26.7 %copy-start.10 = (f32[32,8]{0,1:T(8,128)S(1)}, f32[32,8]{0,1:T(8,128)}, u32[]{:S(2)}) copy-start(f32[32,8]{0,1:T(8,128)} %param.15) | copy-start | bytes 3076
  2205.1 27.0 %copy-start.3 = (s32[32,64]{0,1:T(8,128)S(1)}, s32[32,64]{0,1:T(8,128)}, u32[]{:S(2)}) copy-start(s32[32,64]{0,1:T(8,128)} %copy-done.2) | copy-start | bytes 24580
  2205.1 27.0 %copy-start.6 = (pred[32,64]{0,1:T(8,128)(4,1)S(1)}, pred[32,64]{0,1:T(8,128)(4,1)}, u32[]{:S(2)}) copy-start(pred[32,64]{0,1:T(8,128)(4,1)} %copy-done.5) | copy-start | bytes 6148
  2209.9 49.0 %all-to-all-start.3 = ((bf16[64,2,640]{2,1,0:T(2,128)(2,1)}), bf16[64,2,640]{2,1,0:T(2,128)(2,1)S(1)}, u32[]{:S(2)}, u32[]{:S(2)}) async-start(bf16[64,2,640]{2,1,0:T(2,128)(2,1)} %reshape.185), calls=%async_computation.3 | async-start | bytes 327680 | tf_op jit(solution)/shard_map/all_to_all | solution.py:106
Sparse Core Ops, SparseCore 0:
  10.0 182.1 all-gather.2
  197.7 1682.9 all-reduce.4
where the time goes:
time: 2270 us
  waiting for transfers between devices  1910 us (84%)
  blocking collectives  283 us (12%)
  starting transfers between devices  33.4 us (1%)
    unnamed x6, waiting for transfers between devices  1680 us
    all_gather x1, waiting for transfers between devices, shards(): segment = lax.all_gather(key_value, 'ctx', axis=0, tiled=True)  184 us
    unnamed x1, blocking collectives  119 us
    all_gather x1, blocking collectives, shards(): lax.all_gather(activated, 'ctx', axis=0, tiled=True)  109 us
    all_to_all x1, blocking collectives, shards(): lax.all_to_all(buckets, 'exp', split_axis=0, concat_axis=1, tiled=True)  54.7 us
  transfers between devices with their start and end apart: 8, of which 4 were waited for; matrix products, arithmetic and copies ran while one was open for 1% of the time, Pallas kernels for 0%

commit v1 on v0

v1 whole, which is shorter than its diff:
```python
import jax
import jax.numpy as jnp
from jax import lax
from jax.sharding import Mesh, PartitionSpec as P

HD = 128
KV_HEADS = 4
CAP = 5

NP, NQ = 4, 4
NX, NZ, NY, NC = 4, 2, 4, 2

CTX = ("p", "q")
EXP = ("x", "zh", "y", "core")
PLANE = ("x", "y", "core")
NPLANE = NX * NY * NC
NCTX = NP * NQ

masked_score = -1e30
f32 = jnp.float32
bf16 = jnp.bfloat16


def swap(array, axes):
    return lax.all_to_all(array, axes, split_axis=0, concat_axis=0, tiled=True)


def share(block, axes, count):
    return swap(jnp.broadcast_to(block[None], (count,) + block.shape), axes)


def dot(a, b):
    return jnp.dot(a, b, preferred_element_type=f32)


def neighbour_blocks(blocks, q_index):
    received = []
    for k in range(NQ):
        mine = blocks(jnp.bitwise_xor(q_index, k))
        if k > 0:
            mine = lax.ppermute(mine, "q", [(i, i ^ k) for i in range(NQ)])
        received.append(mine)
    return received


def gather_keys_values(keys_values, x_index):
    rows = keys_values.shape[0]
    pieces = NY * NC
    height = rows // pieces
    piece = lax.axis_index(("y", "core"))
    key_piece = lax.dynamic_slice(keys_values, (piece * height, x_index * HD), (height, HD))
    value_piece = lax.dynamic_slice(
        keys_values, (piece * height, (KV_HEADS + x_index) * HD), (height, HD)
    )
    own = jnp.concatenate([key_piece, value_piece], axis=1)
    column = share(own, CTX, NCTX)
    segment = share(column, ("y", "core"), pieces).reshape(NCTX * rows, 2 * HD)
    number = jnp.arange(NCTX * rows, dtype=jnp.int32)
    key_pos = (
        (number % (NCTX * height)) // height * rows
        + number // (NCTX * height) * height
        + number % height
    )
    return segment[:, :HD], segment[:, HD:], key_pos


def attend(queries, key_part, value_part, key_pos, ctx_index):
    rows = queries.shape[0]
    query_pos = ctx_index * rows + jnp.arange(rows, dtype=jnp.int32)
    scores = (
        jnp.einsum("qd,kd->qk", queries, key_part, preferred_element_type=f32) * HD ** (-0.5)
    )
    allowed = key_pos[None, :] <= query_pos[:, None]
    scores = jnp.where(allowed, scores, masked_score)
    top = jnp.max(scores, axis=-1, keepdims=True)
    weights = jnp.where(allowed, jnp.exp(scores - top), 0.0)
    total = jnp.sum(weights, axis=-1, keepdims=True)
    return (dot(weights.astype(bf16), value_part) / total).astype(bf16)


def shards(
    queries,
    keys_values,
    residual,
    norm_gain,
    out_weight,
    expert_ids,
    gate_values,
    gate_up_weight,
    down_weight,
):
    p_index = lax.axis_index("p")
    q_index = lax.axis_index("q")
    x_index = lax.axis_index("x")
    zh_index = lax.axis_index("zh")
    ctx_index = lax.axis_index(CTX)
    gate_up_weight = gate_up_weight[0]
    down_weight = down_weight[0]
    feat = down_weight.shape[1]
    units = down_weight.shape[0] // NQ
    width = NQ * feat
    model = NP * width

    def gate_up_block(target):
        gate = lax.dynamic_slice(gate_up_weight, (0, target * units), (feat, units))
        up = lax.dynamic_slice(gate_up_weight, (0, (NQ + target) * units), (feat, units))
        return jnp.concatenate([gate, up], axis=1)

    def down_block(target):
        return lax.dynamic_slice(down_weight, (target * units, 0), (units, feat))

    flip = [(i, NZ - 1 - i) for i in range(NZ)]
    other_ids = lax.ppermute(expert_ids, "zh", flip)
    other_gates = lax.ppermute(gate_values, "zh", flip)

    key_part, value_part, key_pos = gather_keys_values(keys_values, x_index)
    weight_in = neighbour_blocks(gate_up_block, q_index)
    weight_out = neighbour_blocks(down_block, q_index)
    attended = attend(queries, key_part, value_part, key_pos, ctx_index)

    share_rows = attended.shape[0] // (NPLANE * NZ)
    attended = (
        attended.reshape(NX, NZ, NY, NC, share_rows, HD)
        .transpose(0, 2, 3, 1, 4, 5)
        .reshape(-1, HD)
    )
    partial = dot(attended, out_weight).astype(bf16).reshape(NPLANE, NZ * share_rows, model)
    partial = jnp.sum(swap(partial, PLANE).astype(f32), axis=0).reshape(NZ, share_rows, model)
    own_group = jnp.arange(NZ)[:, None, None] == zh_index
    partial = partial + jnp.where(own_group, residual.astype(f32)[None], 0.0)
    outgoing = (
        partial.astype(bf16)
        .reshape(NZ * share_rows, NP, 1, 1, width)
        .transpose(1, 2, 3, 0, 4)
    )
    outgoing = jnp.broadcast_to(outgoing, (NP, NQ, NZ, NZ * share_rows, width)).reshape(
        NCTX * NZ, NZ * share_rows, width
    )
    arrived = swap(outgoing, CTX + ("zh",)).reshape(NCTX, NZ, NZ * share_rows, width)
    hidden = jnp.sum(arrived.astype(f32), axis=1).astype(bf16).reshape(-1, width)

    hidden = jnp.concatenate(
        [
            lax.dynamic_slice_in_dim(hidden, jnp.bitwise_xor(q_index, k) * feat, feat, 1)
            for k in range(NQ)
        ],
        axis=1,
    )
    gain = jnp.concatenate(
        [
            lax.dynamic_slice_in_dim(
                norm_gain, (p_index * NQ + jnp.bitwise_xor(q_index, k)) * feat, feat, 0
            )
            for k in range(NQ)
        ]
    )

    token_count = expert_ids.shape[0]
    first = zh_index == 0
    ids = jnp.stack(
        [jnp.where(first, expert_ids, other_ids), jnp.where(first, other_ids, expert_ids)]
    )
    gates = jnp.stack(
        [jnp.where(first, gate_values, other_gates), jnp.where(first, other_gates, gate_values)]
    )
    number = jnp.arange(NPLANE, dtype=jnp.int32)
    experts = (number // (NY * NC) * NZ + zh_index) * (NY * NC) + number % (NY * NC)
    picked = ids[..., None] == experts
    chosen = jnp.sum(picked.astype(jnp.int32), axis=2)
    slot_index = jnp.cumsum(chosen, axis=1, dtype=jnp.int32) - chosen
    gate_table = jnp.sum(jnp.where(picked, gates[..., None], 0.0), axis=2)
    placed = (chosen[..., None] > 0) & (
        slot_index[..., None] == jnp.arange(CAP, dtype=jnp.int32)
    )
    same = jnp.eye(NZ, dtype=bool)[:, :, None, None, None]
    spread = (placed[:, None] & same).astype(f32)
    spread_gate = spread * gate_table[:, None, :, :, None]
    slots = NZ * CAP
    total_slots = NPLANE * slots
    selector = (
        spread.astype(bf16)
        .reshape(NZ, NZ, NCTX, share_rows, NPLANE, CAP)
        .transpose(4, 1, 5, 2, 0, 3)
        .reshape(total_slots, NZ * token_count)
    )
    combine = spread_gate.transpose(0, 2, 3, 1, 4).reshape(NZ * token_count, total_slots)

    buckets = dot(selector, hidden).astype(bf16).reshape(NPLANE, slots, width)
    buffer = swap(buckets, PLANE).reshape(total_slots, width).astype(f32)
    squares = jnp.sum(buffer * buffer, axis=1)
    scaled = (buffer * gain).astype(bf16)
    gate_up = dot(scaled[:, :feat], weight_in[0])
    for k in range(1, NQ):
        gate_up = gate_up + dot(scaled[:, k * feat : (k + 1) * feat], weight_in[k])

    rows = total_slots // NP
    chunks = 2 * units // HD
    high = squares.astype(bf16)
    low = (squares - high.astype(f32)).astype(bf16)
    pair = jnp.stack([high.reshape(NP, rows), low.reshape(NP, rows)], axis=1)
    pair = jnp.pad(pair, ((0, 0), (0, 14), (0, HD - rows)))
    body = (
        gate_up.astype(bf16).reshape(NP, rows, chunks, HD).transpose(0, 2, 1, 3)
    ).reshape(NP, chunks * rows, HD)
    summed = jnp.sum(swap(jnp.concatenate([body, pair], axis=1), "p").astype(f32), axis=0)
    square_sum = summed[chunks * rows] + summed[chunks * rows + 1]
    scale = lax.rsqrt(square_sum[:rows] / model + 1e-06)
    pre = summed[: chunks * rows].reshape(2, chunks // 2, rows, HD) * scale[:, None]
    activated = (jax.nn.silu(pre[0]) * pre[1]).astype(bf16)
    activated = share(activated, "p", NP).reshape(NP, chunks // 2, rows, HD)
    activated = activated.transpose(0, 2, 1, 3).reshape(total_slots, units)

    expert_out = jnp.concatenate(
        [dot(activated, block).astype(bf16) for block in weight_out], axis=1
    )
    returned = swap(expert_out.reshape(NPLANE, slots, width), PLANE).reshape(total_slots, width)
    combine_high = combine.astype(bf16)
    combine_low = (combine - combine_high.astype(f32)).astype(bf16)
    mixed = dot(combine_high, returned) + dot(combine_low, returned)
    mixed = mixed.astype(bf16)
    outgoing = jnp.stack(
        [
            lax.dynamic_slice_in_dim(mixed, jnp.bitwise_xor(q_index, k) * feat, feat, 1)
            for k in range(NQ)
        ]
    ).reshape(NQ * NZ, token_count, feat)
    landed = jnp.sum(swap(outgoing, ("q", "zh")).astype(f32), axis=0)
    stream = hidden[:, :feat].reshape(NCTX, NZ, share_rows, feat)
    stream = lax.dynamic_index_in_dim(stream, zh_index, 1, keepdims=False)
    return (stream.reshape(token_count, feat).astype(f32) + landed).astype(bf16)


def solution(mesh):
    fine = Mesh(mesh.devices.reshape(NP, NQ, NX, NZ, NY, NC), CTX + EXP)
    in_specs = (
        P(CTX, EXP),
        P(CTX, None),
        P(CTX + EXP, None),
        P(),
        P(EXP, None),
        P(EXP, None),
        P(EXP, None),
        P(EXP, CTX, None),
        P(EXP, None, CTX),
    )
    return jax.shard_map(
        shards, mesh=fine, in_specs=in_specs, out_specs=P(EXP, CTX), check_vma=False
    )
```

time: 2270 us -> 376 us (0.17)
  waiting for transfers between devices: 1910 us -> 128 us
  blocking collectives: 283 us -> 104 us
  starting transfers between devices: 33.4 us -> 108 us
    unnamed x6 -> x0, waiting for transfers between devices: 1680 us -> none
    all_gather x1 -> x0, waiting for transfers between devices: 184 us -> none  [shards(): segment = lax.all_gather(key_value, 'ctx', axis=0, tiled=True)]
    unnamed x1 -> x0, blocking collectives: 119 us -> none
    all_gather x1 -> x0, blocking collectives: 109 us -> none  [shards(): lax.all_gather(activated, 'ctx', axis=0, tiled=True)]
    ppermute x0 -> x8, starting transfers between devices: none -> 58.7 us  [the longest x1 21.5 us: shards(): other_ids = lax.ppermute(expert_ids, 'zh', flip)]
    ppermute x0 -> x8, waiting for transfers between devices: none -> 57 us  [the longest x6 35.4 us: neighbour_blocks(): mine = lax.ppermute(mine, 'q', [(i, i ^ k) for i in range(NQ)])]
    all_to_all x1 -> x2, blocking collectives: 54.7 us -> 104 us  [swap(): return lax.all_to_all(array, axes, split_axis=0, concat_axis=0, tiled=True)]
    all_to_all x3 -> x7, waiting for transfers between devices: 44.6 us -> 70.9 us  [swap(): return lax.all_to_all(array, axes, split_axis=0, concat_axis=0, tiled=True)]
  transfers between devices with their start and end apart: 8 -> 15, of which waited for: 4 -> 10; matrix products, arithmetic and copies ran while one was open for 1% -> 4% of each run, Pallas kernels for 0% -> 0%
where the time goes in v1:
time: 376 us; the launch traced here: 371 us
  waiting for transfers between devices  128 us (34%)
  starting transfers between devices  108 us (29%)
  blocking collectives  104 us (28%)
  local copies, waits for them, and re-layouts  14.4 us (4%)
  other arithmetic  8.76 us (2%)
  matrix products  7.56 us (2%)
    all_to_all x2, blocking collectives, swap(): return lax.all_to_all(array, axes, split_axis=0, concat_axis=0, tiled=True)  104 us
    all_to_all x7, waiting for transfers between devices, swap(): return lax.all_to_all(array, axes, split_axis=0, concat_axis=0, tiled=True)  70.9 us
    all_to_all x7, starting transfers between devices, swap(): return lax.all_to_all(array, axes, split_axis=0, concat_axis=0, tiled=True)  49.3 us
    ppermute x6, waiting for transfers between devices, neighbour_blocks(): mine = lax.ppermute(mine, 'q', [(i, i ^ k) for i in range(NQ)])  35.4 us
    ppermute x1, waiting for transfers between devices, shards(): other_ids = lax.ppermute(expert_ids, 'zh', flip)  21.6 us
    ppermute x1, starting transfers between devices, shards(): other_ids = lax.ppermute(expert_ids, 'zh', flip)  21.5 us
    ppermute x6, starting transfers between devices, neighbour_blocks(): mine = lax.ppermute(mine, 'q', [(i, i ^ k) for i in range(NQ)])  19.9 us
    ppermute x1, starting transfers between devices, shards(): other_gates = lax.ppermute(gate_values, 'zh', flip)  17.3 us
  transfers between devices with their start and end apart: 15, of which 10 were waited for; matrix products, arithmetic and copies ran while one was open for 4% of the time, Pallas kernels for 0%

profile of v1, /device:TPU:1, one launch (start us, length us, event | category | flops | bytes accessed | tf_op | source)
XLA Modules:
  0.0 371.0 jit_solution(18168377990919849929)
XLA Ops:
  0.8 48.0 %all_to_all.45 = bf16[16,16,256]{2,1,0:T(8,128)(2,1)S(1)} all-to-all(bf16[16,16,256]{2,1,0:T(8,128)(2,1)S(1)} %broadcast_in_dim.88), channel_id=1, replica_groups=mesh['p'=4,'q'=4,'x'=4,'zh'=2,'y'=4,'core'=2] {'p','q'}, dimensions={0} | all-to-all | bytes 262144 | tf_op jit(solution)/shard_map/all_to_all | solution.py:25
  49.9 6.8 %all-to-all-start.1 = ((bf16[8,16,16,256]{3,2,1,0:T(8,128)(2,1)}), bf16[8,16,16,256]{3,2,1,0:T(8,128)(2,1)S(1)}, u32[]{:S(2)}, u32[]{:S(2)}) async-start(bf16[8,16,16,256]{3,2,1,0:T(8,128)(2,1)} %broadcast_in_dim.89), calls=%async_computation.1 | async-start | bytes 2097152 | tf_op jit(solution)/shard_map/all_to_all | solution.py:25
  56.7 15.1 %all-to-all-done.1 = bf16[8,16,16,256]{3,2,1,0:T(8,128)(2,1)S(1)} async-done(((bf16[8,16,16,256]{3,2,1,0:T(8,128)(2,1)}), bf16[8,16,16,256]{3,2,1,0:T(8,128)(2,1)S(1)}, u32[]{:S(2)}, u32[]{:S(2)}) %all-to-all-start.1) | async-done | bytes 1048608 | tf_op jit(solution)/shard_map/all_to_all | solution.py:25
  75.0 6.1 %all-to-all-start.2 = ((bf16[32,4,4096]{2,1,0:T(4,128)(2,1)}), bf16[32,4,4096]{2,1,0:T(4,128)(2,1)S(1)}, u32[]{:S(2)}, u32[]{:S(2)}) async-start(bf16[32,4,4096]{2,1,0:T(4,128)(2,1)} %reshape.298), calls=%async_computation.2 | async-start | bytes 2097152 | tf_op jit(solution)/shard_map/all_to_all | solution.py:25
  81.4 16.6 %all-to-all-done.2 = bf16[32,4,4096]{2,1,0:T(4,128)(2,1)S(1)} async-done(((bf16[32,4,4096]{2,1,0:T(4,128)(2,1)}), bf16[32,4,4096]{2,1,0:T(4,128)(2,1)S(1)}, u32[]{:S(2)}, u32[]{:S(2)}) %all-to-all-start.2) | async-done | bytes 1048608 | tf_op jit(solution)/shard_map/all_to_all | solution.py:25
  99.4 11.3 %all-to-all-start.3 = ((bf16[32,4,1024]{2,1,0:T(4,128)(2,1)}), bf16[32,4,1024]{2,1,0:T(4,128)(2,1)S(1)}, u32[]{:S(2)}, u32[]{:S(2)}) async-start(bf16[32,4,1024]{2,1,0:T(4,128)(2,1)} %bitcast.7), calls=%async_computation.3 | async-start | bytes 524288 | tf_op jit(solution)/shard_map/all_to_all | solution.py:25
  110.8 21.5 %collective-permute-start = (s32[32,8]{0,1:T(8,128)S(1)}, s32[32,8]{0,1:T(8,128)S(1)}, u32[]{:S(2)}, u32[]{:S(2)}) collective-permute-start(s32[32,8]{0,1:T(8,128)S(1)} %copy-done.5), channel_id=1, source_target_pairs={{0,8},{8,0},{1,9},{9,1},{2,10},{10,2},{3,11},{11,3},{4,12},{12,4},... | collective-permute-start | bytes 3080 | tf_op jit(solution)/shard_map/ppermute | solution.py:113
  132.4 21.6 %collective-permute-done = s32[32,8]{0,1:T(8,128)S(1)} collective-permute-done((s32[32,8]{0,1:T(8,128)S(1)}, s32[32,8]{0,1:T(8,128)S(1)}, u32[]{:S(2)}, u32[]{:S(2)}) %collective-permute-start) | collective-permute-done | bytes 1056 | tf_op jit(solution)/shard_map/ppermute | solution.py:113
  155.0 1.5 fusion.2
  156.5 1.6 convert_element_type.188
  159.9 4.5 %all-to-all-start.4 = ((bf16[32,10,1024]{2,1,0:T(8,128)(2,1)}), bf16[32,10,1024]{2,1,0:T(8,128)(2,1)S(1)}, u32[]{:S(2)}, u32[]{:S(2)}) async-start(bf16[32,10,1024]{2,1,0:T(8,128)(2,1)} %reshape.304), calls=%async_computation.4 | async-start | bytes 2097152 | tf_op jit(solution)/shard_map/all_to_all | solution.py:25
  164.5 2.4 dynamic-slice_bitcast_fusion.6
  167.7 2.5 collective-permute-start.4
  171.0 1.9 collective-permute-start.2
  173.7 5.0 %collective-permute-start.3 = (bf16[256,768]{1,0:T(8,128)(2,1)}, bf16[256,768]{1,0:T(8,128)(2,1)}, u32[]{:S(2)}, u32[]{:S(2)}) collective-permute-start(bf16[256,768]{1,0:T(8,128)(2,1)} %pad_maximum_fusion.3), channel_id=1, source_target_pairs={{0,128},{64,192},{128,0},{192,64},{1,129},{65,193},{129,1},{193,65... | collective-permute-start | bytes 1179656 | tf_op jit(solution)/shard_map/ppermute | solution.py:41
  179.7 1.8 all-to-all-done.4
  182.2 1.3 fusion.32
  183.9 9.5 %collective-permute-done.2 = bf16[256,768]{1,0:T(8,128)(2,1)} collective-permute-done((bf16[256,768]{1,0:T(8,128)(2,1)}, bf16[256,768]{1,0:T(8,128)(2,1)}, u32[]{:S(2)}, u32[]{:S(2)}) %collective-permute-start.2) | collective-permute-done | bytes 393248 | tf_op jit(solution)/shard_map/ppermute | solution.py:41
  194.7 10.7 %collective-permute-done.3 = bf16[256,768]{1,0:T(8,128)(2,1)} collective-permute-done((bf16[256,768]{1,0:T(8,128)(2,1)}, bf16[256,768]{1,0:T(8,128)(2,1)}, u32[]{:S(2)}, u32[]{:S(2)}) %collective-permute-start.3) | collective-permute-done | bytes 393248 | tf_op jit(solution)/shard_map/ppermute | solution.py:41
  205.4 1.3 fusion.4
  207.4 55.6 %all_to_all.46 = bf16[4,496,128]{2,1,0:T(8,128)(2,1)S(1)} all-to-all(bf16[4,496,128]{2,1,0:T(8,128)(2,1)S(1)} %pad_maximum_fusion.1), channel_id=1, replica_groups=mesh['p'=4,'q'=4,'x'=4,'zh'=2,'y'=4,'core'=2] {'p'}, dimensions={0} | all-to-all | bytes 1015808 | tf_op jit(solution)/shard_map/all_to_all | solution.py:25
  264.0 3.4 all-to-all-start.6
  267.4 17.3 %collective-permute-start.1 = (f32[32,8]{0,1:T(8,128)S(1)}, f32[32,8]{0,1:T(8,128)S(1)}, u32[]{:S(2)}, u32[]{:S(2)}) collective-permute-start(f32[32,8]{0,1:T(8,128)S(1)} %copy-done.6), channel_id=1, source_target_pairs={{0,8},{8,0},{1,9},{9,1},{2,10},{10,2},{3,11},{11,3},{4,12},{12,4},... | collective-permute-start | bytes 3080 | tf_op jit(solution)/shard_map/ppermute | solution.py:114
  284.8 1.9 collective-permute-start.5
  286.7 6.4 %collective-permute-start.7 = (bf16[384,256]{1,0:T(8,128)(2,1)S(1)}, bf16[384,256]{1,0:T(8,128)(2,1)S(1)}, u32[]{:S(2)}, u32[]{:S(2)}) collective-permute-start(bf16[384,256]{1,0:T(8,128)(2,1)S(1)} %get-tuple-element.16), channel_id=1, source_target_pairs={{0,192},{64,128},{128,64},{192,0},{1,193},{65,129},{129,65},{193,1... | collective-permute-start | bytes 589832 | tf_op jit(solution)/shard_map/ppermute | solution.py:41
  293.1 2.2 collective-permute-start.6
  295.5 6.8 %collective-permute-done.7 = bf16[384,256]{1,0:T(8,128)(2,1)S(1)} collective-permute-done((bf16[384,256]{1,0:T(8,128)(2,1)S(1)}, bf16[384,256]{1,0:T(8,128)(2,1)S(1)}, u32[]{:S(2)}, u32[]{:S(2)}) %collective-permute-start.7) | collective-permute-done | bytes 196640 | tf_op jit(solution)/shard_map/ppermute | solution.py:41
  302.5 8.4 %collective-permute-done.6 = bf16[384,256]{1,0:T(8,128)(2,1)S(1)} collective-permute-done((bf16[384,256]{1,0:T(8,128)(2,1)S(1)}, bf16[384,256]{1,0:T(8,128)(2,1)S(1)}, u32[]{:S(2)}, u32[]{:S(2)}) %collective-permute-start.6) | collective-permute-done | bytes 196640 | tf_op jit(solution)/shard_map/ppermute | solution.py:41
  313.0 8.4 %all-to-all-start.7 = ((bf16[32,10,1024]{2,1,0:T(8,128)(2,1)}), bf16[32,10,1024]{2,1,0:T(8,128)(2,1)S(1)}, u32[]{:S(2)}, u32[]{:S(2)}) async-start(bf16[32,10,1024]{2,1,0:T(8,128)(2,1)} %reshape.309), calls=%async_computation.7 | async-start | bytes 2097152 | tf_op jit(solution)/shard_map/all_to_all | solution.py:25
  322.7 15.6 %all-to-all-done.7 = bf16[32,10,1024]{2,1,0:T(8,128)(2,1)S(1)} async-done(((bf16[32,10,1024]{2,1,0:T(8,128)(2,1)}), bf16[32,10,1024]{2,1,0:T(8,128)(2,1)S(1)}, u32[]{:S(2)}, u32[]{:S(2)}) %all-to-all-start.7) | async-done | bytes 655392 | tf_op jit(solution)/shard_map/all_to_all | solution.py:25
  339.8 8.8 %all-to-all-start.8 = ((bf16[8,32,256]{2,1,0:T(8,128)(2,1)}), bf16[8,32,256]{2,1,0:T(8,128)(2,1)S(1)}, u32[]{:S(2)}, u32[]{:S(2)}) async-start(bf16[8,32,256]{2,1,0:T(8,128)(2,1)} %bitcast.40), calls=%async_computation.8 | async-start | bytes 262144 | tf_op jit(solution)/shard_map/all_to_all | solution.py:25
  348.6 21.8 %all-to-all-done.8 = bf16[8,32,256]{2,1,0:T(8,128)(2,1)S(1)} async-done(((bf16[8,32,256]{2,1,0:T(8,128)(2,1)}), bf16[8,32,256]{2,1,0:T(8,128)(2,1)S(1)}, u32[]{:S(2)}, u32[]{:S(2)}) %all-to-all-start.8) | async-done | bytes 131104 | tf_op jit(solution)/shard_map/all_to_all | solution.py:25
  (113 shorter events, 22.7 us)
Async XLA Ops:
  0.0 73.4 %copy-start = (bf16[128,4096]{1,0:T(8,128)(2,1)S(1)}, bf16[128,4096]{1,0:T(8,128)(2,1)}, u32[]{:S(2)}) copy-start(bf16[128,4096]{1,0:T(8,128)(2,1)} %param.13) | copy-start | bytes 3145732
  49.9 21.9 %copy-start.7 = (bf16[128,128]{1,0:T(8,128)(2,1)S(1)}, bf16[128,128]{1,0:T(8,128)(2,1)}, u32[]{:S(2)}) copy-start(bf16[128,128]{1,0:T(8,128)(2,1)} %param.9) | copy-start | bytes 98308
  49.9 21.9 %all-to-all-start.1 = ((bf16[8,16,16,256]{3,2,1,0:T(8,128)(2,1)}), bf16[8,16,16,256]{3,2,1,0:T(8,128)(2,1)S(1)}, u32[]{:S(2)}, u32[]{:S(2)}) async-start(bf16[8,16,16,256]{3,2,1,0:T(8,128)(2,1)} %broadcast_in_dim.89), calls=%async_computation.1 | async-start | bytes 2097152 | tf_op jit(solution)/shard_map/all_to_all | solution.py:25
  75.0 6.3 %copy-start.4 = (bf16[2,4096]{1,0:T(2,128)(2,1)S(1)}, bf16[2,4096]{1,0:T(2,128)(2,1)}, u32[]{:S(2)}) copy-start(bf16[2,4096]{1,0:T(2,128)(2,1)} %param.11) | copy-start | bytes 49156
  75.0 23.0 %all-to-all-start.2 = ((bf16[32,4,4096]{2,1,0:T(4,128)(2,1)}), bf16[32,4,4096]{2,1,0:T(4,128)(2,1)S(1)}, u32[]{:S(2)}, u32[]{:S(2)}) async-start(bf16[32,4,4096]{2,1,0:T(4,128)(2,1)} %reshape.298), calls=%async_computation.2 | async-start | bytes 2097152 | tf_op jit(solution)/shard_map/all_to_all | solution.py:25
  81.1 29.7 %copy-start.5 = (s32[32,8]{0,1:T(8,128)S(1)}, s32[32,8]{0,1:T(8,128)}, u32[]{:S(2)}) copy-start(s32[32,8]{0,1:T(8,128)} %param.14) | copy-start | bytes 3076
  99.4 58.7 %all-to-all-start.3 = ((bf16[32,4,1024]{2,1,0:T(4,128)(2,1)}), bf16[32,4,1024]{2,1,0:T(4,128)(2,1)S(1)}, u32[]{:S(2)}, u32[]{:S(2)}) async-start(bf16[32,4,1024]{2,1,0:T(4,128)(2,1)} %bitcast.7), calls=%async_computation.3 | async-start | bytes 524288 | tf_op jit(solution)/shard_map/all_to_all | solution.py:25
  110.8 43.2 %collective-permute-start = (s32[32,8]{0,1:T(8,128)S(1)}, s32[32,8]{0,1:T(8,128)S(1)}, u32[]{:S(2)}, u32[]{:S(2)}) collective-permute-start(s32[32,8]{0,1:T(8,128)S(1)} %copy-done.5), channel_id=1, source_target_pairs={{0,8},{8,0},{1,9},{9,1},{2,10},{10,2},{3,11},{11,3},{4,12},{12,4},... | collective-permute-start | bytes 3080 | tf_op jit(solution)/shard_map/ppermute | solution.py:113
  159.9 21.6 %all-to-all-start.4 = ((bf16[32,10,1024]{2,1,0:T(8,128)(2,1)}), bf16[32,10,1024]{2,1,0:T(8,128)(2,1)S(1)}, u32[]{:S(2)}, u32[]{:S(2)}) async-start(bf16[32,10,1024]{2,1,0:T(8,128)(2,1)} %reshape.304), calls=%async_computation.4 | async-start | bytes 2097152 | tf_op jit(solution)/shard_map/all_to_all | solution.py:25
  167.7 14.6 %collective-permute-start.4 = (bf16[256,768]{1,0:T(8,128)(2,1)}, bf16[256,768]{1,0:T(8,128)(2,1)}, u32[]{:S(2)}, u32[]{:S(2)}) collective-permute-start(bf16[256,768]{1,0:T(8,128)(2,1)} %pad_maximum_fusion.4), channel_id=1, source_target_pairs={{0,192},{64,128},{128,64},{192,0},{1,193},{65,129},{129,65},{193,1... | collective-permute-start | bytes 1179656 | tf_op jit(solution)/shard_map/ppermute | solution.py:41
  171.0 22.4 %collective-permute-start.2 = (bf16[256,768]{1,0:T(8,128)(2,1)}, bf16[256,768]{1,0:T(8,128)(2,1)}, u32[]{:S(2)}, u32[]{:S(2)}) collective-permute-start(bf16[256,768]{1,0:T(8,128)(2,1)} %pad_maximum_fusion.2), channel_id=1, source_target_pairs={{0,64},{64,0},{128,192},{192,128},{1,65},{65,1},{129,193},{193,129... | collective-permute-start | bytes 1179656 | tf_op jit(solution)/shard_map/ppermute | solution.py:41
  173.7 31.7 %collective-permute-start.3 = (bf16[256,768]{1,0:T(8,128)(2,1)}, bf16[256,768]{1,0:T(8,128)(2,1)}, u32[]{:S(2)}, u32[]{:S(2)}) collective-permute-start(bf16[256,768]{1,0:T(8,128)(2,1)} %pad_maximum_fusion.3), channel_id=1, source_target_pairs={{0,128},{64,192},{128,0},{192,64},{1,129},{65,193},{129,1},{193,65... | collective-permute-start | bytes 1179656 | tf_op jit(solution)/shard_map/ppermute | solution.py:41
  182.1 1.5 copy-start.1
  182.1 1.5 copy-start.2
  263.0 4.4 %copy-start.6 = (f32[32,8]{0,1:T(8,128)S(1)}, f32[32,8]{0,1:T(8,128)}, u32[]{:S(2)}) copy-start(f32[32,8]{0,1:T(8,128)} %param.15) | copy-start | bytes 3076
  263.0 21.7 %copy-start.3 = (bf16[1,1536,256]{2,1,0:T(8,128)(2,1)S(1)}, bf16[1,1536,256]{2,1,0:T(8,128)(2,1)}, u32[]{:S(2)}) copy-start(bf16[1,1536,256]{2,1,0:T(8,128)(2,1)} %param.17) | copy-start | bytes 2359300
  264.0 31.3 %all-to-all-start.6 = ((bf16[4,3,80,128]{3,2,1,0:T(8,128)(2,1)}), bf16[4,3,80,128]{3,2,1,0:T(8,128)(2,1)S(1)}, u32[]{:S(2)}, u32[]{:S(2)}) async-start(bf16[4,3,80,128]{3,2,1,0:T(8,128)(2,1)} %broadcast_in_dim.103), calls=%async_computation.6 | async-start | bytes 491520 | tf_op jit(solution)/shard_map/all_to_all | solution.py:25
  267.4 27.9 %collective-permute-start.1 = (f32[32,8]{0,1:T(8,128)S(1)}, f32[32,8]{0,1:T(8,128)S(1)}, u32[]{:S(2)}, u32[]{:S(2)}) collective-permute-start(f32[32,8]{0,1:T(8,128)S(1)} %copy-done.6), channel_id=1, source_target_pairs={{0,8},{8,0},{1,9},{9,1},{2,10},{10,2},{3,11},{11,3},{4,12},{12,4},... | collective-permute-start | bytes 3080 | tf_op jit(solution)/shard_map/ppermute | solution.py:114
  284.8 26.7 %collective-permute-start.5 = (bf16[384,256]{1,0:T(8,128)(2,1)S(1)}, bf16[384,256]{1,0:T(8,128)(2,1)S(1)}, u32[]{:S(2)}, u32[]{:S(2)}) collective-permute-start(bf16[384,256]{1,0:T(8,128)(2,1)S(1)} %get-tuple-element.15), channel_id=1, source_target_pairs={{0,64},{64,0},{128,192},{192,128},{1,65},{65,1},{129,193},{193,129... | collective-permute-start | bytes 589832 | tf_op jit(solution)/shard_map/ppermute | solution.py:41
  286.7 15.5 %collective-permute-start.7 = (bf16[384,256]{1,0:T(8,128)(2,1)S(1)}, bf16[384,256]{1,0:T(8,128)(2,1)S(1)}, u32[]{:S(2)}, u32[]{:S(2)}) collective-permute-start(bf16[384,256]{1,0:T(8,128)(2,1)S(1)} %get-tuple-element.16), channel_id=1, source_target_pairs={{0,192},{64,128},{128,64},{192,0},{1,193},{65,129},{129,65},{193,1... | collective-permute-start | bytes 589832 | tf_op jit(solution)/shard_map/ppermute | solution.py:41
  293.1 17.8 %collective-permute-start.6 = (bf16[384,256]{1,0:T(8,128)(2,1)S(1)}, bf16[384,256]{1,0:T(8,128)(2,1)S(1)}, u32[]{:S(2)}, u32[]{:S(2)}) collective-permute-start(bf16[384,256]{1,0:T(8,128)(2,1)S(1)} %get-tuple-element.17), channel_id=1, source_target_pairs={{0,128},{64,192},{128,0},{192,64},{1,129},{65,193},{129,1},{193,65... | collective-permute-start | bytes 589832 | tf_op jit(solution)/shard_map/ppermute | solution.py:41
  313.0 25.3 %all-to-all-start.7 = ((bf16[32,10,1024]{2,1,0:T(8,128)(2,1)}), bf16[32,10,1024]{2,1,0:T(8,128)(2,1)S(1)}, u32[]{:S(2)}, u32[]{:S(2)}) async-start(bf16[32,10,1024]{2,1,0:T(8,128)(2,1)} %reshape.309), calls=%async_computation.7 | async-start | bytes 2097152 | tf_op jit(solution)/shard_map/all_to_all | solution.py:25
  339.8 30.6 %all-to-all-start.8 = ((bf16[8,32,256]{2,1,0:T(8,128)(2,1)}), bf16[8,32,256]{2,1,0:T(8,128)(2,1)S(1)}, u32[]{:S(2)}, u32[]{:S(2)}) async-start(bf16[8,32,256]{2,1,0:T(8,128)(2,1)} %bitcast.40), calls=%async_computation.8 | async-start | bytes 262144 | tf_op jit(solution)/shard_map/all_to_all | solution.py:25

commit v2 on v1

--- a/solution.py
+++ b/solution.py
@@ -33,35 +33,33 @@
     return jnp.dot(a, b, preferred_element_type=f32)
 
 
-def neighbour_blocks(blocks, q_index):
-    received = []
-    for k in range(NQ):
-        mine = blocks(jnp.bitwise_xor(q_index, k))
-        if k > 0:
-            mine = lax.ppermute(mine, "q", [(i, i ^ k) for i in range(NQ)])
-        received.append(mine)
-    return received
-
-
-def gather_keys_values(keys_values, x_index):
-    rows = keys_values.shape[0]
-    pieces = NY * NC
-    height = rows // pieces
+def from_neighbour(block, k):
+    return lax.ppermute(block, "q", [(i, i ^ k) for i in range(NQ)])
+
+
+def split(value):
+    high = lax.reduce_precision(value, 8, 7)
+    return high.astype(bf16), (value - high).astype(bf16)
+
+
+def gather_column(keys_values, x_index):
+    height = keys_values.shape[0] // (NY * NC)
     piece = lax.axis_index(("y", "core"))
     key_piece = lax.dynamic_slice(keys_values, (piece * height, x_index * HD), (height, HD))
     value_piece = lax.dynamic_slice(
         keys_values, (piece * height, (KV_HEADS + x_index) * HD), (height, HD)
     )
-    own = jnp.concatenate([key_piece, value_piece], axis=1)
-    column = share(own, CTX, NCTX)
-    segment = share(column, ("y", "core"), pieces).reshape(NCTX * rows, 2 * HD)
+    return share(jnp.concatenate([key_piece, value_piece], axis=1), CTX, NCTX)
+
+
+def key_positions(rows):
+    height = rows // (NY * NC)
     number = jnp.arange(NCTX * rows, dtype=jnp.int32)
-    key_pos = (
+    return (
         (number % (NCTX * height)) // height * rows
         + number // (NCTX * height) * height
         + number % height
     )
-    return segment[:, :HD], segment[:, HD:], key_pos
 
 
 def attend(queries, key_part, value_part, key_pos, ctx_index):
@@ -109,14 +107,34 @@
     def down_block(target):
         return lax.dynamic_slice(down_weight, (target * units, 0), (units, feat))
 
-    flip = [(i, NZ - 1 - i) for i in range(NZ)]
-    other_ids = lax.ppermute(expert_ids, "zh", flip)
-    other_gates = lax.ppermute(gate_values, "zh", flip)
-
-    key_part, value_part, key_pos = gather_keys_values(keys_values, x_index)
-    weight_in = neighbour_blocks(gate_up_block, q_index)
-    weight_out = neighbour_blocks(down_block, q_index)
-    attended = attend(queries, key_part, value_part, key_pos, ctx_index)
+    targets = [jnp.bitwise_xor(q_index, k) for k in range(NQ)]
+    blocks_in = [gate_up_block(target) for target in targets]
+    blocks_out = [down_block(target) for target in targets]
+    weight_in = blocks_in[:1]
+    weight_out = blocks_out[:1]
+    early = tuple(range(1, NQ - 1))
+    late = (NQ - 1,)
+
+    def exchange(first, numbers):
+        sent = [blocks_in[k] for k in numbers] + [blocks_out[k] for k in numbers]
+        first, sent = lax.optimization_barrier((first, sent))
+        moved = [from_neighbour(block, k) for block, k in zip(sent, numbers * 2)]
+        return first, moved
+
+    def keep(last, moved):
+        last, moved = lax.optimization_barrier((last, moved))
+        half = len(moved) // 2
+        weight_in.extend(moved[:half])
+        weight_out.extend(moved[half:])
+        return last
+
+    rows = keys_values.shape[0]
+    column, moved = exchange(gather_column(keys_values, x_index), early)
+    segment = keep(share(column, ("y", "core"), NY * NC), moved).reshape(NCTX * rows, 2 * HD)
+    attended = attend(
+        queries, segment[:, :HD], segment[:, HD:], key_positions(rows), ctx_index
+    )
+    attended, moved = exchange(attended, late)
 
     share_rows = attended.shape[0] // (NPLANE * NZ)
     attended = (
@@ -125,19 +143,33 @@
         .reshape(-1, HD)
     )
     partial = dot(attended, out_weight).astype(bf16).reshape(NPLANE, NZ * share_rows, model)
-    partial = jnp.sum(swap(partial, PLANE).astype(f32), axis=0).reshape(NZ, share_rows, model)
+    partial = keep(swap(partial, PLANE), moved)
+    partial = jnp.sum(partial.astype(f32), axis=0).reshape(NZ, share_rows, model)
     own_group = jnp.arange(NZ)[:, None, None] == zh_index
     partial = partial + jnp.where(own_group, residual.astype(f32)[None], 0.0)
-    outgoing = (
-        partial.astype(bf16)
-        .reshape(NZ * share_rows, NP, 1, 1, width)
-        .transpose(1, 2, 3, 0, 4)
-    )
-    outgoing = jnp.broadcast_to(outgoing, (NP, NQ, NZ, NZ * share_rows, width)).reshape(
-        NCTX * NZ, NZ * share_rows, width
-    )
-    arrived = swap(outgoing, CTX + ("zh",)).reshape(NCTX, NZ, NZ * share_rows, width)
-    hidden = jnp.sum(arrived.astype(f32), axis=1).astype(bf16).reshape(-1, width)
+    outgoing = partial.astype(bf16).reshape(NZ * share_rows, NP, width).transpose(1, 0, 2)
+
+    routing = jnp.concatenate([expert_ids.astype(bf16), *split(gate_values)], axis=1)
+    routing = lax.dynamic_slice_in_dim(routing, ctx_index * share_rows, share_rows, 0)
+    routing = jnp.pad(routing, ((0, 0), (0, HD - routing.shape[1])))
+    routing = jnp.where(own_group, routing[None], 0).reshape(1, NZ * share_rows, HD)
+    routing = jnp.broadcast_to(routing, (NP,) + routing.shape[1:])
+    outgoing = jnp.concatenate([outgoing, routing], axis=2)
+    wide = width + HD
+    outgoing = jnp.broadcast_to(
+        outgoing[:, None, None], (NP, NQ, NZ, NZ * share_rows, wide)
+    ).reshape(NCTX * NZ, NZ * share_rows, wide)
+    arrived = swap(outgoing, CTX + ("zh",)).reshape(NCTX, NZ, NZ * share_rows, wide)
+    arrived = jnp.sum(arrived.astype(f32), axis=1)
+    hidden = arrived[:, :, :width].astype(bf16).reshape(-1, width)
+    choices = expert_ids.shape[1]
+    token_count = expert_ids.shape[0]
+    routing = (
+        arrived[:, :, width : width + 3 * choices]
+        .reshape(NCTX, NZ, share_rows, 3, choices)
+        .transpose(3, 1, 0, 2, 4)
+        .reshape(3, NZ, token_count, choices)
+    )
 
     hidden = jnp.concatenate(
         [
@@ -155,26 +187,18 @@
         ]
     )
 
-    token_count = expert_ids.shape[0]
-    first = zh_index == 0
-    ids = jnp.stack(
-        [jnp.where(first, expert_ids, other_ids), jnp.where(first, other_ids, expert_ids)]
-    )
-    gates = jnp.stack(
-        [jnp.where(first, gate_values, other_gates), jnp.where(first, other_gates, gate_values)]
-    )
+    ids = routing[0].astype(jnp.int32)
     number = jnp.arange(NPLANE, dtype=jnp.int32)
     experts = (number // (NY * NC) * NZ + zh_index) * (NY * NC) + number % (NY * NC)
     picked = ids[..., None] == experts
     chosen = jnp.sum(picked.astype(jnp.int32), axis=2)
     slot_index = jnp.cumsum(chosen, axis=1, dtype=jnp.int32) - chosen
-    gate_table = jnp.sum(jnp.where(picked, gates[..., None], 0.0), axis=2)
+    gate_tables = jnp.sum(jnp.where(picked, routing[1:, ..., None], 0.0), axis=3)
     placed = (chosen[..., None] > 0) & (
         slot_index[..., None] == jnp.arange(CAP, dtype=jnp.int32)
     )
     same = jnp.eye(NZ, dtype=bool)[:, :, None, None, None]
     spread = (placed[:, None] & same).astype(f32)
-    spread_gate = spread * gate_table[:, None, :, :, None]
     slots = NZ * CAP
     total_slots = NPLANE * slots
     selector = (
@@ -183,9 +207,14 @@
         .transpose(4, 1, 5, 2, 0, 3)
         .reshape(total_slots, NZ * token_count)
     )
-    combine = spread_gate.transpose(0, 2, 3, 1, 4).reshape(NZ * token_count, total_slots)
-
-    buckets = dot(selector, hidden).astype(bf16).reshape(NPLANE, slots, width)
+    combine = (
+        (spread * gate_tables[:, :, None, :, :, None])
+        .transpose(0, 1, 3, 4, 2, 5)
+        .reshape(2, NZ * token_count, total_slots)
+        .astype(bf16)
+    )
+
+    buckets = dot(selector, hidden).astype(bf16).reshape(NPLANE, -1, HD)
     buffer = swap(buckets, PLANE).reshape(total_slots, width).astype(f32)
     squares = jnp.sum(buffer * buffer, axis=1)
     scaled = (buffer * gain).astype(bf16)
@@ -195,9 +224,8 @@
 
     rows = total_slots // NP
     chunks = 2 * units // HD
-    high = squares.astype(bf16)
-    low = (squares - high.astype(f32)).astype(bf16)
-    pair = jnp.stack([high.reshape(NP, rows), low.reshape(NP, rows)], axis=1)
+    high, low = split(squares.reshape(NP, rows))
+    pair = jnp.stack([high, low], axis=1)
     pair = jnp.pad(pair, ((0, 0), (0, 14), (0, HD - rows)))
     body = (
         gate_up.astype(bf16).reshape(NP, rows, chunks, HD).transpose(0, 2, 1, 3)
@@ -213,10 +241,8 @@
     expert_out = jnp.concatenate(
         [dot(activated, block).astype(bf16) for block in weight_out], axis=1
     )
-    returned = swap(expert_out.reshape(NPLANE, slots, width), PLANE).reshape(total_slots, width)
-    combine_high = combine.astype(bf16)
-    combine_low = (combine - combine_high.astype(f32)).astype(bf16)
-    mixed = dot(combine_high, returned) + dot(combine_low, returned)
+    returned = swap(expert_out.reshape(NPLANE, -1, HD), PLANE).reshape(total_slots, width)
+    mixed = dot(combine[0], returned) + dot(combine[1], returned)
     mixed = mixed.astype(bf16)
     outgoing = jnp.stack(
         [

time: 376 us -> 378 us (level)
  the two profiles are of different devices: /device:TPU:1 before, /device:TPU:33 now
where the time goes in v2:
time: 378 us; the launch traced here: 377 us
  waiting for transfers between devices  162 us (43%)
  starting transfers between devices  118 us (31%)
  blocking collectives  58.7 us (16%)
  local copies, waits for them, and re-layouts  19 us (5%)
  other arithmetic  10.7 us (3%)
  matrix products  6.48 us (2%)
    all_to_all x8, waiting for transfers between devices, swap(): return lax.all_to_all(array, axes, split_axis=0, concat_axis=0, tiled=True)  121 us
    all_to_all x8, starting transfers between devices, swap(): return lax.all_to_all(array, axes, split_axis=0, concat_axis=0, tiled=True)  101 us
    all_to_all x1, blocking collectives, swap(): return lax.all_to_all(array, axes, split_axis=0, concat_axis=0, tiled=True)  58.7 us
    ppermute x6, waiting for transfers between devices, from_neighbour(): return lax.ppermute(block, 'q', [(i, i ^ k) for i in range(NQ)])  41.4 us
    ppermute x6, starting transfers between devices, from_neighbour(): return lax.ppermute(block, 'q', [(i, i ^ k) for i in range(NQ)])  17.1 us
  transfers between devices with their start and end apart: 14, of which 9 were waited for; matrix products, arithmetic and copies ran while one was open for 2% of the time, Pallas kernels for 0%

profile of v2, /device:TPU:33, one launch (start us, length us, event | category | flops | bytes accessed | tf_op | source)
XLA Modules:
  0.0 376.6 jit_solution(15068639414978369828)
XLA Ops:
  1.5 25.3 %all-to-all-start = ((bf16[16,16,256]{2,1,0:T(8,128)(2,1)}), bf16[16,16,256]{2,1,0:T(8,128)(2,1)S(1)}, u32[]{:S(2)}, u32[]{:S(2)}) async-start(bf16[16,16,256]{2,1,0:T(8,128)(2,1)} %broadcast_in_dim.122), calls=%async_computation | async-start | bytes 262144 | tf_op jit(solution)/shard_map/all_to_all | solution.py:25
  26.9 1.9 dynamic-slice_bitcast_fusion.2
  30.8 15.2 %all-to-all-done = bf16[16,16,256]{2,1,0:T(8,128)(2,1)S(1)} async-done(((bf16[16,16,256]{2,1,0:T(8,128)(2,1)}), bf16[16,16,256]{2,1,0:T(8,128)(2,1)S(1)}, u32[]{:S(2)}, u32[]{:S(2)}) %all-to-all-start) | async-done | bytes 131104 | tf_op jit(solution)/shard_map/all_to_all | solution.py:25
  47.1 9.1 %all-to-all-start.1 = ((bf16[8,16,16,256]{3,2,1,0:T(8,128)(2,1)}), bf16[8,16,16,256]{3,2,1,0:T(8,128)(2,1)S(1)}, u32[]{:S(2)}, u32[]{:S(2)}) async-start(bf16[8,16,16,256]{3,2,1,0:T(8,128)(2,1)} %broadcast_in_dim.123), calls=%async_computation.1 | async-start | bytes 2097152 | tf_op jit(solution)/shard_map/all_to_all | solution.py:25
  56.2 2.4 collective-permute-start
  58.5 2.3 collective-permute-start.1
  60.9 2.9 collective-permute-start.2
  63.8 3.9 %collective-permute-start.3 = (bf16[384,256]{1,0:T(8,128)(2,1)S(1)}, bf16[384,256]{1,0:T(8,128)(2,1)S(1)}, u32[]{:S(2)}, u32[]{:S(2)}) collective-permute-start(bf16[384,256]{1,0:T(8,128)(2,1)S(1)} %get-tuple-element.25), channel_id=1, source_target_pairs={{0,128},{64,192},{128,0},{192,64},{1,129},{65,193},{129,1},{193,65... | collective-permute-start | bytes 589832 | tf_op jit(solution)/shard_map/ppermute | solution.py:37
  68.5 13.2 %collective-permute-done.2 = bf16[384,256]{1,0:T(8,128)(2,1)S(1)} collective-permute-done((bf16[384,256]{1,0:T(8,128)(2,1)}, bf16[384,256]{1,0:T(8,128)(2,1)S(1)}, u32[]{:S(2)}, u32[]{:S(2)}) %collective-permute-start.2) | collective-permute-done | bytes 196640 | tf_op jit(solution)/shard_map/ppermute | solution.py:37
  81.7 4.5 %collective-permute-done.3 = bf16[384,256]{1,0:T(8,128)(2,1)S(1)} collective-permute-done((bf16[384,256]{1,0:T(8,128)(2,1)S(1)}, bf16[384,256]{1,0:T(8,128)(2,1)S(1)}, u32[]{:S(2)}, u32[]{:S(2)}) %collective-permute-start.3) | collective-permute-done | bytes 196640 | tf_op jit(solution)/shard_map/ppermute | solution.py:37
  88.9 1.2 reshape.288
  90.2 8.3 %all-to-all-start.2 = ((bf16[32,4,4096]{2,1,0:T(4,128)(2,1)}), bf16[32,4,4096]{2,1,0:T(4,128)(2,1)S(1)}, u32[]{:S(2)}, u32[]{:S(2)}) async-start(bf16[32,4,4096]{2,1,0:T(4,128)(2,1)} %reshape.288), calls=%async_computation.2 | async-start | bytes 2097152 | tf_op jit(solution)/shard_map/all_to_all | solution.py:25
  98.5 3.7 collective-permute-start.4
  102.7 1.9 collective-permute-start.5
  104.7 23.7 %collective-permute-done.5 = bf16[384,256]{1,0:T(8,128)(2,1)S(1)} collective-permute-done((bf16[384,256]{1,0:T(8,128)(2,1)}, bf16[384,256]{1,0:T(8,128)(2,1)S(1)}, u32[]{:S(2)}, u32[]{:S(2)}) %collective-permute-start.5) | collective-permute-done | bytes 196640 | tf_op jit(solution)/shard_map/ppermute | solution.py:37
  130.6 11.4 %all-to-all-start.3 = ((bf16[32,4,1152]{2,1,0:T(4,128)(2,1)}), bf16[32,4,1152]{2,1,0:T(4,128)(2,1)S(1)}, u32[]{:S(2)}, u32[]{:S(2)}) async-start(bf16[32,4,1152]{2,1,0:T(4,128)(2,1)} %bitcast.16), calls=%async_computation.3 | async-start | bytes 589824 | tf_op jit(solution)/shard_map/all_to_all | solution.py:25
  142.0 35.5 %all-to-all-done.3 = bf16[32,4,1152]{2,1,0:T(4,128)(2,1)S(1)} async-done(((bf16[32,4,1152]{2,1,0:T(4,128)(2,1)}), bf16[32,4,1152]{2,1,0:T(4,128)(2,1)S(1)}, u32[]{:S(2)}, u32[]{:S(2)}) %all-to-all-start.3) | async-done | bytes 294944 | tf_op jit(solution)/shard_map/all_to_all | solution.py:25
  179.4 1.5 fusion.2
  180.9 1.6 convert_element_type.177
  182.9 1.1 reshape.294
  184.1 12.0 %all-to-all-start.4 = ((bf16[32,80,128]{2,1,0:T(8,128)(2,1)}), bf16[32,80,128]{2,1,0:T(8,128)(2,1)S(1)}, u32[]{:S(2)}, u32[]{:S(2)}) async-start(bf16[32,80,128]{2,1,0:T(8,128)(2,1)} %reshape.294), calls=%async_computation.4 | async-start | bytes 1310720 | tf_op jit(solution)/shard_map/all_to_all | solution.py:25
  197.6 11.4 %all-to-all-done.4 = bf16[32,80,128]{2,1,0:T(8,128)(2,1)S(1)} async-done(((bf16[32,80,128]{2,1,0:T(8,128)(2,1)}), bf16[32,80,128]{2,1,0:T(8,128)(2,1)S(1)}, u32[]{:S(2)}, u32[]{:S(2)}) %all-to-all-start.4) | async-done | bytes 655392 | tf_op jit(solution)/shard_map/all_to_all | solution.py:25
  213.1 1.3 fusion.4
  215.2 58.7 %all_to_all.45 = bf16[4,496,128]{2,1,0:T(8,128)(2,1)S(1)} all-to-all(bf16[4,496,128]{2,1,0:T(8,128)(2,1)S(1)} %pad_maximum_fusion.1), channel_id=1, replica_groups=mesh['p'=4,'q'=4,'x'=4,'zh'=2,'y'=4,'core'=2] {'p'}, dimensions={0} | all-to-all | bytes 1015808 | tf_op jit(solution)/shard_map/all_to_all | solution.py:25
  274.9 3.4 all-to-all-start.6
  279.7 15.7 %all-to-all-done.6 = bf16[4,3,80,128]{3,2,1,0:T(8,128)(2,1)S(1)} async-done(((bf16[4,3,80,128]{3,2,1,0:T(8,128)(2,1)}), bf16[4,3,80,128]{3,2,1,0:T(8,128)(2,1)S(1)}, u32[]{:S(2)}, u32[]{:S(2)}) %all-to-all-start.6) | async-done | bytes 245792 | tf_op jit(solution)/shard_map/all_to_all | solution.py:25
  296.3 1.2 convolution_convert_fusion.5
  297.5 1.1 reshape.300
  298.7 13.6 %all-to-all-start.7 = ((bf16[32,80,128]{2,1,0:T(8,128)(2,1)}), bf16[32,80,128]{2,1,0:T(8,128)(2,1)S(1)}, u32[]{:S(2)}, u32[]{:S(2)}) async-start(bf16[32,80,128]{2,1,0:T(8,128)(2,1)} %reshape.300), calls=%async_computation.7 | async-start | bytes 1310720 | tf_op jit(solution)/shard_map/all_to_all | solution.py:25
  312.8 12.4 %all-to-all-done.7 = bf16[32,80,128]{2,1,0:T(8,128)(2,1)S(1)} async-done(((bf16[32,80,128]{2,1,0:T(8,128)(2,1)}), bf16[32,80,128]{2,1,0:T(8,128)(2,1)S(1)}, u32[]{:S(2)}, u32[]{:S(2)}) %all-to-all-start.7) | async-done | bytes 655392 | tf_op jit(solution)/shard_map/all_to_all | solution.py:25
  326.7 18.2 %all-to-all-start.8 = ((bf16[8,32,256]{2,1,0:T(8,128)(2,1)}), bf16[8,32,256]{2,1,0:T(8,128)(2,1)S(1)}, u32[]{:S(2)}, u32[]{:S(2)}) async-start(bf16[8,32,256]{2,1,0:T(8,128)(2,1)} %bitcast.41), calls=%async_computation.8 | async-start | bytes 262144 | tf_op jit(solution)/shard_map/all_to_all | solution.py:25
  345.0 30.9 %all-to-all-done.8 = bf16[8,32,256]{2,1,0:T(8,128)(2,1)S(1)} async-done(((bf16[8,32,256]{2,1,0:T(8,128)(2,1)}), bf16[8,32,256]{2,1,0:T(8,128)(2,1)S(1)}, u32[]{:S(2)}, u32[]{:S(2)}) %all-to-all-start.8) | async-done | bytes 131104 | tf_op jit(solution)/shard_map/all_to_all | solution.py:25
  (159 shorter events, 25.1 us)
Async XLA Ops:
  0.0 88.5 %copy-start = (bf16[128,4096]{1,0:T(8,128)(2,1)S(1)}, bf16[128,4096]{1,0:T(8,128)(2,1)}, u32[]{:S(2)}) copy-start(bf16[128,4096]{1,0:T(8,128)(2,1)} %param.13) | copy-start | bytes 3145732
  0.0 28.8 %copy-start.1 = (bf16[1,256,3072]{2,1,0:T(8,128)(2,1)S(1)}, bf16[1,256,3072]{2,1,0:T(8,128)(2,1)}, u32[]{:S(2)}) copy-start(bf16[1,256,3072]{2,1,0:T(8,128)(2,1)} %param.16) | copy-start | bytes 4718596
  1.5 44.4 %all-to-all-start = ((bf16[16,16,256]{2,1,0:T(8,128)(2,1)}), bf16[16,16,256]{2,1,0:T(8,128)(2,1)S(1)}, u32[]{:S(2)}, u32[]{:S(2)}) async-start(bf16[16,16,256]{2,1,0:T(8,128)(2,1)} %broadcast_in_dim.122), calls=%async_computation | async-start | bytes 262144 | tf_op jit(solution)/shard_map/all_to_all | solution.py:25
  47.1 20.7 %copy-start.2 = (bf16[256,384]{1,0:T(8,128)(2,1)S(1)}, bf16[256,384]{1,0:T(8,128)(2,1)}, u32[]{:S(2)}) copy-start(bf16[256,384]{1,0:T(8,128)(2,1)} %get-tuple-element.38) | copy-start | bytes 589828
  47.1 20.7 %copy-start.3 = (bf16[256,384]{1,0:T(8,128)(2,1)S(1)}, bf16[256,384]{1,0:T(8,128)(2,1)}, u32[]{:S(2)}) copy-start(bf16[256,384]{1,0:T(8,128)(2,1)} %get-tuple-element.39) | copy-start | bytes 589828
  47.1 39.8 %copy-start.24 = (bf16[128,128]{1,0:T(8,128)(2,1)S(1)}, bf16[128,128]{1,0:T(8,128)(2,1)}, u32[]{:S(2)}) copy-start(bf16[128,128]{1,0:T(8,128)(2,1)} %param.9) | copy-start | bytes 98308
  47.1 39.8 %all-to-all-start.1 = ((bf16[8,16,16,256]{3,2,1,0:T(8,128)(2,1)}), bf16[8,16,16,256]{3,2,1,0:T(8,128)(2,1)S(1)}, u32[]{:S(2)}, u32[]{:S(2)}) async-start(bf16[8,16,16,256]{3,2,1,0:T(8,128)(2,1)} %broadcast_in_dim.123), calls=%async_computation.1 | async-start | bytes 2097152 | tf_op jit(solution)/shard_map/all_to_all | solution.py:25
  56.2 30.0 %collective-permute-start = (bf16[256,768]{1,0:T(8,128)(2,1)}, bf16[256,768]{1,0:T(8,128)(2,1)S(1)}, u32[]{:S(2)}, u32[]{:S(2)}) collective-permute-start(bf16[256,768]{1,0:T(8,128)(2,1)} %get-tuple-element.22), channel_id=1, source_target_pairs={{0,64},{64,0},{128,192},{192,128},{1,65},{65,1},{129,193},{193,129... | collective-permute-start | bytes 1179656 | tf_op jit(solution)/shard_map/ppermute | solution.py:37
  58.5 28.3 %collective-permute-start.1 = (bf16[256,768]{1,0:T(8,128)(2,1)}, bf16[256,768]{1,0:T(8,128)(2,1)}, u32[]{:S(2)}, u32[]{:S(2)}) collective-permute-start(bf16[256,768]{1,0:T(8,128)(2,1)} %get-tuple-element.23), channel_id=1, source_target_pairs={{0,128},{64,192},{128,0},{192,64},{1,129},{65,193},{129,1},{193,65... | collective-permute-start | bytes 1179656 | tf_op jit(solution)/shard_map/ppermute | solution.py:37
  60.9 20.8 %collective-permute-start.2 = (bf16[384,256]{1,0:T(8,128)(2,1)}, bf16[384,256]{1,0:T(8,128)(2,1)S(1)}, u32[]{:S(2)}, u32[]{:S(2)}) collective-permute-start(bf16[384,256]{1,0:T(8,128)(2,1)} %get-tuple-element.24), channel_id=1, source_target_pairs={{0,64},{64,0},{128,192},{192,128},{1,65},{65,1},{129,193},{193,129... | collective-permute-start | bytes 589832 | tf_op jit(solution)/shard_map/ppermute | solution.py:37
  63.8 22.4 %collective-permute-start.3 = (bf16[384,256]{1,0:T(8,128)(2,1)S(1)}, bf16[384,256]{1,0:T(8,128)(2,1)S(1)}, u32[]{:S(2)}, u32[]{:S(2)}) collective-permute-start(bf16[384,256]{1,0:T(8,128)(2,1)S(1)} %get-tuple-element.25), channel_id=1, source_target_pairs={{0,128},{64,192},{128,0},{192,64},{1,129},{65,193},{129,1},{193,65... | collective-permute-start | bytes 589832 | tf_op jit(solution)/shard_map/ppermute | solution.py:37
  81.7 4.5 %copy-start.9 = (bf16[384,256]{1,0:T(8,128)(2,1)}, bf16[384,256]{1,0:T(8,128)(2,1)S(1)}, u32[]{:S(2)}) copy-start(bf16[384,256]{1,0:T(8,128)(2,1)S(1)} %collective-permute-done.2) | copy-start | bytes 589828
  90.2 8.3 %copy-start.20 = (s32[32,8]{0,1:T(8,128)S(1)}, s32[32,8]{0,1:T(8,128)}, u32[]{:S(2)}) copy-start(s32[32,8]{0,1:T(8,128)} %param.14) | copy-start | bytes 3076
  90.2 8.3 %copy-start.21 = (f32[32,8]{0,1:T(8,128)S(1)}, f32[32,8]{0,1:T(8,128)}, u32[]{:S(2)}) copy-start(f32[32,8]{0,1:T(8,128)} %param.15) | copy-start | bytes 3076
  90.2 8.4 %copy-start.6 = (bf16[256,768]{1,0:T(8,128)(2,1)S(1)}, bf16[256,768]{1,0:T(8,128)(2,1)}, u32[]{:S(2)}) copy-start(bf16[256,768]{1,0:T(8,128)(2,1)} %pad_maximum_fusion.4) | copy-start | bytes 1179652
  90.2 12.5 %copy-start.17 = (bf16[2,4096]{1,0:T(2,128)(2,1)S(1)}, bf16[2,4096]{1,0:T(2,128)(2,1)}, u32[]{:S(2)}) copy-start(bf16[2,4096]{1,0:T(2,128)(2,1)} %param.11) | copy-start | bytes 49156
  90.2 39.0 %all-to-all-start.2 = ((bf16[32,4,4096]{2,1,0:T(4,128)(2,1)}), bf16[32,4,4096]{2,1,0:T(4,128)(2,1)S(1)}, u32[]{:S(2)}, u32[]{:S(2)}) async-start(bf16[32,4,4096]{2,1,0:T(4,128)(2,1)} %reshape.288), calls=%async_computation.2 | async-start | bytes 2097152 | tf_op jit(solution)/shard_map/all_to_all | solution.py:25
  98.5 30.6 %collective-permute-start.4 = (bf16[256,768]{1,0:T(8,128)(2,1)S(1)}, bf16[256,768]{1,0:T(8,128)(2,1)S(1)}, u32[]{:S(2)}, u32[]{:S(2)}) collective-permute-start(bf16[256,768]{1,0:T(8,128)(2,1)S(1)} %copy-done.6), channel_id=1, source_target_pairs={{0,192},{64,128},{128,64},{192,0},{1,193},{65,129},{129,65},{193,1... | collective-permute-start | bytes 1179656 | tf_op jit(solution)/shard_map/ppermute | solution.py:37
  102.7 25.7 %collective-permute-start.5 = (bf16[384,256]{1,0:T(8,128)(2,1)}, bf16[384,256]{1,0:T(8,128)(2,1)S(1)}, u32[]{:S(2)}, u32[]{:S(2)}) collective-permute-start(bf16[384,256]{1,0:T(8,128)(2,1)} %get-tuple-element.29), channel_id=1, source_target_pairs={{0,192},{64,128},{128,64},{192,0},{1,193},{65,129},{129,65},{193,1... | collective-permute-start | bytes 589832 | tf_op jit(solution)/shard_map/ppermute | solution.py:37
  129.1 48.6 %copy-start.7 = (bf16[256,768]{1,0:T(8,128)(2,1)}, bf16[256,768]{1,0:T(8,128)(2,1)S(1)}, u32[]{:S(2)}) copy-start(bf16[256,768]{1,0:T(8,128)(2,1)S(1)} %collective-permute-done.4) | copy-start | bytes 1179652
  130.6 47.0 %all-to-all-start.3 = ((bf16[32,4,1152]{2,1,0:T(4,128)(2,1)}), bf16[32,4,1152]{2,1,0:T(4,128)(2,1)S(1)}, u32[]{:S(2)}, u32[]{:S(2)}) async-start(bf16[32,4,1152]{2,1,0:T(4,128)(2,1)} %bitcast.16), calls=%async_computation.3 | async-start | bytes 589824 | tf_op jit(solution)/shard_map/all_to_all | solution.py:25
  142.0 36.4 %copy-start.22 = (s32[32]{0:T(128)}, s32[32]{0:T(128)S(1)}, u32[]{:S(2)}) copy-start(s32[32]{0:T(128)S(1)} %fusion.77) | copy-start | bytes 388
  184.1 24.9 %all-to-all-start.4 = ((bf16[32,80,128]{2,1,0:T(8,128)(2,1)}), bf16[32,80,128]{2,1,0:T(8,128)(2,1)S(1)}, u32[]{:S(2)}, u32[]{:S(2)}) async-start(bf16[32,80,128]{2,1,0:T(8,128)(2,1)} %reshape.294), calls=%async_computation.4 | async-start | bytes 1310720 | tf_op jit(solution)/shard_map/all_to_all | solution.py:25
  210.8 1.0 copy-start.8
  273.9 4.4 %copy-start.16 = (pred[2,32,32]{2,1,0:T(8,128)(4,1)S(1)}, pred[2,32,32]{2,1,0:T(8,128)(4,1)}, u32[]{:S(2)}) copy-start(pred[2,32,32]{2,1,0:T(8,128)(4,1)} %copy-done.15) | copy-start | bytes 6148
  274.0 4.7 %copy-start.23 = (s32[32]{0:T(128)S(1)}, s32[32]{0:T(128)}, u32[]{:S(2)}) copy-start(s32[32]{0:T(128)} %copy-done.22) | copy-start | bytes 388
  274.9 20.5 %all-to-all-start.6 = ((bf16[4,3,80,128]{3,2,1,0:T(8,128)(2,1)}), bf16[4,3,80,128]{3,2,1,0:T(8,128)(2,1)S(1)}, u32[]{:S(2)}, u32[]{:S(2)}) async-start(bf16[4,3,80,128]{3,2,1,0:T(8,128)(2,1)} %broadcast_in_dim.143), calls=%async_computation.6 | async-start | bytes 491520 | tf_op jit(solution)/shard_map/all_to_all | solution.py:25
  278.8 16.7 %copy-start.14 = (bf16[384,256]{1,0:T(8,128)(2,1)S(1)}, bf16[384,256]{1,0:T(8,128)(2,1)}, u32[]{:S(2)}) copy-start(bf16[384,256]{1,0:T(8,128)(2,1)} %copy-done.13) | copy-start | bytes 589828
  279.1 16.6 %copy-start.12 = (bf16[384,256]{1,0:T(8,128)(2,1)S(1)}, bf16[384,256]{1,0:T(8,128)(2,1)}, u32[]{:S(2)}) copy-start(bf16[384,256]{1,0:T(8,128)(2,1)} %copy-done.11) | copy-start | bytes 589828
  279.3 16.7 %copy-start.10 = (bf16[384,256]{1,0:T(8,128)(2,1)S(1)}, bf16[384,256]{1,0:T(8,128)(2,1)}, u32[]{:S(2)}) copy-start(bf16[384,256]{1,0:T(8,128)(2,1)} %copy-done.9) | copy-start | bytes 589828
  298.7 26.5 %all-to-all-start.7 = ((bf16[32,80,128]{2,1,0:T(8,128)(2,1)}), bf16[32,80,128]{2,1,0:T(8,128)(2,1)S(1)}, u32[]{:S(2)}, u32[]{:S(2)}) async-start(bf16[32,80,128]{2,1,0:T(8,128)(2,1)} %reshape.300), calls=%async_computation.7 | async-start | bytes 1310720 | tf_op jit(solution)/shard_map/all_to_all | solution.py:25
  326.7 49.2 %all-to-all-start.8 = ((bf16[8,32,256]{2,1,0:T(8,128)(2,1)}), bf16[8,32,256]{2,1,0:T(8,128)(2,1)S(1)}, u32[]{:S(2)}, u32[]{:S(2)}) async-start(bf16[8,32,256]{2,1,0:T(8,128)(2,1)} %bitcast.41), calls=%async_computation.8 | async-start | bytes 262144 | tf_op jit(solution)/shard_map/all_to_all | solution.py:25
  (7 other events, 5.2 us)

commit v3 on v2

--- a/solution.py
+++ b/solution.py
@@ -33,8 +33,19 @@
     return jnp.dot(a, b, preferred_element_type=f32)
 
 
-def from_neighbour(block, k):
-    return lax.ppermute(block, "q", [(i, i ^ k) for i in range(NQ)])
+def from_peer(block, axis, count, k):
+    return lax.ppermute(block, axis, [(i, i ^ k) for i in range(count)])
+
+
+def from_peers(blocks, axis, count):
+    return [blocks[0]] + [from_peer(blocks[k], axis, count, k) for k in range(1, count)]
+
+
+def add(blocks):
+    total = blocks[0].astype(f32)
+    for block in blocks[1:]:
+        total = total + block.astype(f32)
+    return total
 
 
 def split(value):
@@ -54,12 +65,12 @@
 
 def key_positions(rows):
     height = rows // (NY * NC)
-    number = jnp.arange(NCTX * rows, dtype=jnp.int32)
-    return (
-        (number % (NCTX * height)) // height * rows
-        + number // (NCTX * height) * height
-        + number % height
-    )
+    core = jnp.bitwise_xor(jnp.arange(NC, dtype=jnp.int32), lax.axis_index("core"))
+    y = jnp.bitwise_xor(jnp.arange(NY, dtype=jnp.int32), lax.axis_index("y"))
+    piece = y[None, :] * NC + core[:, None]
+    ctx = jnp.arange(NCTX, dtype=jnp.int32)[:, None]
+    row = jnp.arange(height, dtype=jnp.int32)
+    return (piece[:, :, None, None] * height + ctx * rows + row).reshape(-1)
 
 
 def attend(queries, key_part, value_part, key_pos, ctx_index):
@@ -110,31 +121,36 @@
     targets = [jnp.bitwise_xor(q_index, k) for k in range(NQ)]
     blocks_in = [gate_up_block(target) for target in targets]
     blocks_out = [down_block(target) for target in targets]
-    weight_in = blocks_in[:1]
-    weight_out = blocks_out[:1]
-    early = tuple(range(1, NQ - 1))
-    late = (NQ - 1,)
-
-    def exchange(first, numbers):
-        sent = [blocks_in[k] for k in numbers] + [blocks_out[k] for k in numbers]
+    moved_in = {0: blocks_in[0]}
+    moved_out = {0: blocks_out[0]}
+
+    def begin(first, into, out):
+        sent = {"in": {k: blocks_in[k] for k in into}, "out": {k: blocks_out[k] for k in out}}
         first, sent = lax.optimization_barrier((first, sent))
-        moved = [from_neighbour(block, k) for block, k in zip(sent, numbers * 2)]
+        moved = jax.tree.map(lambda block: block, sent)
+        for part in moved.values():
+            for k in part:
+                part[k] = from_peer(part[k], "q", NQ, k)
         return first, moved
 
-    def keep(last, moved):
+    def end(last, moved):
         last, moved = lax.optimization_barrier((last, moved))
-        half = len(moved) // 2
-        weight_in.extend(moved[:half])
-        weight_out.extend(moved[half:])
+        moved_in.update(moved["in"])
+        moved_out.update(moved["out"])
         return last
 
+    half, rest = tuple(range(2, 2 + (NQ - 2) // 2)), tuple(range(2 + (NQ - 2) // 2, NQ))
     rows = keys_values.shape[0]
-    column, moved = exchange(gather_column(keys_values, x_index), early)
-    segment = keep(share(column, ("y", "core"), NY * NC), moved).reshape(NCTX * rows, 2 * HD)
+    keys_values, moved = begin(keys_values, (1,), (1,))
+    column = end(gather_column(keys_values, x_index), moved)
+    column, moved = begin(column, half, ())
+    segment = jnp.concatenate(from_peers([column] * NY, "y", NY), axis=0)
+    segment = jnp.concatenate(from_peers([segment] * NC, "core", NC), axis=0)
+    segment = end(segment, moved).reshape(NCTX * rows, 2 * HD)
     attended = attend(
         queries, segment[:, :HD], segment[:, HD:], key_positions(rows), ctx_index
     )
-    attended, moved = exchange(attended, late)
+    attended, moved = begin(attended, rest, ())
 
     share_rows = attended.shape[0] // (NPLANE * NZ)
     attended = (
@@ -143,41 +159,35 @@
         .reshape(-1, HD)
     )
     partial = dot(attended, out_weight).astype(bf16).reshape(NPLANE, NZ * share_rows, model)
-    partial = keep(swap(partial, PLANE), moved)
+    partial = end(swap(partial, PLANE), moved)
     partial = jnp.sum(partial.astype(f32), axis=0).reshape(NZ, share_rows, model)
     own_group = jnp.arange(NZ)[:, None, None] == zh_index
     partial = partial + jnp.where(own_group, residual.astype(f32)[None], 0.0)
-    outgoing = partial.astype(bf16).reshape(NZ * share_rows, NP, width).transpose(1, 0, 2)
+    outgoing = partial.astype(bf16).reshape(NZ * share_rows, NCTX, feat).transpose(1, 0, 2)
 
     routing = jnp.concatenate([expert_ids.astype(bf16), *split(gate_values)], axis=1)
     routing = lax.dynamic_slice_in_dim(routing, ctx_index * share_rows, share_rows, 0)
     routing = jnp.pad(routing, ((0, 0), (0, HD - routing.shape[1])))
     routing = jnp.where(own_group, routing[None], 0).reshape(1, NZ * share_rows, HD)
-    routing = jnp.broadcast_to(routing, (NP,) + routing.shape[1:])
+    routing = jnp.broadcast_to(routing, (NCTX,) + routing.shape[1:])
     outgoing = jnp.concatenate([outgoing, routing], axis=2)
-    wide = width + HD
+    wide = feat + HD
     outgoing = jnp.broadcast_to(
-        outgoing[:, None, None], (NP, NQ, NZ, NZ * share_rows, wide)
+        outgoing[:, None], (NCTX, NZ, NZ * share_rows, wide)
     ).reshape(NCTX * NZ, NZ * share_rows, wide)
     arrived = swap(outgoing, CTX + ("zh",)).reshape(NCTX, NZ, NZ * share_rows, wide)
     arrived = jnp.sum(arrived.astype(f32), axis=1)
-    hidden = arrived[:, :, :width].astype(bf16).reshape(-1, width)
+    hidden = arrived[:, :, :feat].astype(bf16).reshape(-1, feat)
     choices = expert_ids.shape[1]
     token_count = expert_ids.shape[0]
     routing = (
-        arrived[:, :, width : width + 3 * choices]
+        arrived[:, :, feat : feat + 3 * choices]
         .reshape(NCTX, NZ, share_rows, 3, choices)
         .transpose(3, 1, 0, 2, 4)
         .reshape(3, NZ, token_count, choices)
     )
 
-    hidden = jnp.concatenate(
-        [
-            lax.dynamic_slice_in_dim(hidden, jnp.bitwise_xor(q_index, k) * feat, feat, 1)
-            for k in range(NQ)
-        ],
-        axis=1,
-    )
+    hidden = jnp.concatenate(from_peers([hidden] * NQ, "q", NQ), axis=1)
     gain = jnp.concatenate(
         [
             lax.dynamic_slice_in_dim(
@@ -215,12 +225,13 @@
     )
 
     buckets = dot(selector, hidden).astype(bf16).reshape(NPLANE, -1, HD)
-    buffer = swap(buckets, PLANE).reshape(total_slots, width).astype(f32)
+    buckets, moved = begin(buckets, (), half + rest)
+    buffer = end(swap(buckets, PLANE), moved).reshape(total_slots, width).astype(f32)
     squares = jnp.sum(buffer * buffer, axis=1)
     scaled = (buffer * gain).astype(bf16)
-    gate_up = dot(scaled[:, :feat], weight_in[0])
+    gate_up = dot(scaled[:, :feat], moved_in[0])
     for k in range(1, NQ):
-        gate_up = gate_up + dot(scaled[:, k * feat : (k + 1) * feat], weight_in[k])
+        gate_up = gate_up + dot(scaled[:, k * feat : (k + 1) * feat], moved_in[k])
 
     rows = total_slots // NP
     chunks = 2 * units // HD
@@ -230,27 +241,36 @@
     body = (
         gate_up.astype(bf16).reshape(NP, rows, chunks, HD).transpose(0, 2, 1, 3)
     ).reshape(NP, chunks * rows, HD)
-    summed = jnp.sum(swap(jnp.concatenate([body, pair], axis=1), "p").astype(f32), axis=0)
+    body = jnp.concatenate([body, pair], axis=1)
+    parts = [
+        lax.dynamic_index_in_dim(body, jnp.bitwise_xor(p_index, k), 0, keepdims=False)
+        for k in range(NP)
+    ]
+    summed = add(from_peers(parts, "p", NP))
     square_sum = summed[chunks * rows] + summed[chunks * rows + 1]
     scale = lax.rsqrt(square_sum[:rows] / model + 1e-06)
     pre = summed[: chunks * rows].reshape(2, chunks // 2, rows, HD) * scale[:, None]
     activated = (jax.nn.silu(pre[0]) * pre[1]).astype(bf16)
-    activated = share(activated, "p", NP).reshape(NP, chunks // 2, rows, HD)
+    activated = jnp.stack(from_peers([activated] * NP, "p", NP))
+    activated = jnp.stack(
+        [
+            lax.dynamic_index_in_dim(activated, jnp.bitwise_xor(p_index, k), 0, keepdims=False)
+            for k in range(NP)
+        ]
+    )
     activated = activated.transpose(0, 2, 1, 3).reshape(total_slots, units)
 
     expert_out = jnp.concatenate(
-        [dot(activated, block).astype(bf16) for block in weight_out], axis=1
+        [dot(activated, moved_out[k]).astype(bf16) for k in range(NQ)], axis=1
     )
     returned = swap(expert_out.reshape(NPLANE, -1, HD), PLANE).reshape(total_slots, width)
     mixed = dot(combine[0], returned) + dot(combine[1], returned)
-    mixed = mixed.astype(bf16)
-    outgoing = jnp.stack(
-        [
-            lax.dynamic_slice_in_dim(mixed, jnp.bitwise_xor(q_index, k) * feat, feat, 1)
-            for k in range(NQ)
-        ]
-    ).reshape(NQ * NZ, token_count, feat)
-    landed = jnp.sum(swap(outgoing, ("q", "zh")).astype(f32), axis=0)
+    parts = [mixed[:, k * feat : (k + 1) * feat] for k in range(NQ)]
+    landed = add(from_peers(parts[:1] + [part.astype(bf16) for part in parts[1:]], "q", NQ))
+    landed = landed.reshape(NZ, token_count, feat)
+    passed = lax.dynamic_index_in_dim(landed, NZ - 1 - zh_index, 0, keepdims=False)
+    passed = from_peer(passed.astype(bf16), "zh", NZ, 1)
+    landed = lax.dynamic_index_in_dim(landed, zh_index, 0, keepdims=False) + passed.astype(f32)
     stream = hidden[:, :feat].reshape(NCTX, NZ, share_rows, feat)
     stream = lax.dynamic_index_in_dim(stream, zh_index, 1, keepdims=False)
     return (stream.reshape(token_count, feat).astype(f32) + landed).astype(bf16)

time: 378 us -> 372 us (0.984)
  the two profiles are of different devices: /device:TPU:33 before, /device:TPU:1 now
where the time goes in v3:
time: 372 us; the launch traced here: 370 us
  starting transfers between devices  186 us (50%)
  waiting for transfers between devices  148 us (40%)
  local copies, waits for them, and re-layouts  19.5 us (5%)
  other arithmetic  10.5 us (3%)
  matrix products  5.48 us (1%)
    ppermute x23, starting transfers between devices, from_peer(): return lax.ppermute(block, axis, [(i, i ^ k) for i in range(count)])  117 us
    ppermute x23, waiting for transfers between devices, from_peer(): return lax.ppermute(block, axis, [(i, i ^ k) for i in range(count)])  104 us
    all_to_all x5, starting transfers between devices, swap(): return lax.all_to_all(array, axes, split_axis=0, concat_axis=0, tiled=True)  68.7 us
    all_to_all x5, waiting for transfers between devices, swap(): return lax.all_to_all(array, axes, split_axis=0, concat_axis=0, tiled=True)  44.2 us
  transfers between devices with their start and end apart: 28, of which 13 were waited for; matrix products, arithmetic and copies ran while one was open for 3% of the time, Pallas kernels for 0%

profile of v3, /device:TPU:1, one launch (start us, length us, event | category | flops | bytes accessed | tf_op | source)
XLA Modules:
  0.0 370.3 jit_solution(9179796997910296283)
XLA Ops:
  5.0 26.4 %all-to-all-start = ((bf16[16,16,256]{2,1,0:T(8,128)(2,1)}), bf16[16,16,256]{2,1,0:T(8,128)(2,1)S(1)}, u32[]{:S(2)}, u32[]{:S(2)}) async-start(bf16[16,16,256]{2,1,0:T(8,128)(2,1)} %broadcast_in_dim.113), calls=%async_computation | async-start | bytes 262144 | tf_op jit(solution)/shard_map/all_to_all | solution.py:25
  31.5 3.3 collective-permute-start
  36.9 12.1 %collective-permute-done.1 = bf16[384,256]{1,0:T(8,128)(2,1)S(1)} collective-permute-done((bf16[384,256]{1,0:T(8,128)(2,1)S(1)}, bf16[384,256]{1,0:T(8,128)(2,1)S(1)}, u32[]{:S(2)}, u32[]{:S(2)}) %collective-permute-start.1) | collective-permute-done | bytes 196640 | tf_op jit(solution)/shard_map/ppermute | solution.py:37
  49.8 3.1 all-to-all-done
  52.9 3.2 collective-permute-start.2
  56.1 4.5 %collective-permute-start.3 = (bf16[16,16,256]{2,1,0:T(8,128)(2,1)S(1)}, bf16[16,16,256]{2,1,0:T(8,128)(2,1)S(1)}, u32[]{:S(2)}, u32[]{:S(2)}) collective-permute-start(bf16[16,16,256]{2,1,0:T(8,128)(2,1)S(1)} %all-to-all-done), channel_id=1, source_target_pairs={{0,4},{2,6},{4,0},{6,2},{1,5},{3,7},{5,1},{7,3},{8,12},{10,14},{12... | collective-permute-start | bytes 393224 | tf_op jit(solution)/shard_map/ppermute | solution.py:37
  63.5 5.0 %collective-permute-done.4 = bf16[16,16,256]{2,1,0:T(8,128)(2,1)S(1)} collective-permute-done((bf16[16,16,256]{2,1,0:T(8,128)(2,1)S(1)}, bf16[16,16,256]{2,1,0:T(8,128)(2,1)S(1)}, u32[]{:S(2)}, u32[]{:S(2)}) %collective-permute-start.4) | collective-permute-done | bytes 131104 | tf_op jit(solution)/shard_map/ppermute | solution.py:37
  68.7 5.7 %collective-permute-start.5 = (bf16[64,16,256]{2,1,0:T(8,128)(2,1)S(1)}, bf16[64,16,256]{2,1,0:T(8,128)(2,1)S(1)}, u32[]{:S(2)}, u32[]{:S(2)}) collective-permute-start(bf16[64,16,256]{2,1,0:T(8,128)(2,1)S(1)} %pad_maximum_fusion.1), channel_id=1, source_target_pairs={{0,1},{1,0},{2,3},{3,2},{4,5},{5,4},{6,7},{7,6},{8,9},{9,8},{10,11... | collective-permute-start | bytes 1572872 | tf_op jit(solution)/shard_map/ppermute | solution.py:37
  74.4 4.3 %collective-permute-start.6 = (bf16[256,768]{1,0:T(8,128)(2,1)S(1)}, bf16[256,768]{1,0:T(8,128)(2,1)S(1)}, u32[]{:S(2)}, u32[]{:S(2)}) collective-permute-start(bf16[256,768]{1,0:T(8,128)(2,1)S(1)} %get-tuple-element.30), channel_id=1, source_target_pairs={{0,128},{64,192},{128,0},{192,64},{1,129},{65,193},{129,1},{193,65... | collective-permute-start | bytes 1179656 | tf_op jit(solution)/shard_map/ppermute | solution.py:37
  78.8 17.4 %collective-permute-done.6 = bf16[256,768]{1,0:T(8,128)(2,1)S(1)} collective-permute-done((bf16[256,768]{1,0:T(8,128)(2,1)S(1)}, bf16[256,768]{1,0:T(8,128)(2,1)S(1)}, u32[]{:S(2)}, u32[]{:S(2)}) %collective-permute-start.6) | collective-permute-done | bytes 393248 | tf_op jit(solution)/shard_map/ppermute | solution.py:37
  99.5 5.0 %all-to-all-start.1 = ((bf16[32,4,4096]{2,1,0:T(4,128)(2,1)}), bf16[32,4,4096]{2,1,0:T(4,128)(2,1)S(1)}, u32[]{:S(2)}, u32[]{:S(2)}) async-start(bf16[32,4,4096]{2,1,0:T(4,128)(2,1)} %reshape.306), calls=%async_computation.1 | async-start | bytes 2097152 | tf_op jit(solution)/shard_map/all_to_all | solution.py:25
  104.6 3.9 %collective-permute-start.7 = (bf16[256,768]{1,0:T(8,128)(2,1)S(1)}, bf16[256,768]{1,0:T(8,128)(2,1)S(1)}, u32[]{:S(2)}, u32[]{:S(2)}) collective-permute-start(bf16[256,768]{1,0:T(8,128)(2,1)S(1)} %copy-done.4), channel_id=1, source_target_pairs={{0,192},{64,128},{128,64},{192,0},{1,193},{65,129},{129,65},{193,1... | collective-permute-start | bytes 1179656 | tf_op jit(solution)/shard_map/ppermute | solution.py:37
  109.0 9.8 %collective-permute-done.7 = bf16[256,768]{1,0:T(8,128)(2,1)S(1)} collective-permute-done((bf16[256,768]{1,0:T(8,128)(2,1)S(1)}, bf16[256,768]{1,0:T(8,128)(2,1)S(1)}, u32[]{:S(2)}, u32[]{:S(2)}) %collective-permute-start.7) | collective-permute-done | bytes 393248 | tf_op jit(solution)/shard_map/ppermute | solution.py:37
  118.8 2.7 all-to-all-done.1
  122.7 18.7 %all-to-all-start.2 = ((bf16[32,4,384]{2,1,0:T(4,128)(2,1)}), bf16[32,4,384]{2,1,0:T(4,128)(2,1)S(1)}, u32[]{:S(2)}, u32[]{:S(2)}) async-start(bf16[32,4,384]{2,1,0:T(4,128)(2,1)} %bitcast.14), calls=%async_computation.2 | async-start | bytes 196608 | tf_op jit(solution)/shard_map/all_to_all | solution.py:25
  141.4 26.0 %all-to-all-done.2 = bf16[32,4,384]{2,1,0:T(4,128)(2,1)S(1)} async-done(((bf16[32,4,384]{2,1,0:T(4,128)(2,1)}), bf16[32,4,384]{2,1,0:T(4,128)(2,1)S(1)}, u32[]{:S(2)}, u32[]{:S(2)}) %all-to-all-start.2) | async-done | bytes 98336 | tf_op jit(solution)/shard_map/all_to_all | solution.py:25
  170.2 3.2 collective-permute-start.8
  173.3 4.0 %collective-permute-start.9 = (bf16[64,256]{1,0:T(8,128)(2,1)S(1)}, bf16[64,256]{1,0:T(8,128)(2,1)S(1)}, u32[]{:S(2)}, u32[]{:S(2)}) collective-permute-start(bf16[64,256]{1,0:T(8,128)(2,1)S(1)} %reshape.310), channel_id=1, source_target_pairs={{0,128},{64,192},{128,0},{192,64},{1,129},{65,193},{129,1},{193,65... | collective-permute-start | bytes 98312 | tf_op jit(solution)/shard_map/ppermute | solution.py:37
  182.6 10.4 %all-to-all-start.3 = ((bf16[32,80,128]{2,1,0:T(8,128)(2,1)}), bf16[32,80,128]{2,1,0:T(8,128)(2,1)S(1)}, u32[]{:S(2)}, u32[]{:S(2)}) async-start(bf16[32,80,128]{2,1,0:T(8,128)(2,1)} %reshape.311), calls=%async_computation.3 | async-start | bytes 1310720 | tf_op jit(solution)/shard_map/all_to_all | solution.py:25
  198.7 3.2 collective-permute-start.12
  202.0 11.5 %collective-permute-done.11 = bf16[384,256]{1,0:T(8,128)(2,1)S(1)} collective-permute-done((bf16[384,256]{1,0:T(8,128)(2,1)S(1)}, bf16[384,256]{1,0:T(8,128)(2,1)S(1)}, u32[]{:S(2)}, u32[]{:S(2)}) %collective-permute-start.11) | collective-permute-done | bytes 196640 | tf_op jit(solution)/shard_map/ppermute | solution.py:37
  221.3 2.9 collective-permute-start.13
  226.4 15.9 %collective-permute-start.15 = (bf16[496,128]{1,0:T(8,128)(2,1)S(1)}, bf16[496,128]{1,0:T(8,128)(2,1)S(1)}, u32[]{:S(2)}, u32[]{:S(2)}) collective-permute-start(bf16[496,128]{1,0:T(8,128)(2,1)S(1)} %get-tuple-element.58), channel_id=1, source_target_pairs={{0,768},{256,512},{512,256},{768,0},{1,769},{257,513},{513,257},{7... | collective-permute-start | bytes 380936 | tf_op jit(solution)/shard_map/ppermute | solution.py:37
  243.3 19.4 %collective-permute-done.15 = bf16[496,128]{1,0:T(8,128)(2,1)S(1)} collective-permute-done((bf16[496,128]{1,0:T(8,128)(2,1)S(1)}, bf16[496,128]{1,0:T(8,128)(2,1)S(1)}, u32[]{:S(2)}, u32[]{:S(2)}) %collective-permute-start.15) | collective-permute-done | bytes 127008 | tf_op jit(solution)/shard_map/ppermute | solution.py:37
  263.0 19.6 %collective-permute-start.16 = (bf16[3,80,128]{2,1,0:T(8,128)(2,1)S(1)}, bf16[3,80,128]{2,1,0:T(8,128)(2,1)S(1)}, u32[]{:S(2)}, u32[]{:S(2)}) collective-permute-start(bf16[3,80,128]{2,1,0:T(8,128)(2,1)S(1)} %fusion.48), channel_id=1, source_target_pairs={{0,256},{256,0},{512,768},{768,512},{1,257},{257,1},{513,769},{769... | collective-permute-start | bytes 184328 | tf_op jit(solution)/shard_map/ppermute | solution.py:37
  284.5 11.8 %collective-permute-start.18 = (bf16[3,80,128]{2,1,0:T(8,128)(2,1)S(1)}, bf16[3,80,128]{2,1,0:T(8,128)(2,1)S(1)}, u32[]{:S(2)}, u32[]{:S(2)}) collective-permute-start(bf16[3,80,128]{2,1,0:T(8,128)(2,1)S(1)} %fusion.48), channel_id=1, source_target_pairs={{0,768},{256,512},{512,256},{768,0},{1,769},{257,513},{513,257},{7... | collective-permute-start | bytes 184328 | tf_op jit(solution)/shard_map/ppermute | solution.py:37
  296.4 13.9 %collective-permute-done.17 = bf16[3,80,128]{2,1,0:T(8,128)(2,1)S(1)} collective-permute-done((bf16[3,80,128]{2,1,0:T(8,128)(2,1)S(1)}, bf16[3,80,128]{2,1,0:T(8,128)(2,1)S(1)}, u32[]{:S(2)}, u32[]{:S(2)}) %collective-permute-start.17) | collective-permute-done | bytes 61472 | tf_op jit(solution)/shard_map/ppermute | solution.py:37
  314.2 8.1 %all-to-all-start.4 = ((bf16[32,80,128]{2,1,0:T(8,128)(2,1)}), bf16[32,80,128]{2,1,0:T(8,128)(2,1)S(1)}, u32[]{:S(2)}, u32[]{:S(2)}) async-start(bf16[32,80,128]{2,1,0:T(8,128)(2,1)} %reshape.317), calls=%async_computation.4 | async-start | bytes 1310720 | tf_op jit(solution)/shard_map/all_to_all | solution.py:25
  322.9 12.3 %all-to-all-done.4 = bf16[32,80,128]{2,1,0:T(8,128)(2,1)S(1)} async-done(((bf16[32,80,128]{2,1,0:T(8,128)(2,1)}), bf16[32,80,128]{2,1,0:T(8,128)(2,1)S(1)}, u32[]{:S(2)}, u32[]{:S(2)}) %all-to-all-start.4) | async-done | bytes 655392 | tf_op jit(solution)/shard_map/all_to_all | solution.py:25
  340.0 5.5 %collective-permute-start.21 = (bf16[64,256]{1,0:T(8,128)(2,1)S(1)}, bf16[64,256]{1,0:T(8,128)(2,1)S(1)}, u32[]{:S(2)}, u32[]{:S(2)}) collective-permute-start(bf16[64,256]{1,0:T(8,128)(2,1)S(1)} %get-tuple-element.66), channel_id=1, source_target_pairs={{0,192},{64,128},{128,64},{192,0},{1,193},{65,129},{129,65},{193,1... | collective-permute-start | bytes 98312 | tf_op jit(solution)/shard_map/ppermute | solution.py:37
  346.8 9.4 %collective-permute-start.22 = (bf16[32,256]{1,0:T(8,128)(2,1)S(1)}, bf16[32,256]{1,0:T(8,128)(2,1)S(1)}, u32[]{:S(2)}, u32[]{:S(2)}) collective-permute-start(bf16[32,256]{1,0:T(8,128)(2,1)S(1)} %fusion.69), channel_id=1, source_target_pairs={{0,8},{8,0},{1,9},{9,1},{2,10},{10,2},{3,11},{11,3},{4,12},{12,4},... | collective-permute-start | bytes 49160 | tf_op jit(solution)/shard_map/ppermute | solution.py:37
  356.3 13.3 %collective-permute-done.22 = bf16[32,256]{1,0:T(8,128)(2,1)S(1)} collective-permute-done((bf16[32,256]{1,0:T(8,128)(2,1)S(1)}, bf16[32,256]{1,0:T(8,128)(2,1)S(1)}, u32[]{:S(2)}, u32[]{:S(2)}) %collective-permute-start.22) | collective-permute-done | bytes 16416 | tf_op jit(solution)/shard_map/ppermute | solution.py:37
  (202 shorter events, 53.3 us)
Async XLA Ops:
  0.0 97.8 %copy-start = (bf16[128,4096]{1,0:T(8,128)(2,1)S(1)}, bf16[128,4096]{1,0:T(8,128)(2,1)}, u32[]{:S(2)}) copy-start(bf16[128,4096]{1,0:T(8,128)(2,1)} %param.13) | copy-start | bytes 3145732
  5.0 47.9 %all-to-all-start = ((bf16[16,16,256]{2,1,0:T(8,128)(2,1)}), bf16[16,16,256]{2,1,0:T(8,128)(2,1)S(1)}, u32[]{:S(2)}, u32[]{:S(2)}) async-start(bf16[16,16,256]{2,1,0:T(8,128)(2,1)} %broadcast_in_dim.113), calls=%async_computation | async-start | bytes 262144 | tf_op jit(solution)/shard_map/all_to_all | solution.py:25
  31.5 18.3 %collective-permute-start = (bf16[256,768]{1,0:T(8,128)(2,1)S(1)}, bf16[256,768]{1,0:T(8,128)(2,1)S(1)}, u32[]{:S(2)}, u32[]{:S(2)}) collective-permute-start(bf16[256,768]{1,0:T(8,128)(2,1)S(1)} %get-tuple-element.26), channel_id=1, source_target_pairs={{0,64},{64,0},{128,192},{192,128},{1,65},{65,1},{129,193},{193,129... | collective-permute-start | bytes 1179656 | tf_op jit(solution)/shard_map/ppermute | solution.py:37
  34.7 14.3 %collective-permute-start.1 = (bf16[384,256]{1,0:T(8,128)(2,1)S(1)}, bf16[384,256]{1,0:T(8,128)(2,1)S(1)}, u32[]{:S(2)}, u32[]{:S(2)}) collective-permute-start(bf16[384,256]{1,0:T(8,128)(2,1)S(1)} %get-tuple-element.27), channel_id=1, source_target_pairs={{0,64},{64,0},{128,192},{192,128},{1,65},{65,1},{129,193},{193,129... | collective-permute-start | bytes 589832 | tf_op jit(solution)/shard_map/ppermute | solution.py:37
  52.9 10.6 %collective-permute-start.2 = (bf16[16,16,256]{2,1,0:T(8,128)(2,1)S(1)}, bf16[16,16,256]{2,1,0:T(8,128)(2,1)S(1)}, u32[]{:S(2)}, u32[]{:S(2)}) collective-permute-start(bf16[16,16,256]{2,1,0:T(8,128)(2,1)S(1)} %all-to-all-done), channel_id=1, source_target_pairs={{0,2},{2,0},{4,6},{6,4},{1,3},{3,1},{5,7},{7,5},{8,10},{10,8},{12,... | collective-permute-start | bytes 393224 | tf_op jit(solution)/shard_map/ppermute | solution.py:37
  56.1 7.4 %collective-permute-start.3 = (bf16[16,16,256]{2,1,0:T(8,128)(2,1)S(1)}, bf16[16,16,256]{2,1,0:T(8,128)(2,1)S(1)}, u32[]{:S(2)}, u32[]{:S(2)}) collective-permute-start(bf16[16,16,256]{2,1,0:T(8,128)(2,1)S(1)} %all-to-all-done), channel_id=1, source_target_pairs={{0,4},{2,6},{4,0},{6,2},{1,5},{3,7},{5,1},{7,3},{8,12},{10,14},{12... | collective-permute-start | bytes 393224 | tf_op jit(solution)/shard_map/ppermute | solution.py:37
  60.6 7.9 %collective-permute-start.4 = (bf16[16,16,256]{2,1,0:T(8,128)(2,1)S(1)}, bf16[16,16,256]{2,1,0:T(8,128)(2,1)S(1)}, u32[]{:S(2)}, u32[]{:S(2)}) collective-permute-start(bf16[16,16,256]{2,1,0:T(8,128)(2,1)S(1)} %all-to-all-done), channel_id=1, source_target_pairs={{0,6},{2,4},{4,2},{6,0},{1,7},{3,5},{5,3},{7,1},{8,14},{10,12},{12... | collective-permute-start | bytes 393224 | tf_op jit(solution)/shard_map/ppermute | solution.py:37
  68.6 27.6 %copy-start.26 = (bf16[128,128]{1,0:T(8,128)(2,1)S(1)}, bf16[128,128]{1,0:T(8,128)(2,1)}, u32[]{:S(2)}) copy-start(bf16[128,128]{1,0:T(8,128)(2,1)} %param.9) | copy-start | bytes 98308
  68.7 10.1 %collective-permute-start.5 = (bf16[64,16,256]{2,1,0:T(8,128)(2,1)S(1)}, bf16[64,16,256]{2,1,0:T(8,128)(2,1)S(1)}, u32[]{:S(2)}, u32[]{:S(2)}) collective-permute-start(bf16[64,16,256]{2,1,0:T(8,128)(2,1)S(1)} %pad_maximum_fusion.1), channel_id=1, source_target_pairs={{0,1},{1,0},{2,3},{3,2},{4,5},{5,4},{6,7},{7,6},{8,9},{9,8},{10,11... | collective-permute-start | bytes 1572872 | tf_op jit(solution)/shard_map/ppermute | solution.py:37
  74.4 21.8 %collective-permute-start.6 = (bf16[256,768]{1,0:T(8,128)(2,1)S(1)}, bf16[256,768]{1,0:T(8,128)(2,1)S(1)}, u32[]{:S(2)}, u32[]{:S(2)}) collective-permute-start(bf16[256,768]{1,0:T(8,128)(2,1)S(1)} %get-tuple-element.30), channel_id=1, source_target_pairs={{0,128},{64,192},{128,0},{192,64},{1,129},{65,193},{129,1},{193,65... | collective-permute-start | bytes 1179656 | tf_op jit(solution)/shard_map/ppermute | solution.py:37
  99.5 22.0 %all-to-all-start.1 = ((bf16[32,4,4096]{2,1,0:T(4,128)(2,1)}), bf16[32,4,4096]{2,1,0:T(4,128)(2,1)S(1)}, u32[]{:S(2)}, u32[]{:S(2)}) async-start(bf16[32,4,4096]{2,1,0:T(4,128)(2,1)} %reshape.306), calls=%async_computation.1 | async-start | bytes 2097152 | tf_op jit(solution)/shard_map/all_to_all | solution.py:25
  104.6 14.2 %collective-permute-start.7 = (bf16[256,768]{1,0:T(8,128)(2,1)S(1)}, bf16[256,768]{1,0:T(8,128)(2,1)S(1)}, u32[]{:S(2)}, u32[]{:S(2)}) collective-permute-start(bf16[256,768]{1,0:T(8,128)(2,1)S(1)} %copy-done.4), channel_id=1, source_target_pairs={{0,192},{64,128},{128,64},{192,0},{1,193},{65,129},{129,65},{193,1... | collective-permute-start | bytes 1179656 | tf_op jit(solution)/shard_map/ppermute | solution.py:37
  118.8 49.2 %copy-start.5 = (bf16[256,768]{1,0:T(8,128)(2,1)}, bf16[256,768]{1,0:T(8,128)(2,1)S(1)}, u32[]{:S(2)}) copy-start(bf16[256,768]{1,0:T(8,128)(2,1)S(1)} %collective-permute-done.7) | copy-start | bytes 1179652
  122.7 44.7 %all-to-all-start.2 = ((bf16[32,4,384]{2,1,0:T(4,128)(2,1)}), bf16[32,4,384]{2,1,0:T(4,128)(2,1)S(1)}, u32[]{:S(2)}, u32[]{:S(2)}) async-start(bf16[32,4,384]{2,1,0:T(4,128)(2,1)} %bitcast.14), calls=%async_computation.2 | async-start | bytes 196608 | tf_op jit(solution)/shard_map/all_to_all | solution.py:25
  168.0 13.1 %collective-permute-start.10 = (bf16[64,256]{1,0:T(8,128)(2,1)S(1)}, bf16[64,256]{1,0:T(8,128)(2,1)S(1)}, u32[]{:S(2)}, u32[]{:S(2)}) collective-permute-start(bf16[64,256]{1,0:T(8,128)(2,1)S(1)} %reshape.310), channel_id=1, source_target_pairs={{0,192},{64,128},{128,64},{192,0},{1,193},{65,129},{129,65},{193,1... | collective-permute-start | bytes 98312 | tf_op jit(solution)/shard_map/ppermute | solution.py:37
  170.2 11.0 %collective-permute-start.8 = (bf16[64,256]{1,0:T(8,128)(2,1)S(1)}, bf16[64,256]{1,0:T(8,128)(2,1)S(1)}, u32[]{:S(2)}, u32[]{:S(2)}) collective-permute-start(bf16[64,256]{1,0:T(8,128)(2,1)S(1)} %reshape.310), channel_id=1, source_target_pairs={{0,64},{64,0},{128,192},{192,128},{1,65},{65,1},{129,193},{193,129... | collective-permute-start | bytes 98312 | tf_op jit(solution)/shard_map/ppermute | solution.py:37
  173.3 7.8 %collective-permute-start.9 = (bf16[64,256]{1,0:T(8,128)(2,1)S(1)}, bf16[64,256]{1,0:T(8,128)(2,1)S(1)}, u32[]{:S(2)}, u32[]{:S(2)}) collective-permute-start(bf16[64,256]{1,0:T(8,128)(2,1)S(1)} %reshape.310), channel_id=1, source_target_pairs={{0,128},{64,192},{128,0},{192,64},{1,129},{65,193},{129,1},{193,65... | collective-permute-start | bytes 98312 | tf_op jit(solution)/shard_map/ppermute | solution.py:37
  182.6 31.0 %all-to-all-start.3 = ((bf16[32,80,128]{2,1,0:T(8,128)(2,1)}), bf16[32,80,128]{2,1,0:T(8,128)(2,1)S(1)}, u32[]{:S(2)}, u32[]{:S(2)}) async-start(bf16[32,80,128]{2,1,0:T(8,128)(2,1)} %reshape.311), calls=%async_computation.3 | async-start | bytes 1310720 | tf_op jit(solution)/shard_map/all_to_all | solution.py:25
  196.1 17.5 %collective-permute-start.11 = (bf16[384,256]{1,0:T(8,128)(2,1)S(1)}, bf16[384,256]{1,0:T(8,128)(2,1)S(1)}, u32[]{:S(2)}, u32[]{:S(2)}) collective-permute-start(bf16[384,256]{1,0:T(8,128)(2,1)S(1)} %copy-done.12), channel_id=1, source_target_pairs={{0,128},{64,192},{128,0},{192,64},{1,129},{65,193},{129,1},{193,65... | collective-permute-start | bytes 589832 | tf_op jit(solution)/shard_map/ppermute | solution.py:37
  198.7 14.9 %collective-permute-start.12 = (bf16[384,256]{1,0:T(8,128)(2,1)S(1)}, bf16[384,256]{1,0:T(8,128)(2,1)S(1)}, u32[]{:S(2)}, u32[]{:S(2)}) collective-permute-start(bf16[384,256]{1,0:T(8,128)(2,1)S(1)} %copy-done.11), channel_id=1, source_target_pairs={{0,192},{64,128},{128,64},{192,0},{1,193},{65,129},{129,65},{193,1... | collective-permute-start | bytes 589832 | tf_op jit(solution)/shard_map/ppermute | solution.py:37
  221.3 21.9 %collective-permute-start.13 = (bf16[496,128]{1,0:T(8,128)(2,1)S(1)}, bf16[496,128]{1,0:T(8,128)(2,1)S(1)}, u32[]{:S(2)}, u32[]{:S(2)}) collective-permute-start(bf16[496,128]{1,0:T(8,128)(2,1)S(1)} %get-tuple-element.56), channel_id=1, source_target_pairs={{0,256},{256,0},{512,768},{768,512},{1,257},{257,1},{513,769},{769... | collective-permute-start | bytes 380936 | tf_op jit(solution)/shard_map/ppermute | solution.py:37
  224.3 19.0 %collective-permute-start.14 = (bf16[496,128]{1,0:T(8,128)(2,1)S(1)}, bf16[496,128]{1,0:T(8,128)(2,1)S(1)}, u32[]{:S(2)}, u32[]{:S(2)}) collective-permute-start(bf16[496,128]{1,0:T(8,128)(2,1)S(1)} %get-tuple-element.57), channel_id=1, source_target_pairs={{0,512},{256,768},{512,0},{768,256},{1,513},{257,769},{513,1},{769... | collective-permute-start | bytes 380936 | tf_op jit(solution)/shard_map/ppermute | solution.py:37
  226.4 36.3 %collective-permute-start.15 = (bf16[496,128]{1,0:T(8,128)(2,1)S(1)}, bf16[496,128]{1,0:T(8,128)(2,1)S(1)}, u32[]{:S(2)}, u32[]{:S(2)}) collective-permute-start(bf16[496,128]{1,0:T(8,128)(2,1)S(1)} %get-tuple-element.58), channel_id=1, source_target_pairs={{0,768},{256,512},{512,256},{768,0},{1,769},{257,513},{513,257},{7... | collective-permute-start | bytes 380936 | tf_op jit(solution)/shard_map/ppermute | solution.py:37
  262.9 47.7 %copy-start.14 = (bf16[384,256]{1,0:T(8,128)(2,1)S(1)}, bf16[384,256]{1,0:T(8,128)(2,1)}, u32[]{:S(2)}) copy-start(bf16[384,256]{1,0:T(8,128)(2,1)} %copy-done.13) | copy-start | bytes 589828
  263.0 33.4 %collective-permute-start.16 = (bf16[3,80,128]{2,1,0:T(8,128)(2,1)S(1)}, bf16[3,80,128]{2,1,0:T(8,128)(2,1)S(1)}, u32[]{:S(2)}, u32[]{:S(2)}) collective-permute-start(bf16[3,80,128]{2,1,0:T(8,128)(2,1)S(1)} %fusion.48), channel_id=1, source_target_pairs={{0,256},{256,0},{512,768},{768,512},{1,257},{257,1},{513,769},{769... | collective-permute-start | bytes 184328 | tf_op jit(solution)/shard_map/ppermute | solution.py:37
  282.6 27.7 %collective-permute-start.17 = (bf16[3,80,128]{2,1,0:T(8,128)(2,1)S(1)}, bf16[3,80,128]{2,1,0:T(8,128)(2,1)S(1)}, u32[]{:S(2)}, u32[]{:S(2)}) collective-permute-start(bf16[3,80,128]{2,1,0:T(8,128)(2,1)S(1)} %fusion.48), channel_id=1, source_target_pairs={{0,512},{256,768},{512,0},{768,256},{1,513},{257,769},{513,1},{769... | collective-permute-start | bytes 184328 | tf_op jit(solution)/shard_map/ppermute | solution.py:37
  284.5 25.8 %collective-permute-start.18 = (bf16[3,80,128]{2,1,0:T(8,128)(2,1)S(1)}, bf16[3,80,128]{2,1,0:T(8,128)(2,1)S(1)}, u32[]{:S(2)}, u32[]{:S(2)}) collective-permute-start(bf16[3,80,128]{2,1,0:T(8,128)(2,1)S(1)} %fusion.48), channel_id=1, source_target_pairs={{0,768},{256,512},{512,256},{768,0},{1,769},{257,513},{513,257},{7... | collective-permute-start | bytes 184328 | tf_op jit(solution)/shard_map/ppermute | solution.py:37
  314.2 21.1 %all-to-all-start.4 = ((bf16[32,80,128]{2,1,0:T(8,128)(2,1)}), bf16[32,80,128]{2,1,0:T(8,128)(2,1)S(1)}, u32[]{:S(2)}, u32[]{:S(2)}) async-start(bf16[32,80,128]{2,1,0:T(8,128)(2,1)} %reshape.317), calls=%async_computation.4 | async-start | bytes 1310720 | tf_op jit(solution)/shard_map/all_to_all | solution.py:25
  336.1 9.3 %collective-permute-start.19 = (bf16[64,256]{1,0:T(8,128)(2,1)S(1)}, bf16[64,256]{1,0:T(8,128)(2,1)S(1)}, u32[]{:S(2)}, u32[]{:S(2)}) collective-permute-start(bf16[64,256]{1,0:T(8,128)(2,1)S(1)} %get-tuple-element.65), channel_id=1, source_target_pairs={{0,64},{64,0},{128,192},{192,128},{1,65},{65,1},{129,193},{193,129... | collective-permute-start | bytes 98312 | tf_op jit(solution)/shard_map/ppermute | solution.py:37
  338.0 7.4 %collective-permute-start.20 = (bf16[64,256]{1,0:T(8,128)(2,1)S(1)}, bf16[64,256]{1,0:T(8,128)(2,1)S(1)}, u32[]{:S(2)}, u32[]{:S(2)}) collective-permute-start(bf16[64,256]{1,0:T(8,128)(2,1)S(1)} %get-tuple-element.67), channel_id=1, source_target_pairs={{0,128},{64,192},{128,0},{192,64},{1,129},{65,193},{129,1},{193,65... | collective-permute-start | bytes 98312 | tf_op jit(solution)/shard_map/ppermute | solution.py:37
  340.0 6.8 %collective-permute-start.21 = (bf16[64,256]{1,0:T(8,128)(2,1)S(1)}, bf16[64,256]{1,0:T(8,128)(2,1)S(1)}, u32[]{:S(2)}, u32[]{:S(2)}) collective-permute-start(bf16[64,256]{1,0:T(8,128)(2,1)S(1)} %get-tuple-element.66), channel_id=1, source_target_pairs={{0,192},{64,128},{128,64},{192,0},{1,193},{65,129},{129,65},{193,1... | collective-permute-start | bytes 98312 | tf_op jit(solution)/shard_map/ppermute | solution.py:37
  346.8 22.9 %collective-permute-start.22 = (bf16[32,256]{1,0:T(8,128)(2,1)S(1)}, bf16[32,256]{1,0:T(8,128)(2,1)S(1)}, u32[]{:S(2)}, u32[]{:S(2)}) collective-permute-start(bf16[32,256]{1,0:T(8,128)(2,1)S(1)} %fusion.69), channel_id=1, source_target_pairs={{0,8},{8,0},{1,9},{9,1},{2,10},{10,2},{3,11},{11,3},{4,12},{12,4},... | collective-permute-start | bytes 49160 | tf_op jit(solution)/shard_map/ppermute | solution.py:37
  (23 other events, 139.9 us)

commit v4 on v3

--- a/solution.py
+++ b/solution.py
@@ -1,6 +1,8 @@
 import jax
 import jax.numpy as jnp
 from jax import lax
+from jax.experimental import pallas as pl
+from jax.experimental.pallas import tpu as pltpu
 from jax.sharding import Mesh, PartitionSpec as P
 
 HD = 128
@@ -65,12 +67,65 @@
 
 def key_positions(rows):
     height = rows // (NY * NC)
-    core = jnp.bitwise_xor(jnp.arange(NC, dtype=jnp.int32), lax.axis_index("core"))
-    y = jnp.bitwise_xor(jnp.arange(NY, dtype=jnp.int32), lax.axis_index("y"))
-    piece = y[None, :] * NC + core[:, None]
-    ctx = jnp.arange(NCTX, dtype=jnp.int32)[:, None]
-    row = jnp.arange(height, dtype=jnp.int32)
-    return (piece[:, :, None, None] * height + ctx * rows + row).reshape(-1)
+    number = jnp.arange(NCTX * rows, dtype=jnp.int32)
+    return (
+        (number % (NCTX * height)) // height * rows
+        + number // (NCTX * height) * height
+        + number % height
+    )
+
+
+def call(kernel, shape, *operands):
+    return pl.pallas_call(
+        kernel,
+        out_shape=jax.ShapeDtypeStruct(shape, bf16),
+        compiler_params=pltpu.CompilerParams(vmem_limit_bytes=32 * 1024 * 1024),
+    )(*operands)
+
+
+def gate_up_kernel(buffer_ref, gain_ref, *refs):
+    out_ref = refs[-1]
+    feat, units = refs[0].shape
+    rows = buffer_ref.shape[0] // NP
+    buffer = buffer_ref[...].astype(f32)
+    squares = jnp.sum(buffer * buffer, axis=1, keepdims=True)
+    scaled = (buffer * gain_ref[...]).astype(bf16)
+    for half in range(2):
+        total = dot(scaled[:, :feat], refs[half * NQ][...])
+        for k in range(1, NQ):
+            total = total + dot(scaled[:, k * feat : (k + 1) * feat], refs[half * NQ + k][...])
+        total = total.astype(bf16)
+        for p in range(NP):
+            for chunk in range(units // HD):
+                start = (half * (units // HD) + chunk) * rows
+                out_ref[p, start : start + rows, :] = total[
+                    p * rows : (p + 1) * rows, chunk * HD : (chunk + 1) * HD
+                ]
+    body = 2 * (units // HD) * rows
+    lane = lax.broadcasted_iota(jnp.int32, (rows, HD), 1)
+    on_diagonal = lane == lax.broadcasted_iota(jnp.int32, (rows, HD), 0)
+    row = lax.broadcasted_iota(jnp.int32, (16, HD), 0)
+    for p in range(NP):
+        column = jnp.broadcast_to(squares[p * rows : (p + 1) * rows], (rows, HD))
+        line = jnp.sum(jnp.where(on_diagonal, column, 0.0), axis=0, keepdims=True)
+        high = line.astype(bf16).astype(f32)
+        pair = jnp.where(row == 0, high, jnp.where(row == 1, line - high, 0.0))
+        out_ref[p, body : body + 16, :] = pair.astype(bf16)
+
+
+def down_kernel(activated_ref, *refs):
+    out_ref = refs[-1]
+    parts, chunks, rows, _ = activated_ref.shape
+    feat = refs[0].shape[1]
+    activated = jnp.concatenate(
+        [
+            jnp.concatenate([activated_ref[p, chunk] for chunk in range(chunks)], axis=1)
+            for p in range(parts)
+        ],
+        axis=0,
+    )
+    for k in range(NQ):
+        out_ref[:, k * feat : (k + 1) * feat] = dot(activated, refs[k][...]).astype(bf16)
 
 
 def attend(queries, key_part, value_part, key_pos, ctx_index):
@@ -110,47 +165,45 @@
     width = NQ * feat
     model = NP * width
 
-    def gate_up_block(target):
-        gate = lax.dynamic_slice(gate_up_weight, (0, target * units), (feat, units))
-        up = lax.dynamic_slice(gate_up_weight, (0, (NQ + target) * units), (feat, units))
-        return jnp.concatenate([gate, up], axis=1)
+    def gate_block(target):
+        return lax.dynamic_slice(gate_up_weight, (0, target * units), (feat, units))
+
+    def up_block(target):
+        return lax.dynamic_slice(gate_up_weight, (0, (NQ + target) * units), (feat, units))
 
     def down_block(target):
         return lax.dynamic_slice(down_weight, (target * units, 0), (units, feat))
 
     targets = [jnp.bitwise_xor(q_index, k) for k in range(NQ)]
-    blocks_in = [gate_up_block(target) for target in targets]
-    blocks_out = [down_block(target) for target in targets]
-    moved_in = {0: blocks_in[0]}
-    moved_out = {0: blocks_out[0]}
-
-    def begin(first, into, out):
-        sent = {"in": {k: blocks_in[k] for k in into}, "out": {k: blocks_out[k] for k in out}}
-        first, sent = lax.optimization_barrier((first, sent))
-        moved = jax.tree.map(lambda block: block, sent)
-        for part in moved.values():
-            for k in part:
-                part[k] = from_peer(part[k], "q", NQ, k)
-        return first, moved
-
-    def end(last, moved):
-        last, moved = lax.optimization_barrier((last, moved))
-        moved_in.update(moved["in"])
-        moved_out.update(moved["out"])
+    sent = {
+        name: [block(target) for target in targets]
+        for name, block in (("gate", gate_block), ("up", up_block), ("down", down_block))
+    }
+    moved = {(name, 0): blocks[0] for name, blocks in sent.items()}
+
+    def begin(first, *units_sent):
+        blocks = [sent[name][k] for name, k in units_sent]
+        first, blocks = lax.optimization_barrier((first, blocks))
+        arriving = [from_peer(block, "q", NQ, k) for block, (_, k) in zip(blocks, units_sent)]
+        return first, (units_sent, arriving)
+
+    def end(last, flight):
+        units_sent, arriving = flight
+        last, arriving = lax.optimization_barrier((last, arriving))
+        moved.update(zip(units_sent, arriving))
         return last
 
-    half, rest = tuple(range(2, 2 + (NQ - 2) // 2)), tuple(range(2 + (NQ - 2) // 2, NQ))
     rows = keys_values.shape[0]
-    keys_values, moved = begin(keys_values, (1,), (1,))
-    column = end(gather_column(keys_values, x_index), moved)
-    column, moved = begin(column, half, ())
-    segment = jnp.concatenate(from_peers([column] * NY, "y", NY), axis=0)
-    segment = jnp.concatenate(from_peers([segment] * NC, "core", NC), axis=0)
-    segment = end(segment, moved).reshape(NCTX * rows, 2 * HD)
+    keys_values, flight = begin(
+        keys_values, ("gate", 1), ("up", 1), ("down", 1), ("gate", 2)
+    )
+    column = end(gather_column(keys_values, x_index), flight)
+    column, flight = begin(column, ("up", 2))
+    segment = end(share(column, ("y", "core"), NY * NC), flight).reshape(NCTX * rows, 2 * HD)
     attended = attend(
         queries, segment[:, :HD], segment[:, HD:], key_positions(rows), ctx_index
     )
-    attended, moved = begin(attended, rest, ())
+    attended, flight = begin(attended, ("gate", 3), ("up", 3))
 
     share_rows = attended.shape[0] // (NPLANE * NZ)
     attended = (
@@ -159,7 +212,7 @@
         .reshape(-1, HD)
     )
     partial = dot(attended, out_weight).astype(bf16).reshape(NPLANE, NZ * share_rows, model)
-    partial = end(swap(partial, PLANE), moved)
+    partial = end(swap(partial, PLANE), flight)
     partial = jnp.sum(partial.astype(f32), axis=0).reshape(NZ, share_rows, model)
     own_group = jnp.arange(NZ)[:, None, None] == zh_index
     partial = partial + jnp.where(own_group, residual.astype(f32)[None], 0.0)
@@ -171,6 +224,7 @@
     routing = jnp.where(own_group, routing[None], 0).reshape(1, NZ * share_rows, HD)
     routing = jnp.broadcast_to(routing, (NCTX,) + routing.shape[1:])
     outgoing = jnp.concatenate([outgoing, routing], axis=2)
+    outgoing, flight = begin(outgoing, ("down", 2))
     wide = feat + HD
     outgoing = jnp.broadcast_to(
         outgoing[:, None], (NCTX, NZ, NZ * share_rows, wide)
@@ -187,7 +241,7 @@
         .reshape(3, NZ, token_count, choices)
     )
 
-    hidden = jnp.concatenate(from_peers([hidden] * NQ, "q", NQ), axis=1)
+    hidden = end(jnp.concatenate(from_peers([hidden] * NQ, "q", NQ), axis=1), flight)
     gain = jnp.concatenate(
         [
             lax.dynamic_slice_in_dim(
@@ -225,23 +279,19 @@
     )
 
     buckets = dot(selector, hidden).astype(bf16).reshape(NPLANE, -1, HD)
-    buckets, moved = begin(buckets, (), half + rest)
-    buffer = end(swap(buckets, PLANE), moved).reshape(total_slots, width).astype(f32)
-    squares = jnp.sum(buffer * buffer, axis=1)
-    scaled = (buffer * gain).astype(bf16)
-    gate_up = dot(scaled[:, :feat], moved_in[0])
-    for k in range(1, NQ):
-        gate_up = gate_up + dot(scaled[:, k * feat : (k + 1) * feat], moved_in[k])
+    buckets, flight = begin(buckets, ("down", 3))
+    buffer = end(swap(buckets, PLANE), flight).reshape(total_slots, width)
 
     rows = total_slots // NP
     chunks = 2 * units // HD
-    high, low = split(squares.reshape(NP, rows))
-    pair = jnp.stack([high, low], axis=1)
-    pair = jnp.pad(pair, ((0, 0), (0, 14), (0, HD - rows)))
-    body = (
-        gate_up.astype(bf16).reshape(NP, rows, chunks, HD).transpose(0, 2, 1, 3)
-    ).reshape(NP, chunks * rows, HD)
-    body = jnp.concatenate([body, pair], axis=1)
+    names = [(name, k) for name in ("gate", "up") for k in range(NQ)]
+    body = call(
+        gate_up_kernel,
+        (NP, chunks * rows + 16, HD),
+        buffer,
+        gain[None],
+        *[moved[name] for name in names],
+    )
     parts = [
         lax.dynamic_index_in_dim(body, jnp.bitwise_xor(p_index, k), 0, keepdims=False)
         for k in range(NP)
@@ -251,17 +301,12 @@
     scale = lax.rsqrt(square_sum[:rows] / model + 1e-06)
     pre = summed[: chunks * rows].reshape(2, chunks // 2, rows, HD) * scale[:, None]
     activated = (jax.nn.silu(pre[0]) * pre[1]).astype(bf16)
-    activated = jnp.stack(from_peers([activated] * NP, "p", NP))
-    activated = jnp.stack(
-        [
-            lax.dynamic_index_in_dim(activated, jnp.bitwise_xor(p_index, k), 0, keepdims=False)
-            for k in range(NP)
-        ]
-    )
-    activated = activated.transpose(0, 2, 1, 3).reshape(total_slots, units)
-
-    expert_out = jnp.concatenate(
-        [dot(activated, moved_out[k]).astype(bf16) for k in range(NQ)], axis=1
+    activated = share(activated, "p", NP)
+    expert_out = call(
+        down_kernel,
+        (total_slots, width),
+        activated.reshape(NP, chunks // 2, rows, HD),
+        *[moved["down", k] for k in range(NQ)],
     )
     returned = swap(expert_out.reshape(NPLANE, -1, HD), PLANE).reshape(total_slots, width)
     mixed = dot(combine[0], returned) + dot(combine[1], returned)

time: 372 us -> 358 us (0.962)
  waiting for transfers between devices: 148 us -> 133 us
  local copies, waits for them, and re-layouts: 19.5 us -> 24.2 us
    ppermute x23 -> x19, waiting for transfers between devices: 104 us -> 66.5 us  [from_peer(): return lax.ppermute(block, axis, [(i, i ^ k) for i in range(count)])]
    all_to_all x5 -> x7, starting transfers between devices: 68.7 us -> 103 us  [swap(): return lax.all_to_all(array, axes, split_axis=0, concat_axis=0, tiled=True)]
    ppermute x23 -> x19, starting transfers between devices: 117 us -> 83.2 us  [from_peer(): return lax.ppermute(block, axis, [(i, i ^ k) for i in range(count)])]
    all_to_all x5 -> x7, waiting for transfers between devices: 44.2 us -> 66.7 us  [swap(): return lax.all_to_all(array, axes, split_axis=0, concat_axis=0, tiled=True)]
  transfers between devices with their start and end apart: 28 -> 26, of which waited for: 13 -> 15; matrix products, arithmetic and copies ran while one was open for 3% -> 3% of each run, Pallas kernels for 0% -> 0%
where the time goes in v4:
time: 358 us; the launch traced here: 356 us
  starting transfers between devices  186 us (52%)
  waiting for transfers between devices  133 us (37%)
  local copies, waits for them, and re-layouts  24.2 us (7%)
  other arithmetic  7.31 us (2%)
    all_to_all x7, starting transfers between devices, swap(): return lax.all_to_all(array, axes, split_axis=0, concat_axis=0, tiled=True)  103 us
    ppermute x19, starting transfers between devices, from_peer(): return lax.ppermute(block, axis, [(i, i ^ k) for i in range(count)])  83.2 us
    all_to_all x7, waiting for transfers between devices, swap(): return lax.all_to_all(array, axes, split_axis=0, concat_axis=0, tiled=True)  66.7 us
    ppermute x19, waiting for transfers between devices, from_peer(): return lax.ppermute(block, axis, [(i, i ^ k) for i in range(count)])  66.5 us
  transfers between devices with their start and end apart: 26, of which 15 were waited for; matrix products, arithmetic and copies ran while one was open for 3% of the time, Pallas kernels for 0%

profile of v4, /device:TPU:1, one launch (start us, length us, event | category | flops | bytes accessed | tf_op | source)
XLA Modules:
  0.0 356.1 jit_solution(12638307369278453110)
XLA Ops:
  4.7 26.4 %all-to-all-start = ((bf16[16,16,256]{2,1,0:T(8,128)(2,1)}), bf16[16,16,256]{2,1,0:T(8,128)(2,1)S(1)}, u32[]{:S(2)}, u32[]{:S(2)}) async-start(bf16[16,16,256]{2,1,0:T(8,128)(2,1)} %broadcast_in_dim.124), calls=%async_computation | async-start | bytes 262144 | tf_op jit(solution)/shard_map/all_to_all | solution.py:27
  31.1 3.3 collective-permute-start
  36.4 3.3 collective-permute-start.2
  39.7 4.0 %collective-permute-start.3 = (bf16[256,384]{1,0:T(8,128)(2,1)}, bf16[256,384]{1,0:T(8,128)(2,1)S(1)}, u32[]{:S(2)}, u32[]{:S(2)}) collective-permute-start(bf16[256,384]{1,0:T(8,128)(2,1)} %get-tuple-element.37), channel_id=1, source_target_pairs={{0,128},{64,192},{128,0},{192,64},{1,129},{65,193},{129,1},{193,65... | collective-permute-start | bytes 589832 | tf_op jit(solution)/shard_map/ppermute | solution.py:39
  44.2 9.5 %collective-permute-done.2.refs_1_ = bf16[384,256]{1,0:T(8,128)(2,1)S(1)} collective-permute-done((bf16[384,256]{1,0:T(8,128)(2,1)}, bf16[384,256]{1,0:T(8,128)(2,1)S(1)}, u32[]{:S(2)}, u32[]{:S(2)}) %collective-permute-start.2) | collective-permute-done | bytes 196640 | tf_op jit(solution)/shard_map/ppermute | solution.py:39
  54.8 6.5 %all-to-all-start.1 = ((bf16[8,16,16,256]{3,2,1,0:T(8,128)(2,1)}), bf16[8,16,16,256]{3,2,1,0:T(8,128)(2,1)S(1)}, u32[]{:S(2)}, u32[]{:S(2)}) async-start(bf16[8,16,16,256]{3,2,1,0:T(8,128)(2,1)} %broadcast_in_dim.125), calls=%async_computation.1 | async-start | bytes 2097152 | tf_op jit(solution)/shard_map/all_to_all | solution.py:27
  61.3 4.7 %collective-permute-start.4 = (bf16[256,384]{1,0:T(8,128)(2,1)}, bf16[256,384]{1,0:T(8,128)(2,1)S(1)}, u32[]{:S(2)}, u32[]{:S(2)}) collective-permute-start(bf16[256,384]{1,0:T(8,128)(2,1)} %get-tuple-element.40), channel_id=1, source_target_pairs={{0,128},{64,192},{128,0},{192,64},{1,129},{65,193},{129,1},{193,65... | collective-permute-start | bytes 589832 | tf_op jit(solution)/shard_map/ppermute | solution.py:39
  66.1 5.4 %collective-permute-done.4.refs_6_ = bf16[256,384]{1,0:T(8,128)(2,1)S(1)} collective-permute-done((bf16[256,384]{1,0:T(8,128)(2,1)}, bf16[256,384]{1,0:T(8,128)(2,1)S(1)}, u32[]{:S(2)}, u32[]{:S(2)}) %collective-permute-start.4) | collective-permute-done | bytes 196640 | tf_op jit(solution)/shard_map/ppermute | solution.py:39
  71.5 4.9 %all-to-all-done.1 = bf16[8,16,16,256]{3,2,1,0:T(8,128)(2,1)S(1)} async-done(((bf16[8,16,16,256]{3,2,1,0:T(8,128)(2,1)}), bf16[8,16,16,256]{3,2,1,0:T(8,128)(2,1)S(1)}, u32[]{:S(2)}, u32[]{:S(2)}) %all-to-all-start.1) | async-done | bytes 1048608 | tf_op jit(solution)/shard_map/all_to_all | solution.py:27
  79.7 6.1 %all-to-all-start.2 = ((bf16[32,4,4096]{2,1,0:T(4,128)(2,1)}), bf16[32,4,4096]{2,1,0:T(4,128)(2,1)}, u32[]{:S(2)}, u32[]{:S(2)}) async-start(bf16[32,4,4096]{2,1,0:T(4,128)(2,1)} %reshape.248), calls=%async_computation.2 | async-start | bytes 2097152 | tf_op jit(solution)/shard_map/all_to_all | solution.py:27
  86.3 7.0 %collective-permute-start.5 = (bf16[256,384]{1,0:T(8,128)(2,1)S(1)}, bf16[256,384]{1,0:T(8,128)(2,1)S(1)}, u32[]{:S(2)}, u32[]{:S(2)}) collective-permute-start(bf16[256,384]{1,0:T(8,128)(2,1)S(1)} %copy-done.20), channel_id=1, source_target_pairs={{0,192},{64,128},{128,64},{192,0},{1,193},{65,129},{129,65},{193,1... | collective-permute-start | bytes 589832 | tf_op jit(solution)/shard_map/ppermute | solution.py:39
  95.4 3.1 collective-permute-done.5.refs_3_
  98.5 4.5 %collective-permute-done.6.refs_7_ = bf16[256,384]{1,0:T(8,128)(2,1)S(1)} collective-permute-done((bf16[256,384]{1,0:T(8,128)(2,1)S(1)}, bf16[256,384]{1,0:T(8,128)(2,1)S(1)}, u32[]{:S(2)}, u32[]{:S(2)}) %collective-permute-start.6) | collective-permute-done | bytes 196640 | tf_op jit(solution)/shard_map/ppermute | solution.py:39
  105.5 24.3 %all-to-all-start.3 = ((bf16[32,4,384]{2,1,0:T(4,128)(2,1)}), bf16[32,4,384]{2,1,0:T(4,128)(2,1)S(1)}, u32[]{:S(2)}, u32[]{:S(2)}) async-start(bf16[32,4,384]{2,1,0:T(4,128)(2,1)} %bitcast.15), calls=%async_computation.3 | async-start | bytes 196608 | tf_op jit(solution)/shard_map/all_to_all | solution.py:27
  129.9 4.0 %collective-permute-start.10 = (bf16[384,256]{1,0:T(8,128)(2,1)}, bf16[384,256]{1,0:T(8,128)(2,1)S(1)}, u32[]{:S(2)}, u32[]{:S(2)}) collective-permute-start(bf16[384,256]{1,0:T(8,128)(2,1)} %get-tuple-element.47), channel_id=1, source_target_pairs={{0,128},{64,192},{128,0},{192,64},{1,129},{65,193},{129,1},{193,65... | collective-permute-start | bytes 589832 | tf_op jit(solution)/shard_map/ppermute | solution.py:39
  133.9 22.4 %all-to-all-done.3 = bf16[32,4,384]{2,1,0:T(4,128)(2,1)S(1)} async-done(((bf16[32,4,384]{2,1,0:T(4,128)(2,1)}), bf16[32,4,384]{2,1,0:T(4,128)(2,1)S(1)}, u32[]{:S(2)}, u32[]{:S(2)}) %all-to-all-start.3) | async-done | bytes 98336 | tf_op jit(solution)/shard_map/all_to_all | solution.py:27
  159.4 3.9 %collective-permute-start.8 = (bf16[64,256]{1,0:T(8,128)(2,1)S(1)}, bf16[64,256]{1,0:T(8,128)(2,1)}, u32[]{:S(2)}, u32[]{:S(2)}) collective-permute-start(bf16[64,256]{1,0:T(8,128)(2,1)S(1)} %reshape.251), channel_id=1, source_target_pairs={{0,128},{64,192},{128,0},{192,64},{1,129},{65,193},{129,1},{193,65... | collective-permute-start | bytes 98312 | tf_op jit(solution)/shard_map/ppermute | solution.py:39
  163.3 3.5 collective-permute-start.9
  175.0 10.9 %all-to-all-start.4 = ((bf16[32,80,128]{2,1,0:T(8,128)(2,1)}), bf16[32,80,128]{2,1,0:T(8,128)(2,1)}, u32[]{:S(2)}, u32[]{:S(2)}) async-start(bf16[32,80,128]{2,1,0:T(8,128)(2,1)} %reshape.254), calls=%async_computation.4 | async-start | bytes 1310720 | tf_op jit(solution)/shard_map/all_to_all | solution.py:27
  189.2 6.7 %collective-permute-done.11.refs_3_ = bf16[384,256]{1,0:T(8,128)(2,1)S(1)} collective-permute-done((bf16[384,256]{1,0:T(8,128)(2,1)S(1)}, bf16[384,256]{1,0:T(8,128)(2,1)S(1)}, u32[]{:S(2)}, u32[]{:S(2)}) %collective-permute-start.11) | collective-permute-done | bytes 196640 | tf_op jit(solution)/shard_map/ppermute | solution.py:39
  196.0 2.9 all-to-all-done.4
  206.7 7.2 %collective-permute-start.12 = (bf16[496,128]{1,0:T(8,128)(2,1)S(1)}, bf16[496,128]{1,0:T(8,128)(2,1)S(1)}, u32[]{:S(2)}, u32[]{:S(2)}) collective-permute-start(bf16[496,128]{1,0:T(8,128)(2,1)S(1)} %get-tuple-element.73), channel_id=1, source_target_pairs={{0,256},{256,0},{512,768},{768,512},{1,257},{257,1},{513,769},{769... | collective-permute-start | bytes 380936 | tf_op jit(solution)/shard_map/ppermute | solution.py:39
  215.9 12.0 %collective-permute-start.14 = (bf16[496,128]{1,0:T(8,128)(2,1)S(1)}, bf16[496,128]{1,0:T(8,128)(2,1)S(1)}, u32[]{:S(2)}, u32[]{:S(2)}) collective-permute-start(bf16[496,128]{1,0:T(8,128)(2,1)S(1)} %get-tuple-element.74), channel_id=1, source_target_pairs={{0,768},{256,512},{512,256},{768,0},{1,769},{257,513},{513,257},{7... | collective-permute-start | bytes 380936 | tf_op jit(solution)/shard_map/ppermute | solution.py:39
  228.0 18.3 %collective-permute-done.13 = bf16[496,128]{1,0:T(8,128)(2,1)S(1)} collective-permute-done((bf16[496,128]{1,0:T(8,128)(2,1)S(1)}, bf16[496,128]{1,0:T(8,128)(2,1)S(1)}, u32[]{:S(2)}, u32[]{:S(2)}) %collective-permute-start.13) | collective-permute-done | bytes 127008 | tf_op jit(solution)/shard_map/ppermute | solution.py:39
  246.3 5.3 %collective-permute-done.14 = bf16[496,128]{1,0:T(8,128)(2,1)S(1)} collective-permute-done((bf16[496,128]{1,0:T(8,128)(2,1)S(1)}, bf16[496,128]{1,0:T(8,128)(2,1)S(1)}, u32[]{:S(2)}, u32[]{:S(2)}) %collective-permute-start.14) | collective-permute-done | bytes 127008 | tf_op jit(solution)/shard_map/ppermute | solution.py:39
  252.5 19.3 %all-to-all-start.5 = ((bf16[4,3,80,128]{3,2,1,0:T(8,128)(2,1)}), bf16[4,3,80,128]{3,2,1,0:T(8,128)(2,1)S(1)}, u32[]{:S(2)}, u32[]{:S(2)}) async-start(bf16[4,3,80,128]{3,2,1,0:T(8,128)(2,1)} %broadcast_in_dim.146), calls=%async_computation.5 | async-start | bytes 491520 | tf_op jit(solution)/shard_map/all_to_all | solution.py:27
  272.1 25.2 %all-to-all-done.5.activated_ref = bf16[4,3,80,128]{3,2,1,0:T(8,128)(2,1)S(1)} async-done(((bf16[4,3,80,128]{3,2,1,0:T(8,128)(2,1)}), bf16[4,3,80,128]{3,2,1,0:T(8,128)(2,1)S(1)}, u32[]{:S(2)}, u32[]{:S(2)}) %all-to-all-start.5) | async-done | bytes 245792 | tf_op jit(solution)/shard_map/all_to_all | solution.py:27
  299.0 9.2 %all-to-all-start.6 = ((bf16[32,80,128]{2,1,0:T(8,128)(2,1)}), bf16[32,80,128]{2,1,0:T(8,128)(2,1)S(1)}, u32[]{:S(2)}, u32[]{:S(2)}) async-start(bf16[32,80,128]{2,1,0:T(8,128)(2,1)} %reshape.257), calls=%async_computation.6 | async-start | bytes 1310720 | tf_op jit(solution)/shard_map/all_to_all | solution.py:27
  309.8 11.3 %all-to-all-done.6 = bf16[32,80,128]{2,1,0:T(8,128)(2,1)S(1)} async-done(((bf16[32,80,128]{2,1,0:T(8,128)(2,1)}), bf16[32,80,128]{2,1,0:T(8,128)(2,1)S(1)}, u32[]{:S(2)}, u32[]{:S(2)}) %all-to-all-start.6) | async-done | bytes 655392 | tf_op jit(solution)/shard_map/all_to_all | solution.py:27
  325.9 5.5 %collective-permute-start.17 = (bf16[64,256]{1,0:T(8,128)(2,1)S(1)}, bf16[64,256]{1,0:T(8,128)(2,1)S(1)}, u32[]{:S(2)}, u32[]{:S(2)}) collective-permute-start(bf16[64,256]{1,0:T(8,128)(2,1)S(1)} %get-tuple-element.79), channel_id=1, source_target_pairs={{0,192},{64,128},{128,64},{192,0},{1,193},{65,129},{129,65},{193,1... | collective-permute-start | bytes 98312 | tf_op jit(solution)/shard_map/ppermute | solution.py:39
  332.7 10.9 %collective-permute-start.18 = (bf16[32,256]{1,0:T(8,128)(2,1)S(1)}, bf16[32,256]{1,0:T(8,128)(2,1)S(1)}, u32[]{:S(2)}, u32[]{:S(2)}) collective-permute-start(bf16[32,256]{1,0:T(8,128)(2,1)S(1)} %fusion.33), channel_id=1, source_target_pairs={{0,8},{8,0},{1,9},{9,1},{2,10},{10,2},{3,11},{11,3},{4,12},{12,4},... | collective-permute-start | bytes 49160 | tf_op jit(solution)/shard_map/ppermute | solution.py:39
  343.6 11.9 %collective-permute-done.18 = bf16[32,256]{1,0:T(8,128)(2,1)S(1)} collective-permute-done((bf16[32,256]{1,0:T(8,128)(2,1)S(1)}, bf16[32,256]{1,0:T(8,128)(2,1)S(1)}, u32[]{:S(2)}, u32[]{:S(2)}) %collective-permute-start.18) | collective-permute-done | bytes 16416 | tf_op jit(solution)/shard_map/ppermute | solution.py:39
  (169 shorter events, 51.9 us)
Async XLA Ops:
  0.0 78.0 %copy-start = (bf16[128,4096]{1,0:T(8,128)(2,1)S(1)}, bf16[128,4096]{1,0:T(8,128)(2,1)}, u32[]{:S(2)}) copy-start(bf16[128,4096]{1,0:T(8,128)(2,1)} %param.13) | copy-start | bytes 3145732
  4.7 49.0 %all-to-all-start = ((bf16[16,16,256]{2,1,0:T(8,128)(2,1)}), bf16[16,16,256]{2,1,0:T(8,128)(2,1)S(1)}, u32[]{:S(2)}, u32[]{:S(2)}) async-start(bf16[16,16,256]{2,1,0:T(8,128)(2,1)} %broadcast_in_dim.124), calls=%async_computation | async-start | bytes 262144 | tf_op jit(solution)/shard_map/all_to_all | solution.py:27
  31.1 12.6 %collective-permute-start = (bf16[256,384]{1,0:T(8,128)(2,1)}, bf16[256,384]{1,0:T(8,128)(2,1)S(1)}, u32[]{:S(2)}, u32[]{:S(2)}) collective-permute-start(bf16[256,384]{1,0:T(8,128)(2,1)} %get-tuple-element.34), channel_id=1, source_target_pairs={{0,64},{64,0},{128,192},{192,128},{1,65},{65,1},{129,193},{193,129... | collective-permute-start | bytes 589832 | tf_op jit(solution)/shard_map/ppermute | solution.py:39
  34.4 9.8 %collective-permute-start.1 = (bf16[256,384]{1,0:T(8,128)(2,1)}, bf16[256,384]{1,0:T(8,128)(2,1)S(1)}, u32[]{:S(2)}, u32[]{:S(2)}) collective-permute-start(bf16[256,384]{1,0:T(8,128)(2,1)} %get-tuple-element.35), channel_id=1, source_target_pairs={{0,64},{64,0},{128,192},{192,128},{1,65},{65,1},{129,193},{193,129... | collective-permute-start | bytes 589832 | tf_op jit(solution)/shard_map/ppermute | solution.py:39
  36.4 17.2 %collective-permute-start.2 = (bf16[384,256]{1,0:T(8,128)(2,1)}, bf16[384,256]{1,0:T(8,128)(2,1)S(1)}, u32[]{:S(2)}, u32[]{:S(2)}) collective-permute-start(bf16[384,256]{1,0:T(8,128)(2,1)} %get-tuple-element.36), channel_id=1, source_target_pairs={{0,64},{64,0},{128,192},{192,128},{1,65},{65,1},{129,193},{193,129... | collective-permute-start | bytes 589832 | tf_op jit(solution)/shard_map/ppermute | solution.py:39
  39.7 14.0 %collective-permute-start.3 = (bf16[256,384]{1,0:T(8,128)(2,1)}, bf16[256,384]{1,0:T(8,128)(2,1)S(1)}, u32[]{:S(2)}, u32[]{:S(2)}) collective-permute-start(bf16[256,384]{1,0:T(8,128)(2,1)} %get-tuple-element.37), channel_id=1, source_target_pairs={{0,128},{64,192},{128,0},{192,64},{1,129},{65,193},{129,1},{193,65... | collective-permute-start | bytes 589832 | tf_op jit(solution)/shard_map/ppermute | solution.py:39
  53.7 22.7 %copy-start.27 = (bf16[128,128]{1,0:T(8,128)(2,1)S(1)}, bf16[128,128]{1,0:T(8,128)(2,1)}, u32[]{:S(2)}) copy-start(bf16[128,128]{1,0:T(8,128)(2,1)} %param.9) | copy-start | bytes 98308
  54.8 21.6 %all-to-all-start.1 = ((bf16[8,16,16,256]{3,2,1,0:T(8,128)(2,1)}), bf16[8,16,16,256]{3,2,1,0:T(8,128)(2,1)S(1)}, u32[]{:S(2)}, u32[]{:S(2)}) async-start(bf16[8,16,16,256]{3,2,1,0:T(8,128)(2,1)} %broadcast_in_dim.125), calls=%async_computation.1 | async-start | bytes 2097152 | tf_op jit(solution)/shard_map/all_to_all | solution.py:27
  61.3 10.2 %collective-permute-start.4 = (bf16[256,384]{1,0:T(8,128)(2,1)}, bf16[256,384]{1,0:T(8,128)(2,1)S(1)}, u32[]{:S(2)}, u32[]{:S(2)}) collective-permute-start(bf16[256,384]{1,0:T(8,128)(2,1)} %get-tuple-element.40), channel_id=1, source_target_pairs={{0,128},{64,192},{128,0},{192,64},{1,129},{65,193},{129,1},{193,65... | collective-permute-start | bytes 589832 | tf_op jit(solution)/shard_map/ppermute | solution.py:39
  79.7 23.3 %all-to-all-start.2 = ((bf16[32,4,4096]{2,1,0:T(4,128)(2,1)}), bf16[32,4,4096]{2,1,0:T(4,128)(2,1)}, u32[]{:S(2)}, u32[]{:S(2)}) async-start(bf16[32,4,4096]{2,1,0:T(4,128)(2,1)} %reshape.248), calls=%async_computation.2 | async-start | bytes 2097152 | tf_op jit(solution)/shard_map/all_to_all | solution.py:27
  86.3 12.1 %collective-permute-start.5 = (bf16[256,384]{1,0:T(8,128)(2,1)S(1)}, bf16[256,384]{1,0:T(8,128)(2,1)S(1)}, u32[]{:S(2)}, u32[]{:S(2)}) collective-permute-start(bf16[256,384]{1,0:T(8,128)(2,1)S(1)} %copy-done.20), channel_id=1, source_target_pairs={{0,192},{64,128},{128,64},{192,0},{1,193},{65,129},{129,65},{193,1... | collective-permute-start | bytes 589832 | tf_op jit(solution)/shard_map/ppermute | solution.py:39
  93.3 9.6 %collective-permute-start.6 = (bf16[256,384]{1,0:T(8,128)(2,1)S(1)}, bf16[256,384]{1,0:T(8,128)(2,1)S(1)}, u32[]{:S(2)}, u32[]{:S(2)}) collective-permute-start(bf16[256,384]{1,0:T(8,128)(2,1)S(1)} %copy-done.19), channel_id=1, source_target_pairs={{0,192},{64,128},{128,64},{192,0},{1,193},{65,129},{129,65},{193,1... | collective-permute-start | bytes 589832 | tf_op jit(solution)/shard_map/ppermute | solution.py:39
  98.5 69.6 %copy-start.9 = (bf16[256,384]{1,0:T(8,128)(2,1)}, bf16[256,384]{1,0:T(8,128)(2,1)S(1)}, u32[]{:S(2)}) copy-start(bf16[256,384]{1,0:T(8,128)(2,1)S(1)} %collective-permute-done.5.refs_3_) | copy-start | bytes 589828
  103.0 65.1 %copy-start.11 = (bf16[256,384]{1,0:T(8,128)(2,1)}, bf16[256,384]{1,0:T(8,128)(2,1)S(1)}, u32[]{:S(2)}) copy-start(bf16[256,384]{1,0:T(8,128)(2,1)S(1)} %collective-permute-done.6.refs_7_) | copy-start | bytes 589828
  105.5 50.8 %all-to-all-start.3 = ((bf16[32,4,384]{2,1,0:T(4,128)(2,1)}), bf16[32,4,384]{2,1,0:T(4,128)(2,1)S(1)}, u32[]{:S(2)}, u32[]{:S(2)}) async-start(bf16[32,4,384]{2,1,0:T(4,128)(2,1)} %bitcast.15), calls=%async_computation.3 | async-start | bytes 196608 | tf_op jit(solution)/shard_map/all_to_all | solution.py:27
  129.9 42.8 %collective-permute-start.10 = (bf16[384,256]{1,0:T(8,128)(2,1)}, bf16[384,256]{1,0:T(8,128)(2,1)S(1)}, u32[]{:S(2)}, u32[]{:S(2)}) collective-permute-start(bf16[384,256]{1,0:T(8,128)(2,1)} %get-tuple-element.47), channel_id=1, source_target_pairs={{0,128},{64,192},{128,0},{192,64},{1,129},{65,193},{129,1},{193,65... | collective-permute-start | bytes 589832 | tf_op jit(solution)/shard_map/ppermute | solution.py:39
  157.5 14.3 %copy-start.23 = (bf16[64,256]{1,0:T(8,128)(2,1)}, bf16[64,256]{1,0:T(8,128)(2,1)S(1)}, u32[]{:S(2)}) copy-start(bf16[64,256]{1,0:T(8,128)(2,1)S(1)} %reshape.251) | copy-start | bytes 98308
  157.5 14.3 %collective-permute-start.7 = (bf16[64,256]{1,0:T(8,128)(2,1)S(1)}, bf16[64,256]{1,0:T(8,128)(2,1)}, u32[]{:S(2)}, u32[]{:S(2)}) collective-permute-start(bf16[64,256]{1,0:T(8,128)(2,1)S(1)} %reshape.251), channel_id=1, source_target_pairs={{0,64},{64,0},{128,192},{192,128},{1,65},{65,1},{129,193},{193,129... | collective-permute-start | bytes 98312 | tf_op jit(solution)/shard_map/ppermute | solution.py:39
  159.4 12.4 %collective-permute-start.8 = (bf16[64,256]{1,0:T(8,128)(2,1)S(1)}, bf16[64,256]{1,0:T(8,128)(2,1)}, u32[]{:S(2)}, u32[]{:S(2)}) collective-permute-start(bf16[64,256]{1,0:T(8,128)(2,1)S(1)} %reshape.251), channel_id=1, source_target_pairs={{0,128},{64,192},{128,0},{192,64},{1,129},{65,193},{129,1},{193,65... | collective-permute-start | bytes 98312 | tf_op jit(solution)/shard_map/ppermute | solution.py:39
  163.3 8.5 %collective-permute-start.9 = (bf16[64,256]{1,0:T(8,128)(2,1)S(1)}, bf16[64,256]{1,0:T(8,128)(2,1)}, u32[]{:S(2)}, u32[]{:S(2)}) collective-permute-start(bf16[64,256]{1,0:T(8,128)(2,1)S(1)} %reshape.251), channel_id=1, source_target_pairs={{0,192},{64,128},{128,64},{192,0},{1,193},{65,129},{129,65},{193,1... | collective-permute-start | bytes 98312 | tf_op jit(solution)/shard_map/ppermute | solution.py:39
  175.0 23.9 %all-to-all-start.4 = ((bf16[32,80,128]{2,1,0:T(8,128)(2,1)}), bf16[32,80,128]{2,1,0:T(8,128)(2,1)}, u32[]{:S(2)}, u32[]{:S(2)}) async-start(bf16[32,80,128]{2,1,0:T(8,128)(2,1)} %reshape.254), calls=%async_computation.4 | async-start | bytes 1310720 | tf_op jit(solution)/shard_map/all_to_all | solution.py:27
  185.9 10.0 %collective-permute-start.11 = (bf16[384,256]{1,0:T(8,128)(2,1)S(1)}, bf16[384,256]{1,0:T(8,128)(2,1)S(1)}, u32[]{:S(2)}, u32[]{:S(2)}) collective-permute-start(bf16[384,256]{1,0:T(8,128)(2,1)S(1)} %copy-done.18), channel_id=1, source_target_pairs={{0,192},{64,128},{128,64},{192,0},{1,193},{65,129},{129,65},{193,1... | collective-permute-start | bytes 589832 | tf_op jit(solution)/shard_map/ppermute | solution.py:39
  206.7 65.1 %copy-start.15 = (s32[2,32,32]{2,1,0:T(8,128)S(1)}, s32[2,32,32]{2,1,0:T(8,128)}, u32[]{:S(2)}) copy-start(s32[2,32,32]{2,1,0:T(8,128)} %copy-done.14) | copy-start | bytes 24580
  206.7 21.2 %collective-permute-start.12 = (bf16[496,128]{1,0:T(8,128)(2,1)S(1)}, bf16[496,128]{1,0:T(8,128)(2,1)S(1)}, u32[]{:S(2)}, u32[]{:S(2)}) collective-permute-start(bf16[496,128]{1,0:T(8,128)(2,1)S(1)} %get-tuple-element.73), channel_id=1, source_target_pairs={{0,256},{256,0},{512,768},{768,512},{1,257},{257,1},{513,769},{769... | collective-permute-start | bytes 380936 | tf_op jit(solution)/shard_map/ppermute | solution.py:39
  213.9 32.4 %collective-permute-start.13 = (bf16[496,128]{1,0:T(8,128)(2,1)S(1)}, bf16[496,128]{1,0:T(8,128)(2,1)S(1)}, u32[]{:S(2)}, u32[]{:S(2)}) collective-permute-start(bf16[496,128]{1,0:T(8,128)(2,1)S(1)} %get-tuple-element.75), channel_id=1, source_target_pairs={{0,512},{256,768},{512,0},{768,256},{1,513},{257,769},{513,1},{769... | collective-permute-start | bytes 380936 | tf_op jit(solution)/shard_map/ppermute | solution.py:39
  215.9 35.6 %collective-permute-start.14 = (bf16[496,128]{1,0:T(8,128)(2,1)S(1)}, bf16[496,128]{1,0:T(8,128)(2,1)S(1)}, u32[]{:S(2)}, u32[]{:S(2)}) collective-permute-start(bf16[496,128]{1,0:T(8,128)(2,1)S(1)} %get-tuple-element.74), channel_id=1, source_target_pairs={{0,768},{256,512},{512,256},{768,0},{1,769},{257,513},{513,257},{7... | collective-permute-start | bytes 380936 | tf_op jit(solution)/shard_map/ppermute | solution.py:39
  252.5 44.9 %all-to-all-start.5 = ((bf16[4,3,80,128]{3,2,1,0:T(8,128)(2,1)}), bf16[4,3,80,128]{3,2,1,0:T(8,128)(2,1)S(1)}, u32[]{:S(2)}, u32[]{:S(2)}) async-start(bf16[4,3,80,128]{3,2,1,0:T(8,128)(2,1)} %broadcast_in_dim.146), calls=%async_computation.5 | async-start | bytes 491520 | tf_op jit(solution)/shard_map/all_to_all | solution.py:27
  299.0 22.1 %all-to-all-start.6 = ((bf16[32,80,128]{2,1,0:T(8,128)(2,1)}), bf16[32,80,128]{2,1,0:T(8,128)(2,1)S(1)}, u32[]{:S(2)}, u32[]{:S(2)}) async-start(bf16[32,80,128]{2,1,0:T(8,128)(2,1)} %reshape.257), calls=%async_computation.6 | async-start | bytes 1310720 | tf_op jit(solution)/shard_map/all_to_all | solution.py:27
  322.0 9.4 %collective-permute-start.15 = (bf16[64,256]{1,0:T(8,128)(2,1)S(1)}, bf16[64,256]{1,0:T(8,128)(2,1)S(1)}, u32[]{:S(2)}, u32[]{:S(2)}) collective-permute-start(bf16[64,256]{1,0:T(8,128)(2,1)S(1)} %get-tuple-element.78), channel_id=1, source_target_pairs={{0,64},{64,0},{128,192},{192,128},{1,65},{65,1},{129,193},{193,129... | collective-permute-start | bytes 98312 | tf_op jit(solution)/shard_map/ppermute | solution.py:39
  323.9 7.4 %collective-permute-start.16 = (bf16[64,256]{1,0:T(8,128)(2,1)S(1)}, bf16[64,256]{1,0:T(8,128)(2,1)S(1)}, u32[]{:S(2)}, u32[]{:S(2)}) collective-permute-start(bf16[64,256]{1,0:T(8,128)(2,1)S(1)} %get-tuple-element.80), channel_id=1, source_target_pairs={{0,128},{64,192},{128,0},{192,64},{1,129},{65,193},{129,1},{193,65... | collective-permute-start | bytes 98312 | tf_op jit(solution)/shard_map/ppermute | solution.py:39
  325.9 6.8 %collective-permute-start.17 = (bf16[64,256]{1,0:T(8,128)(2,1)S(1)}, bf16[64,256]{1,0:T(8,128)(2,1)S(1)}, u32[]{:S(2)}, u32[]{:S(2)}) collective-permute-start(bf16[64,256]{1,0:T(8,128)(2,1)S(1)} %get-tuple-element.79), channel_id=1, source_target_pairs={{0,192},{64,128},{128,64},{192,0},{1,193},{65,129},{129,65},{193,1... | collective-permute-start | bytes 98312 | tf_op jit(solution)/shard_map/ppermute | solution.py:39
  332.7 22.8 %collective-permute-start.18 = (bf16[32,256]{1,0:T(8,128)(2,1)S(1)}, bf16[32,256]{1,0:T(8,128)(2,1)S(1)}, u32[]{:S(2)}, u32[]{:S(2)}) collective-permute-start(bf16[32,256]{1,0:T(8,128)(2,1)S(1)} %fusion.33), channel_id=1, source_target_pairs={{0,8},{8,0},{1,9},{9,1},{2,10},{10,2},{3,11},{11,3},{4,12},{12,4},... | collective-permute-start | bytes 49160 | tf_op jit(solution)/shard_map/ppermute | solution.py:39
  (22 other events, 118.6 us)

commit v5 on v4

--- a/solution.py
+++ b/solution.py
@@ -75,25 +75,44 @@
     )
 
 
-def call(kernel, shape, *operands):
+def call(kernel, shape, operands, weights):
     return pl.pallas_call(
         kernel,
         out_shape=jax.ShapeDtypeStruct(shape, bf16),
+        in_specs=[pl.BlockSpec(memory_space=pltpu.VMEM)] * len(operands)
+        + [pl.BlockSpec(memory_space=pl.ANY)] * len(weights),
+        out_specs=pl.BlockSpec(memory_space=pltpu.VMEM),
+        scratch_shapes=[
+            pltpu.VMEM((len(weights),) + weights[0].shape, bf16),
+            pltpu.SemaphoreType.DMA((len(weights),)),
+        ],
         compiler_params=pltpu.CompilerParams(vmem_limit_bytes=32 * 1024 * 1024),
-    )(*operands)
+    )(*operands, *weights)
+
+
+def fetch(weights, held, semaphores):
+    copies = [
+        pltpu.make_async_copy(weight, held.at[i], semaphores.at[i])
+        for i, weight in enumerate(weights)
+    ]
+    for copy in copies:
+        copy.start()
+    return copies
 
 
 def gate_up_kernel(buffer_ref, gain_ref, *refs):
-    out_ref = refs[-1]
-    feat, units = refs[0].shape
+    *weights, out_ref, held, semaphores = refs
+    copies = fetch(weights, held, semaphores)
+    _, feat, units = held.shape
     rows = buffer_ref.shape[0] // NP
     buffer = buffer_ref[...].astype(f32)
     squares = jnp.sum(buffer * buffer, axis=1, keepdims=True)
     scaled = (buffer * gain_ref[...]).astype(bf16)
     for half in range(2):
-        total = dot(scaled[:, :feat], refs[half * NQ][...])
-        for k in range(1, NQ):
-            total = total + dot(scaled[:, k * feat : (k + 1) * feat], refs[half * NQ + k][...])
+        total = jnp.zeros((buffer.shape[0], units), f32)
+        for k in range(NQ):
+            copies[half * NQ + k].wait()
+            total = total + dot(scaled[:, k * feat : (k + 1) * feat], held[half * NQ + k])
         total = total.astype(bf16)
         for p in range(NP):
             for chunk in range(units // HD):
@@ -114,9 +133,10 @@
 
 
 def down_kernel(activated_ref, *refs):
-    out_ref = refs[-1]
+    *weights, out_ref, held, semaphores = refs
+    copies = fetch(weights, held, semaphores)
     parts, chunks, rows, _ = activated_ref.shape
-    feat = refs[0].shape[1]
+    feat = held.shape[2]
     activated = jnp.concatenate(
         [
             jnp.concatenate([activated_ref[p, chunk] for chunk in range(chunks)], axis=1)
@@ -125,7 +145,8 @@
         axis=0,
     )
     for k in range(NQ):
-        out_ref[:, k * feat : (k + 1) * feat] = dot(activated, refs[k][...]).astype(bf16)
+        copies[k].wait()
+        out_ref[:, k * feat : (k + 1) * feat] = dot(activated, held[k]).astype(bf16)
 
 
 def attend(queries, key_part, value_part, key_pos, ctx_index):
@@ -183,7 +204,8 @@
 
     def begin(first, *units_sent):
         blocks = [sent[name][k] for name, k in units_sent]
-        first, blocks = lax.optimization_barrier((first, blocks))
+        if first is not None:
+            first, blocks = lax.optimization_barrier((first, blocks))
         arriving = [from_peer(block, "q", NQ, k) for block, (_, k) in zip(blocks, units_sent)]
         return first, (units_sent, arriving)
 
@@ -194,9 +216,7 @@
         return last
 
     rows = keys_values.shape[0]
-    keys_values, flight = begin(
-        keys_values, ("gate", 1), ("up", 1), ("down", 1), ("gate", 2)
-    )
+    _, flight = begin(None, ("gate", 1), ("up", 1), ("gate", 2))
     column = end(gather_column(keys_values, x_index), flight)
     column, flight = begin(column, ("up", 2))
     segment = end(share(column, ("y", "core"), NY * NC), flight).reshape(NCTX * rows, 2 * HD)
@@ -219,29 +239,22 @@
     outgoing = partial.astype(bf16).reshape(NZ * share_rows, NCTX, feat).transpose(1, 0, 2)
 
     routing = jnp.concatenate([expert_ids.astype(bf16), *split(gate_values)], axis=1)
-    routing = lax.dynamic_slice_in_dim(routing, ctx_index * share_rows, share_rows, 0)
-    routing = jnp.pad(routing, ((0, 0), (0, HD - routing.shape[1])))
-    routing = jnp.where(own_group, routing[None], 0).reshape(1, NZ * share_rows, HD)
-    routing = jnp.broadcast_to(routing, (NCTX,) + routing.shape[1:])
-    outgoing = jnp.concatenate([outgoing, routing], axis=2)
-    outgoing, flight = begin(outgoing, ("down", 2))
-    wide = feat + HD
+    outgoing, routing = lax.optimization_barrier((outgoing, routing))
+    other = from_peer(routing, "zh", NZ, 1)
+    first = zh_index == 0
+    routing = jnp.stack([jnp.where(first, routing, other), jnp.where(first, other, routing)])
+    outgoing, flight = begin(outgoing, ("down", 1), ("down", 2), ("down", 3))
     outgoing = jnp.broadcast_to(
-        outgoing[:, None], (NCTX, NZ, NZ * share_rows, wide)
-    ).reshape(NCTX * NZ, NZ * share_rows, wide)
-    arrived = swap(outgoing, CTX + ("zh",)).reshape(NCTX, NZ, NZ * share_rows, wide)
-    arrived = jnp.sum(arrived.astype(f32), axis=1)
-    hidden = arrived[:, :, :feat].astype(bf16).reshape(-1, feat)
+        outgoing[:, None], (NCTX, NZ, NZ * share_rows, feat)
+    ).reshape(NCTX * NZ, NZ * share_rows, feat)
+    arrived = swap(outgoing, CTX + ("zh",)).reshape(NCTX, NZ, NZ * share_rows, feat)
+    arrived = end(arrived, flight).astype(f32)
+    hidden = jnp.sum(arrived, axis=1).astype(bf16).reshape(-1, feat)
     choices = expert_ids.shape[1]
     token_count = expert_ids.shape[0]
-    routing = (
-        arrived[:, :, feat : feat + 3 * choices]
-        .reshape(NCTX, NZ, share_rows, 3, choices)
-        .transpose(3, 1, 0, 2, 4)
-        .reshape(3, NZ, token_count, choices)
-    )
-
-    hidden = end(jnp.concatenate(from_peers([hidden] * NQ, "q", NQ), axis=1), flight)
+    routing = routing.reshape(NZ, token_count, 3, choices).transpose(2, 0, 1, 3).astype(f32)
+
+    hidden = jnp.concatenate(from_peers([hidden] * NQ, "q", NQ), axis=1)
     gain = jnp.concatenate(
         [
             lax.dynamic_slice_in_dim(
@@ -279,8 +292,7 @@
     )
 
     buckets = dot(selector, hidden).astype(bf16).reshape(NPLANE, -1, HD)
-    buckets, flight = begin(buckets, ("down", 3))
-    buffer = end(swap(buckets, PLANE), flight).reshape(total_slots, width)
+    buffer = swap(buckets, PLANE).reshape(total_slots, width)
 
     rows = total_slots // NP
     chunks = 2 * units // HD
@@ -288,9 +300,8 @@
     body = call(
         gate_up_kernel,
         (NP, chunks * rows + 16, HD),
-        buffer,
-        gain[None],
-        *[moved[name] for name in names],
+        (buffer, gain[None]),
+        [moved[name] for name in names],
     )
     parts = [
         lax.dynamic_index_in_dim(body, jnp.bitwise_xor(p_index, k), 0, keepdims=False)
@@ -305,8 +316,8 @@
     expert_out = call(
         down_kernel,
         (total_slots, width),
-        activated.reshape(NP, chunks // 2, rows, HD),
-        *[moved["down", k] for k in range(NQ)],
+        (activated.reshape(NP, chunks // 2, rows, HD),),
+        [moved["down", k] for k in range(NQ)],
     )
     returned = swap(expert_out.reshape(NPLANE, -1, HD), PLANE).reshape(total_slots, width)
     mixed = dot(combine[0], returned) + dot(combine[1], returned)

time: 358 us -> 361 us (level)
  Pallas kernels: 1.35 us -> 5.85 us
  starting transfers between devices: 186 us -> 182 us
  waiting for transfers between devices: 133 us -> 137 us
    ppermute x19 -> x20, waiting for transfers between devices: 66.5 us -> 85 us  [from_peer(): return lax.ppermute(block, axis, [(i, i ^ k) for i in range(count)])]
    all_to_all x7, waiting for transfers between devices: 66.7 us -> 51.6 us  [swap(): return lax.all_to_all(array, axes, split_axis=0, concat_axis=0, tiled=True)]
    all_to_all x7, starting transfers between devices: 103 us -> 87.8 us  [swap(): return lax.all_to_all(array, axes, split_axis=0, concat_axis=0, tiled=True)]
    ppermute x19 -> x20, starting transfers between devices: 83.2 us -> 94.4 us  [from_peer(): return lax.ppermute(block, axis, [(i, i ^ k) for i in range(count)])]
    pallas_call x2, Pallas kernels: 1.35 us -> 5.85 us  [call(): pl.pallas_call(kernel, out_shape=jax.ShapeDtypeStruct(shape, bf16), in_sp...]
  transfers between devices with their start and end apart: 26 -> 27, of which waited for: 15 -> 17; matrix products, arithmetic and copies ran while one was open for 3% -> 4% of each run, Pallas kernels for 0% -> 0%
where the time goes in v5:
time: 361 us; the launch traced here: 358 us
  starting transfers between devices  182 us (50%)
  waiting for transfers between devices  137 us (38%)
  local copies, waits for them, and re-layouts  23.1 us (6%)
  other arithmetic  7.29 us (2%)
  Pallas kernels  5.85 us (2%)
    ppermute x20, starting transfers between devices, from_peer(): return lax.ppermute(block, axis, [(i, i ^ k) for i in range(count)])  94.4 us
    all_to_all x7, starting transfers between devices, swap(): return lax.all_to_all(array, axes, split_axis=0, concat_axis=0, tiled=True)  87.8 us
    ppermute x20, waiting for transfers between devices, from_peer(): return lax.ppermute(block, axis, [(i, i ^ k) for i in range(count)])  85 us
    all_to_all x7, waiting for transfers between devices, swap(): return lax.all_to_all(array, axes, split_axis=0, concat_axis=0, tiled=True)  51.6 us
  transfers between devices with their start and end apart: 27, of which 17 were waited for; matrix products, arithmetic and copies ran while one was open for 4% of the time, Pallas kernels for 0%

profile of v5, /device:TPU:1, one launch (start us, length us, event | category | flops | bytes accessed | tf_op | source)
XLA Modules:
  0.0 358.4 jit_solution(11508452418180044227)
XLA Ops:
  1.5 26.4 %all-to-all-start = ((bf16[16,16,256]{2,1,0:T(8,128)(2,1)}), bf16[16,16,256]{2,1,0:T(8,128)(2,1)S(1)}, u32[]{:S(2)}, u32[]{:S(2)}) async-start(bf16[16,16,256]{2,1,0:T(8,128)(2,1)} %broadcast_in_dim.94), calls=%async_computation | async-start | bytes 262144 | tf_op jit(solution)/shard_map/all_to_all | solution.py:27
  30.4 3.2 collective-permute-start
  35.7 4.1 %collective-permute-start.2 = (bf16[256,384]{1,0:T(8,128)(2,1)S(1)}, bf16[256,384]{1,0:T(8,128)(2,1)S(1)}, u32[]{:S(2)}, u32[]{:S(2)}) collective-permute-start(bf16[256,384]{1,0:T(8,128)(2,1)S(1)} %get-tuple-element.57), channel_id=1, source_target_pairs={{0,128},{64,192},{128,0},{192,64},{1,129},{65,193},{129,1},{193,65... | collective-permute-start | bytes 589832 | tf_op jit(solution)/shard_map/ppermute | solution.py:39
  39.8 8.1 %collective-permute-done.1.refs_5_ = bf16[256,384]{1,0:T(8,128)(2,1)S(1)} collective-permute-done((bf16[256,384]{1,0:T(8,128)(2,1)S(1)}, bf16[256,384]{1,0:T(8,128)(2,1)S(1)}, u32[]{:S(2)}, u32[]{:S(2)}) %collective-permute-start.1) | collective-permute-done | bytes 196640 | tf_op jit(solution)/shard_map/ppermute | solution.py:39
  50.9 7.1 %all-to-all-start.1 = ((bf16[8,16,16,256]{3,2,1,0:T(8,128)(2,1)}), bf16[8,16,16,256]{3,2,1,0:T(8,128)(2,1)S(1)}, u32[]{:S(2)}, u32[]{:S(2)}) async-start(bf16[8,16,16,256]{3,2,1,0:T(8,128)(2,1)} %broadcast_in_dim.95), calls=%async_computation.1 | async-start | bytes 2097152 | tf_op jit(solution)/shard_map/all_to_all | solution.py:27
  60.5 11.1 %collective-permute-done.3.refs_6_ = bf16[256,384]{1,0:T(8,128)(2,1)S(1)} collective-permute-done((bf16[256,384]{1,0:T(8,128)(2,1)S(1)}, bf16[256,384]{1,0:T(8,128)(2,1)S(1)}, u32[]{:S(2)}, u32[]{:S(2)}) %collective-permute-start.3) | collective-permute-done | bytes 196640 | tf_op jit(solution)/shard_map/ppermute | solution.py:39
  76.5 6.5 %all-to-all-start.2 = ((bf16[32,4,4096]{2,1,0:T(4,128)(2,1)}), bf16[32,4,4096]{2,1,0:T(4,128)(2,1)}, u32[]{:S(2)}, u32[]{:S(2)}) async-start(bf16[32,4,4096]{2,1,0:T(4,128)(2,1)} %reshape.226), calls=%async_computation.2 | async-start | bytes 2097152 | tf_op jit(solution)/shard_map/all_to_all | solution.py:27
  83.3 3.5 collective-permute-start.4
  86.8 3.6 collective-permute-start.5
  93.3 4.3 %collective-permute-done.5.refs_7_ = bf16[256,384]{1,0:T(8,128)(2,1)S(1)} collective-permute-done((bf16[256,384]{1,0:T(8,128)(2,1)S(1)}, bf16[256,384]{1,0:T(8,128)(2,1)S(1)}, u32[]{:S(2)}, u32[]{:S(2)}) %collective-permute-start.5) | collective-permute-done | bytes 196640 | tf_op jit(solution)/shard_map/ppermute | solution.py:39
  101.7 11.6 %collective-permute-start.9 = (bf16[32,24]{0,1:T(8,128)(2,1)S(1)}, bf16[32,24]{0,1:T(8,128)(2,1)S(1)}, u32[]{:S(2)}, u32[]{:S(2)}) collective-permute-start(bf16[32,24]{0,1:T(8,128)(2,1)S(1)} %pad_maximum_fusion.1), channel_id=1, source_target_pairs={{0,8},{8,0},{1,9},{9,1},{2,10},{10,2},{3,11},{11,3},{4,12},{12,4},... | collective-permute-start | bytes 4616 | tf_op jit(solution)/shard_map/ppermute | solution.py:39
  113.9 20.7 %all-to-all-start.3 = ((bf16[32,4,256]{2,1,0:T(4,128)(2,1)}), bf16[32,4,256]{2,1,0:T(4,128)(2,1)S(1)}, u32[]{:S(2)}, u32[]{:S(2)}) async-start(bf16[32,4,256]{2,1,0:T(4,128)(2,1)} %bitcast.15), calls=%async_computation.3 | async-start | bytes 131072 | tf_op jit(solution)/shard_map/all_to_all | solution.py:27
  134.6 3.1 collective-permute-start.6
  137.8 4.0 %collective-permute-start.7 = (bf16[384,256]{1,0:T(8,128)(2,1)S(1)}, bf16[384,256]{1,0:T(8,128)(2,1)S(1)}, u32[]{:S(2)}, u32[]{:S(2)}) collective-permute-start(bf16[384,256]{1,0:T(8,128)(2,1)S(1)} %copy-done.17), channel_id=1, source_target_pairs={{0,128},{64,192},{128,0},{192,64},{1,129},{65,193},{129,1},{193,65... | collective-permute-start | bytes 589832 | tf_op jit(solution)/shard_map/ppermute | solution.py:39
  145.0 3.7 %collective-permute-done.6.refs_1_ = bf16[384,256]{1,0:T(8,128)(2,1)S(1)} collective-permute-done((bf16[384,256]{1,0:T(8,128)(2,1)}, bf16[384,256]{1,0:T(8,128)(2,1)S(1)}, u32[]{:S(2)}, u32[]{:S(2)}) %collective-permute-start.6) | collective-permute-done | bytes 196640 | tf_op jit(solution)/shard_map/ppermute | solution.py:39
  149.6 7.9 %collective-permute-done.8.refs_3_ = bf16[384,256]{1,0:T(8,128)(2,1)S(1)} collective-permute-done((bf16[384,256]{1,0:T(8,128)(2,1)S(1)}, bf16[384,256]{1,0:T(8,128)(2,1)S(1)}, u32[]{:S(2)}, u32[]{:S(2)}) %collective-permute-start.8) | collective-permute-done | bytes 196640 | tf_op jit(solution)/shard_map/ppermute | solution.py:39
  157.6 2.9 collective-permute-start.12
  160.5 7.0 %collective-permute-start.11 = (bf16[64,256]{1,0:T(8,128)(2,1)S(1)}, bf16[64,256]{1,0:T(8,128)(2,1)S(1)}, u32[]{:S(2)}, u32[]{:S(2)}) collective-permute-start(bf16[64,256]{1,0:T(8,128)(2,1)S(1)} %reshape.230), channel_id=1, source_target_pairs={{0,128},{64,192},{128,0},{192,64},{1,129},{65,193},{129,1},{193,65... | collective-permute-start | bytes 98312 | tf_op jit(solution)/shard_map/ppermute | solution.py:39
  176.2 9.5 %all-to-all-start.4 = ((bf16[32,80,128]{2,1,0:T(8,128)(2,1)}), bf16[32,80,128]{2,1,0:T(8,128)(2,1)}, u32[]{:S(2)}, u32[]{:S(2)}) async-start(bf16[32,80,128]{2,1,0:T(8,128)(2,1)} %reshape.231), calls=%async_computation.4 | async-start | bytes 1310720 | tf_op jit(solution)/shard_map/all_to_all | solution.py:27
  186.7 12.0 %all-to-all-done.4 = bf16[32,80,128]{2,1,0:T(8,128)(2,1)} async-done(((bf16[32,80,128]{2,1,0:T(8,128)(2,1)}), bf16[32,80,128]{2,1,0:T(8,128)(2,1)}, u32[]{:S(2)}, u32[]{:S(2)}) %all-to-all-start.4) | async-done | bytes 655392 | tf_op jit(solution)/shard_map/all_to_all | solution.py:27
  205.6 3.5 shard_map.91
  209.2 15.9 %collective-permute-start.15 = (bf16[496,128]{1,0:T(8,128)(2,1)S(1)}, bf16[496,128]{1,0:T(8,128)(2,1)S(1)}, u32[]{:S(2)}, u32[]{:S(2)}) collective-permute-start(bf16[496,128]{1,0:T(8,128)(2,1)S(1)} %get-tuple-element.66), channel_id=1, source_target_pairs={{0,768},{256,512},{512,256},{768,0},{1,769},{257,513},{513,257},{7... | collective-permute-start | bytes 380936 | tf_op jit(solution)/shard_map/ppermute | solution.py:39
  227.0 3.2 collective-permute-start.13
  230.3 16.0 %collective-permute-done.15 = bf16[496,128]{1,0:T(8,128)(2,1)S(1)} collective-permute-done((bf16[496,128]{1,0:T(8,128)(2,1)S(1)}, bf16[496,128]{1,0:T(8,128)(2,1)S(1)}, u32[]{:S(2)}, u32[]{:S(2)}) %collective-permute-start.15) | collective-permute-done | bytes 127008 | tf_op jit(solution)/shard_map/ppermute | solution.py:39
  246.3 19.6 %collective-permute-done.14 = bf16[496,128]{1,0:T(8,128)(2,1)S(1)} collective-permute-done((bf16[496,128]{1,0:T(8,128)(2,1)S(1)}, bf16[496,128]{1,0:T(8,128)(2,1)S(1)}, u32[]{:S(2)}, u32[]{:S(2)}) %collective-permute-start.14) | collective-permute-done | bytes 127008 | tf_op jit(solution)/shard_map/ppermute | solution.py:39
  266.8 10.2 %all-to-all-start.5 = ((bf16[4,3,80,128]{3,2,1,0:T(8,128)(2,1)}), bf16[4,3,80,128]{3,2,1,0:T(8,128)(2,1)S(1)}, u32[]{:S(2)}, u32[]{:S(2)}) async-start(bf16[4,3,80,128]{3,2,1,0:T(8,128)(2,1)} %broadcast_in_dim.110), calls=%async_computation.5 | async-start | bytes 491520 | tf_op jit(solution)/shard_map/all_to_all | solution.py:27
  278.4 21.3 %all-to-all-done.5.activated_ref = bf16[4,3,80,128]{3,2,1,0:T(8,128)(2,1)S(1)} async-done(((bf16[4,3,80,128]{3,2,1,0:T(8,128)(2,1)}), bf16[4,3,80,128]{3,2,1,0:T(8,128)(2,1)S(1)}, u32[]{:S(2)}, u32[]{:S(2)}) %all-to-all-start.5) | async-done | bytes 245792 | tf_op jit(solution)/shard_map/all_to_all | solution.py:27
  303.1 7.4 %all-to-all-start.6 = ((bf16[32,80,128]{2,1,0:T(8,128)(2,1)}), bf16[32,80,128]{2,1,0:T(8,128)(2,1)S(1)}, u32[]{:S(2)}, u32[]{:S(2)}) async-start(bf16[32,80,128]{2,1,0:T(8,128)(2,1)} %reshape.234), calls=%async_computation.6 | async-start | bytes 1310720 | tf_op jit(solution)/shard_map/all_to_all | solution.py:27
  311.0 12.4 %all-to-all-done.6 = bf16[32,80,128]{2,1,0:T(8,128)(2,1)S(1)} async-done(((bf16[32,80,128]{2,1,0:T(8,128)(2,1)}), bf16[32,80,128]{2,1,0:T(8,128)(2,1)S(1)}, u32[]{:S(2)}, u32[]{:S(2)}) %all-to-all-start.6) | async-done | bytes 655392 | tf_op jit(solution)/shard_map/all_to_all | solution.py:27
  328.1 5.5 %collective-permute-start.16 = (bf16[64,256]{1,0:T(8,128)(2,1)S(1)}, bf16[64,256]{1,0:T(8,128)(2,1)S(1)}, u32[]{:S(2)}, u32[]{:S(2)}) collective-permute-start(bf16[64,256]{1,0:T(8,128)(2,1)S(1)} %get-tuple-element.70), channel_id=1, source_target_pairs={{0,64},{64,0},{128,192},{192,128},{1,65},{65,1},{129,193},{193,129... | collective-permute-start | bytes 98312 | tf_op jit(solution)/shard_map/ppermute | solution.py:39
  334.9 12.6 %collective-permute-start.19 = (bf16[32,256]{1,0:T(8,128)(2,1)S(1)}, bf16[32,256]{1,0:T(8,128)(2,1)S(1)}, u32[]{:S(2)}, u32[]{:S(2)}) collective-permute-start(bf16[32,256]{1,0:T(8,128)(2,1)S(1)} %fusion.40), channel_id=1, source_target_pairs={{0,8},{8,0},{1,9},{9,1},{2,10},{10,2},{3,11},{11,3},{4,12},{12,4},... | collective-permute-start | bytes 49160 | tf_op jit(solution)/shard_map/ppermute | solution.py:39
  347.6 10.1 %collective-permute-done.19 = bf16[32,256]{1,0:T(8,128)(2,1)S(1)} collective-permute-done((bf16[32,256]{1,0:T(8,128)(2,1)S(1)}, bf16[32,256]{1,0:T(8,128)(2,1)S(1)}, u32[]{:S(2)}, u32[]{:S(2)}) %collective-permute-start.19) | collective-permute-done | bytes 16416 | tf_op jit(solution)/shard_map/ppermute | solution.py:39
  (149 shorter events, 59.6 us)
Async XLA Ops:
  0.0 74.8 %copy-start = (bf16[128,4096]{1,0:T(8,128)(2,1)S(1)}, bf16[128,4096]{1,0:T(8,128)(2,1)}, u32[]{:S(2)}) copy-start(bf16[128,4096]{1,0:T(8,128)(2,1)} %param.13) | copy-start | bytes 3145732
  1.5 48.4 %all-to-all-start = ((bf16[16,16,256]{2,1,0:T(8,128)(2,1)}), bf16[16,16,256]{2,1,0:T(8,128)(2,1)S(1)}, u32[]{:S(2)}, u32[]{:S(2)}) async-start(bf16[16,16,256]{2,1,0:T(8,128)(2,1)} %broadcast_in_dim.94), calls=%async_computation | async-start | bytes 262144 | tf_op jit(solution)/shard_map/all_to_all | solution.py:27
  30.4 9.4 %collective-permute-start = (bf16[256,384]{1,0:T(8,128)(2,1)S(1)}, bf16[256,384]{1,0:T(8,128)(2,1)S(1)}, u32[]{:S(2)}, u32[]{:S(2)}) collective-permute-start(bf16[256,384]{1,0:T(8,128)(2,1)S(1)} %get-tuple-element.59), channel_id=1, source_target_pairs={{0,64},{64,0},{128,192},{192,128},{1,65},{65,1},{129,193},{193,129... | collective-permute-start | bytes 589832 | tf_op jit(solution)/shard_map/ppermute | solution.py:39
  33.6 14.3 %collective-permute-start.1 = (bf16[256,384]{1,0:T(8,128)(2,1)S(1)}, bf16[256,384]{1,0:T(8,128)(2,1)S(1)}, u32[]{:S(2)}, u32[]{:S(2)}) collective-permute-start(bf16[256,384]{1,0:T(8,128)(2,1)S(1)} %get-tuple-element.58), channel_id=1, source_target_pairs={{0,64},{64,0},{128,192},{192,128},{1,65},{65,1},{129,193},{193,129... | collective-permute-start | bytes 589832 | tf_op jit(solution)/shard_map/ppermute | solution.py:39
  35.7 12.2 %collective-permute-start.2 = (bf16[256,384]{1,0:T(8,128)(2,1)S(1)}, bf16[256,384]{1,0:T(8,128)(2,1)S(1)}, u32[]{:S(2)}, u32[]{:S(2)}) collective-permute-start(bf16[256,384]{1,0:T(8,128)(2,1)S(1)} %get-tuple-element.57), channel_id=1, source_target_pairs={{0,128},{64,192},{128,0},{192,64},{1,129},{65,193},{129,1},{193,65... | collective-permute-start | bytes 589832 | tf_op jit(solution)/shard_map/ppermute | solution.py:39
  50.9 22.2 %all-to-all-start.1 = ((bf16[8,16,16,256]{3,2,1,0:T(8,128)(2,1)}), bf16[8,16,16,256]{3,2,1,0:T(8,128)(2,1)S(1)}, u32[]{:S(2)}, u32[]{:S(2)}) async-start(bf16[8,16,16,256]{3,2,1,0:T(8,128)(2,1)} %broadcast_in_dim.95), calls=%async_computation.1 | async-start | bytes 2097152 | tf_op jit(solution)/shard_map/all_to_all | solution.py:27
  58.1 13.5 %collective-permute-start.3 = (bf16[256,384]{1,0:T(8,128)(2,1)S(1)}, bf16[256,384]{1,0:T(8,128)(2,1)S(1)}, u32[]{:S(2)}, u32[]{:S(2)}) collective-permute-start(bf16[256,384]{1,0:T(8,128)(2,1)S(1)} %get-tuple-element.31), channel_id=1, source_target_pairs={{0,128},{64,192},{128,0},{192,64},{1,129},{65,193},{129,1},{193,65... | collective-permute-start | bytes 589832 | tf_op jit(solution)/shard_map/ppermute | solution.py:39
  76.5 23.5 %all-to-all-start.2 = ((bf16[32,4,4096]{2,1,0:T(4,128)(2,1)}), bf16[32,4,4096]{2,1,0:T(4,128)(2,1)}, u32[]{:S(2)}, u32[]{:S(2)}) async-start(bf16[32,4,4096]{2,1,0:T(4,128)(2,1)} %reshape.226), calls=%async_computation.2 | async-start | bytes 2097152 | tf_op jit(solution)/shard_map/all_to_all | solution.py:27
  83.3 10.0 %collective-permute-start.4 = (bf16[256,384]{1,0:T(8,128)(2,1)S(1)}, bf16[256,384]{1,0:T(8,128)(2,1)S(1)}, u32[]{:S(2)}, u32[]{:S(2)}) collective-permute-start(bf16[256,384]{1,0:T(8,128)(2,1)S(1)} %copy-done.15), channel_id=1, source_target_pairs={{0,192},{64,128},{128,64},{192,0},{1,193},{65,129},{129,65},{193,1... | collective-permute-start | bytes 589832 | tf_op jit(solution)/shard_map/ppermute | solution.py:39
  86.8 10.8 %collective-permute-start.5 = (bf16[256,384]{1,0:T(8,128)(2,1)S(1)}, bf16[256,384]{1,0:T(8,128)(2,1)S(1)}, u32[]{:S(2)}, u32[]{:S(2)}) collective-permute-start(bf16[256,384]{1,0:T(8,128)(2,1)S(1)} %copy-done.14), channel_id=1, source_target_pairs={{0,192},{64,128},{128,64},{192,0},{1,193},{65,129},{129,65},{193,1... | collective-permute-start | bytes 589832 | tf_op jit(solution)/shard_map/ppermute | solution.py:39
  91.3 46.5 %copy-start.17 = (bf16[384,256]{1,0:T(8,128)(2,1)S(1)}, bf16[384,256]{1,0:T(8,128)(2,1)}, u32[]{:S(2)}) copy-start(bf16[384,256]{1,0:T(8,128)(2,1)} %get-tuple-element.40) | copy-start | bytes 589828
  91.3 50.5 %copy-start.16 = (bf16[384,256]{1,0:T(8,128)(2,1)S(1)}, bf16[384,256]{1,0:T(8,128)(2,1)}, u32[]{:S(2)}) copy-start(bf16[384,256]{1,0:T(8,128)(2,1)} %get-tuple-element.41) | copy-start | bytes 589828
  93.3 78.7 %copy-start.9 = (bf16[256,384]{1,0:T(8,128)(2,1)}, bf16[256,384]{1,0:T(8,128)(2,1)S(1)}, u32[]{:S(2)}) copy-start(bf16[256,384]{1,0:T(8,128)(2,1)S(1)} %collective-permute-done.4.refs_3_) | copy-start | bytes 589828
  97.6 74.4 %copy-start.11 = (bf16[256,384]{1,0:T(8,128)(2,1)}, bf16[256,384]{1,0:T(8,128)(2,1)S(1)}, u32[]{:S(2)}) copy-start(bf16[256,384]{1,0:T(8,128)(2,1)S(1)} %collective-permute-done.5.refs_7_) | copy-start | bytes 589828
  101.7 42.3 %collective-permute-start.9 = (bf16[32,24]{0,1:T(8,128)(2,1)S(1)}, bf16[32,24]{0,1:T(8,128)(2,1)S(1)}, u32[]{:S(2)}, u32[]{:S(2)}) collective-permute-start(bf16[32,24]{0,1:T(8,128)(2,1)S(1)} %pad_maximum_fusion.1), channel_id=1, source_target_pairs={{0,8},{8,0},{1,9},{9,1},{2,10},{10,2},{3,11},{11,3},{4,12},{12,4},... | collective-permute-start | bytes 4616 | tf_op jit(solution)/shard_map/ppermute | solution.py:39
  113.9 43.6 %all-to-all-start.3 = ((bf16[32,4,256]{2,1,0:T(4,128)(2,1)}), bf16[32,4,256]{2,1,0:T(4,128)(2,1)S(1)}, u32[]{:S(2)}, u32[]{:S(2)}) async-start(bf16[32,4,256]{2,1,0:T(4,128)(2,1)} %bitcast.15), calls=%async_computation.3 | async-start | bytes 131072 | tf_op jit(solution)/shard_map/all_to_all | solution.py:27
  134.6 14.1 %collective-permute-start.6 = (bf16[384,256]{1,0:T(8,128)(2,1)}, bf16[384,256]{1,0:T(8,128)(2,1)S(1)}, u32[]{:S(2)}, u32[]{:S(2)}) collective-permute-start(bf16[384,256]{1,0:T(8,128)(2,1)} %get-tuple-element.39), channel_id=1, source_target_pairs={{0,64},{64,0},{128,192},{192,128},{1,65},{65,1},{129,193},{193,129... | collective-permute-start | bytes 589832 | tf_op jit(solution)/shard_map/ppermute | solution.py:39
  137.8 11.8 %collective-permute-start.7 = (bf16[384,256]{1,0:T(8,128)(2,1)S(1)}, bf16[384,256]{1,0:T(8,128)(2,1)S(1)}, u32[]{:S(2)}, u32[]{:S(2)}) collective-permute-start(bf16[384,256]{1,0:T(8,128)(2,1)S(1)} %copy-done.17), channel_id=1, source_target_pairs={{0,128},{64,192},{128,0},{192,64},{1,129},{65,193},{129,1},{193,65... | collective-permute-start | bytes 589832 | tf_op jit(solution)/shard_map/ppermute | solution.py:39
  141.8 15.7 %collective-permute-start.8 = (bf16[384,256]{1,0:T(8,128)(2,1)S(1)}, bf16[384,256]{1,0:T(8,128)(2,1)S(1)}, u32[]{:S(2)}, u32[]{:S(2)}) collective-permute-start(bf16[384,256]{1,0:T(8,128)(2,1)S(1)} %copy-done.16), channel_id=1, source_target_pairs={{0,192},{64,128},{128,64},{192,0},{1,193},{65,129},{129,65},{193,1... | collective-permute-start | bytes 589832 | tf_op jit(solution)/shard_map/ppermute | solution.py:39
  157.6 17.0 %collective-permute-start.12 = (bf16[64,256]{1,0:T(8,128)(2,1)S(1)}, bf16[64,256]{1,0:T(8,128)(2,1)S(1)}, u32[]{:S(2)}, u32[]{:S(2)}) collective-permute-start(bf16[64,256]{1,0:T(8,128)(2,1)S(1)} %reshape.230), channel_id=1, source_target_pairs={{0,192},{64,128},{128,64},{192,0},{1,193},{65,129},{129,65},{193,1... | collective-permute-start | bytes 98312 | tf_op jit(solution)/shard_map/ppermute | solution.py:39
  160.5 14.1 %collective-permute-start.11 = (bf16[64,256]{1,0:T(8,128)(2,1)S(1)}, bf16[64,256]{1,0:T(8,128)(2,1)S(1)}, u32[]{:S(2)}, u32[]{:S(2)}) collective-permute-start(bf16[64,256]{1,0:T(8,128)(2,1)S(1)} %reshape.230), channel_id=1, source_target_pairs={{0,128},{64,192},{128,0},{192,64},{1,129},{65,193},{129,1},{193,65... | collective-permute-start | bytes 98312 | tf_op jit(solution)/shard_map/ppermute | solution.py:39
  167.5 7.1 %collective-permute-start.10 = (bf16[64,256]{1,0:T(8,128)(2,1)S(1)}, bf16[64,256]{1,0:T(8,128)(2,1)S(1)}, u32[]{:S(2)}, u32[]{:S(2)}) collective-permute-start(bf16[64,256]{1,0:T(8,128)(2,1)S(1)} %reshape.230), channel_id=1, source_target_pairs={{0,64},{64,0},{128,192},{192,128},{1,65},{65,1},{129,193},{193,129... | collective-permute-start | bytes 98312 | tf_op jit(solution)/shard_map/ppermute | solution.py:39
  176.2 22.5 %all-to-all-start.4 = ((bf16[32,80,128]{2,1,0:T(8,128)(2,1)}), bf16[32,80,128]{2,1,0:T(8,128)(2,1)}, u32[]{:S(2)}, u32[]{:S(2)}) async-start(bf16[32,80,128]{2,1,0:T(8,128)(2,1)} %reshape.231), calls=%async_computation.4 | async-start | bytes 1310720 | tf_op jit(solution)/shard_map/all_to_all | solution.py:27
  209.2 37.1 %collective-permute-start.15 = (bf16[496,128]{1,0:T(8,128)(2,1)S(1)}, bf16[496,128]{1,0:T(8,128)(2,1)S(1)}, u32[]{:S(2)}, u32[]{:S(2)}) collective-permute-start(bf16[496,128]{1,0:T(8,128)(2,1)S(1)} %get-tuple-element.66), channel_id=1, source_target_pairs={{0,768},{256,512},{512,256},{768,0},{1,769},{257,513},{513,257},{7... | collective-permute-start | bytes 380936 | tf_op jit(solution)/shard_map/ppermute | solution.py:39
  225.1 40.8 %collective-permute-start.14 = (bf16[496,128]{1,0:T(8,128)(2,1)S(1)}, bf16[496,128]{1,0:T(8,128)(2,1)S(1)}, u32[]{:S(2)}, u32[]{:S(2)}) collective-permute-start(bf16[496,128]{1,0:T(8,128)(2,1)S(1)} %get-tuple-element.67), channel_id=1, source_target_pairs={{0,512},{256,768},{512,0},{768,256},{1,513},{257,769},{513,1},{769... | collective-permute-start | bytes 380936 | tf_op jit(solution)/shard_map/ppermute | solution.py:39
  227.0 38.8 %collective-permute-start.13 = (bf16[496,128]{1,0:T(8,128)(2,1)S(1)}, bf16[496,128]{1,0:T(8,128)(2,1)S(1)}, u32[]{:S(2)}, u32[]{:S(2)}) collective-permute-start(bf16[496,128]{1,0:T(8,128)(2,1)S(1)} %get-tuple-element.65), channel_id=1, source_target_pairs={{0,256},{256,0},{512,768},{768,512},{1,257},{257,1},{513,769},{769... | collective-permute-start | bytes 380936 | tf_op jit(solution)/shard_map/ppermute | solution.py:39
  266.8 32.8 %all-to-all-start.5 = ((bf16[4,3,80,128]{3,2,1,0:T(8,128)(2,1)}), bf16[4,3,80,128]{3,2,1,0:T(8,128)(2,1)S(1)}, u32[]{:S(2)}, u32[]{:S(2)}) async-start(bf16[4,3,80,128]{3,2,1,0:T(8,128)(2,1)} %broadcast_in_dim.110), calls=%async_computation.5 | async-start | bytes 491520 | tf_op jit(solution)/shard_map/all_to_all | solution.py:27
  303.1 20.3 %all-to-all-start.6 = ((bf16[32,80,128]{2,1,0:T(8,128)(2,1)}), bf16[32,80,128]{2,1,0:T(8,128)(2,1)S(1)}, u32[]{:S(2)}, u32[]{:S(2)}) async-start(bf16[32,80,128]{2,1,0:T(8,128)(2,1)} %reshape.234), calls=%async_computation.6 | async-start | bytes 1310720 | tf_op jit(solution)/shard_map/all_to_all | solution.py:27
  324.2 9.3 %collective-permute-start.18 = (bf16[64,256]{1,0:T(8,128)(2,1)S(1)}, bf16[64,256]{1,0:T(8,128)(2,1)S(1)}, u32[]{:S(2)}, u32[]{:S(2)}) collective-permute-start(bf16[64,256]{1,0:T(8,128)(2,1)S(1)} %get-tuple-element.71), channel_id=1, source_target_pairs={{0,192},{64,128},{128,64},{192,0},{1,193},{65,129},{129,65},{193,1... | collective-permute-start | bytes 98312 | tf_op jit(solution)/shard_map/ppermute | solution.py:39
  326.2 7.4 %collective-permute-start.17 = (bf16[64,256]{1,0:T(8,128)(2,1)S(1)}, bf16[64,256]{1,0:T(8,128)(2,1)S(1)}, u32[]{:S(2)}, u32[]{:S(2)}) collective-permute-start(bf16[64,256]{1,0:T(8,128)(2,1)S(1)} %get-tuple-element.72), channel_id=1, source_target_pairs={{0,128},{64,192},{128,0},{192,64},{1,129},{65,193},{129,1},{193,65... | collective-permute-start | bytes 98312 | tf_op jit(solution)/shard_map/ppermute | solution.py:39
  328.1 6.8 %collective-permute-start.16 = (bf16[64,256]{1,0:T(8,128)(2,1)S(1)}, bf16[64,256]{1,0:T(8,128)(2,1)S(1)}, u32[]{:S(2)}, u32[]{:S(2)}) collective-permute-start(bf16[64,256]{1,0:T(8,128)(2,1)S(1)} %get-tuple-element.70), channel_id=1, source_target_pairs={{0,64},{64,0},{128,192},{192,128},{1,65},{65,1},{129,193},{193,129... | collective-permute-start | bytes 98312 | tf_op jit(solution)/shard_map/ppermute | solution.py:39
  334.9 22.9 %collective-permute-start.19 = (bf16[32,256]{1,0:T(8,128)(2,1)S(1)}, bf16[32,256]{1,0:T(8,128)(2,1)S(1)}, u32[]{:S(2)}, u32[]{:S(2)}) collective-permute-start(bf16[32,256]{1,0:T(8,128)(2,1)S(1)} %fusion.40), channel_id=1, source_target_pairs={{0,8},{8,0},{1,9},{9,1},{2,10},{10,2},{3,11},{11,3},{4,12},{12,4},... | collective-permute-start | bytes 49160 | tf_op jit(solution)/shard_map/ppermute | solution.py:39
  (17 other events, 100.6 us)

commit v6 on v5

--- a/solution.py
+++ b/solution.py
@@ -80,7 +80,7 @@
         kernel,
         out_shape=jax.ShapeDtypeStruct(shape, bf16),
         in_specs=[pl.BlockSpec(memory_space=pltpu.VMEM)] * len(operands)
-        + [pl.BlockSpec(memory_space=pl.ANY)] * len(weights),
+        + [pl.BlockSpec(memory_space=pltpu.HBM)] * len(weights),
         out_specs=pl.BlockSpec(memory_space=pltpu.VMEM),
         scratch_shapes=[
             pltpu.VMEM((len(weights),) + weights[0].shape, bf16),
@@ -241,18 +241,18 @@
     routing = jnp.concatenate([expert_ids.astype(bf16), *split(gate_values)], axis=1)
     outgoing, routing = lax.optimization_barrier((outgoing, routing))
     other = from_peer(routing, "zh", NZ, 1)
-    first = zh_index == 0
-    routing = jnp.stack([jnp.where(first, routing, other), jnp.where(first, other, routing)])
     outgoing, flight = begin(outgoing, ("down", 1), ("down", 2), ("down", 3))
     outgoing = jnp.broadcast_to(
         outgoing[:, None], (NCTX, NZ, NZ * share_rows, feat)
     ).reshape(NCTX * NZ, NZ * share_rows, feat)
     arrived = swap(outgoing, CTX + ("zh",)).reshape(NCTX, NZ, NZ * share_rows, feat)
-    arrived = end(arrived, flight).astype(f32)
-    hidden = jnp.sum(arrived, axis=1).astype(bf16).reshape(-1, feat)
+    arrived, other = lax.optimization_barrier((end(arrived, flight), other))
+    hidden = jnp.sum(arrived.astype(f32), axis=1).astype(bf16).reshape(-1, feat)
     choices = expert_ids.shape[1]
     token_count = expert_ids.shape[0]
-    routing = routing.reshape(NZ, token_count, 3, choices).transpose(2, 0, 1, 3).astype(f32)
+    first = zh_index == 0
+    routing = jnp.stack([jnp.where(first, routing, other), jnp.where(first, other, routing)])
+    routing = routing.astype(f32)
 
     hidden = jnp.concatenate(from_peers([hidden] * NQ, "q", NQ), axis=1)
     gain = jnp.concatenate(
@@ -264,32 +264,43 @@
         ]
     )
 
-    ids = routing[0].astype(jnp.int32)
     number = jnp.arange(NPLANE, dtype=jnp.int32)
     experts = (number // (NY * NC) * NZ + zh_index) * (NY * NC) + number % (NY * NC)
-    picked = ids[..., None] == experts
-    chosen = jnp.sum(picked.astype(jnp.int32), axis=2)
-    slot_index = jnp.cumsum(chosen, axis=1, dtype=jnp.int32) - chosen
-    gate_tables = jnp.sum(jnp.where(picked, routing[1:, ..., None], 0.0), axis=3)
-    placed = (chosen[..., None] > 0) & (
-        slot_index[..., None] == jnp.arange(CAP, dtype=jnp.int32)
-    )
-    same = jnp.eye(NZ, dtype=bool)[:, :, None, None, None]
-    spread = (placed[:, None] & same).astype(f32)
+    experts = experts.astype(f32)
     slots = NZ * CAP
     total_slots = NPLANE * slots
-    selector = (
-        spread.astype(bf16)
-        .reshape(NZ, NZ, NCTX, share_rows, NPLANE, CAP)
-        .transpose(4, 1, 5, 2, 0, 3)
-        .reshape(total_slots, NZ * token_count)
-    )
-    combine = (
-        (spread * gate_tables[:, :, None, :, :, None])
-        .transpose(0, 1, 3, 4, 2, 5)
-        .reshape(2, NZ * token_count, total_slots)
-        .astype(bf16)
-    )
+    tokens = NZ * token_count
+    slot_number = jnp.arange(total_slots, dtype=jnp.int32)
+    slot_group = slot_number % slots // CAP
+    slot_value = (slot_number % CAP).astype(f32)
+    owner = (slot_number[None, :] // slots == number[:, None]).astype(bf16)
+
+    def slots_of(table, group, time):
+        picked = table[:, :choices, None] == experts
+        chosen = jnp.sum(picked.astype(f32), axis=1)
+        before = (group[:, None] == group[None, :]) & (time[None, :] < time[:, None])
+        slot = dot(before.astype(bf16), chosen.astype(bf16))
+        return jnp.where(chosen > 0, slot, -1.0).astype(bf16), picked
+
+    row = jnp.arange(tokens, dtype=jnp.int32)
+    group = row // share_rows % NZ
+    table = (
+        routing.reshape(NZ, NCTX, share_rows, -1).transpose(1, 0, 2, 3).reshape(tokens, -1)
+    )
+    slot, _ = slots_of(table, group, row)
+    slot = lax.dot_general(owner, slot, (((0,), (1,)), ((), ())), preferred_element_type=f32)
+    selector = (slot == slot_value[:, None]) & (slot_group[:, None] == group[None, :])
+    selector = selector.astype(bf16)
+
+    group = row // token_count
+    table = routing.reshape(tokens, -1)
+    slot, picked = slots_of(table, group, row)
+    taken = (dot(slot, owner) == slot_value[None, :]) & (slot_group[None, :] == group[:, None])
+    combine = []
+    for part in (1, 2):
+        gates = table[:, part * choices : (part + 1) * choices, None]
+        gates = jnp.sum(jnp.where(picked, gates, 0.0), axis=1).astype(bf16)
+        combine.append(jnp.where(taken, dot(gates, owner), 0.0).astype(bf16))
 
     buckets = dot(selector, hidden).astype(bf16).reshape(NPLANE, -1, HD)
     buffer = swap(buckets, PLANE).reshape(total_slots, width)

time: 361 us -> 360 us (level)
  blocking collectives: 0 us -> 34 us
  waiting for transfers between devices: 137 us -> 116 us
  starting transfers between devices: 182 us -> 177 us
  local copies, waits for them, and re-layouts: 23.1 us -> 18.9 us
  other arithmetic: 7.29 us -> 3.38 us
    all_to_all x0 -> x1, blocking collectives: none -> 34 us  [swap(): return lax.all_to_all(array, axes, split_axis=0, concat_axis=0, tiled=True)]
    all_to_all x7 -> x6, waiting for transfers between devices: 51.6 us -> 30.6 us  [swap(): return lax.all_to_all(array, axes, split_axis=0, concat_axis=0, tiled=True)]
    all_to_all x7 -> x6, starting transfers between devices: 87.8 us -> 74.6 us  [swap(): return lax.all_to_all(array, axes, split_axis=0, concat_axis=0, tiled=True)]
    ppermute x20, starting transfers between devices: 94.4 us -> 102 us  [from_peer(): return lax.ppermute(block, axis, [(i, i ^ k) for i in range(count)])]
  transfers between devices with their start and end apart: 27 -> 26, of which waited for: 17 -> 15; matrix products, arithmetic and copies ran while one was open for 4% -> 2% of each run, Pallas kernels for 0% -> 0%
where the time goes in v6:
time: 360 us; the launch traced here: 359 us
  starting transfers between devices  177 us (49%)
  waiting for transfers between devices  116 us (32%)
  blocking collectives  34 us (9%)
  local copies, waits for them, and re-layouts  18.9 us (5%)
  Pallas kernels  5.84 us (2%)
    ppermute x20, starting transfers between devices, from_peer(): return lax.ppermute(block, axis, [(i, i ^ k) for i in range(count)])  102 us
    ppermute x20, waiting for transfers between devices, from_peer(): return lax.ppermute(block, axis, [(i, i ^ k) for i in range(count)])  85 us
    all_to_all x6, starting transfers between devices, swap(): return lax.all_to_all(array, axes, split_axis=0, concat_axis=0, tiled=True)  74.6 us
    all_to_all x1, blocking collectives, swap(): return lax.all_to_all(array, axes, split_axis=0, concat_axis=0, tiled=True)  34 us
    all_to_all x6, waiting for transfers between devices, swap(): return lax.all_to_all(array, axes, split_axis=0, concat_axis=0, tiled=True)  30.6 us
  transfers between devices with their start and end apart: 26, of which 15 were waited for; matrix products, arithmetic and copies ran while one was open for 2% of the time, Pallas kernels for 0%

profile of v6, /device:TPU:1, one launch (start us, length us, event | category | flops | bytes accessed | tf_op | source)
XLA Modules:
  0.0 358.8 jit_solution(6089732617891187042)
XLA Ops:
  1.5 26.4 %all-to-all-start = ((bf16[16,16,256]{2,1,0:T(8,128)(2,1)}), bf16[16,16,256]{2,1,0:T(8,128)(2,1)S(1)}, u32[]{:S(2)}, u32[]{:S(2)}) async-start(bf16[16,16,256]{2,1,0:T(8,128)(2,1)} %broadcast_in_dim.118), calls=%async_computation | async-start | bytes 262144 | tf_op jit(solution)/shard_map/all_to_all | solution.py:27
  28.0 2.4 dynamic-slice_bitcast_fusion.1
  30.4 3.2 collective-permute-start
  35.7 4.1 %collective-permute-start.2 = (bf16[256,384]{1,0:T(8,128)(2,1)S(1)}, bf16[256,384]{1,0:T(8,128)(2,1)S(1)}, u32[]{:S(2)}, u32[]{:S(2)}) collective-permute-start(bf16[256,384]{1,0:T(8,128)(2,1)S(1)} %get-tuple-element.65), channel_id=1, source_target_pairs={{0,128},{64,192},{128,0},{192,64},{1,129},{65,193},{129,1},{193,65... | collective-permute-start | bytes 589832 | tf_op jit(solution)/shard_map/ppermute | solution.py:39
  39.8 8.0 %collective-permute-done.1.refs_5_ = bf16[256,384]{1,0:T(8,128)(2,1)S(1)} collective-permute-done((bf16[256,384]{1,0:T(8,128)(2,1)S(1)}, bf16[256,384]{1,0:T(8,128)(2,1)S(1)}, u32[]{:S(2)}, u32[]{:S(2)}) %collective-permute-start.1) | collective-permute-done | bytes 196640 | tf_op jit(solution)/shard_map/ppermute | solution.py:39
  50.9 7.1 %all-to-all-start.1 = ((bf16[8,16,16,256]{3,2,1,0:T(8,128)(2,1)}), bf16[8,16,16,256]{3,2,1,0:T(8,128)(2,1)S(1)}, u32[]{:S(2)}, u32[]{:S(2)}) async-start(bf16[8,16,16,256]{3,2,1,0:T(8,128)(2,1)} %broadcast_in_dim.119), calls=%async_computation.1 | async-start | bytes 2097152 | tf_op jit(solution)/shard_map/all_to_all | solution.py:27
  60.5 11.1 %collective-permute-done.3.refs_6_ = bf16[256,384]{1,0:T(8,128)(2,1)S(1)} collective-permute-done((bf16[256,384]{1,0:T(8,128)(2,1)S(1)}, bf16[256,384]{1,0:T(8,128)(2,1)S(1)}, u32[]{:S(2)}, u32[]{:S(2)}) %collective-permute-start.3) | collective-permute-done | bytes 196640 | tf_op jit(solution)/shard_map/ppermute | solution.py:39
  76.5 6.5 %all-to-all-start.2 = ((bf16[32,4,4096]{2,1,0:T(4,128)(2,1)}), bf16[32,4,4096]{2,1,0:T(4,128)(2,1)}, u32[]{:S(2)}, u32[]{:S(2)}) async-start(bf16[32,4,4096]{2,1,0:T(4,128)(2,1)} %reshape.323), calls=%async_computation.2 | async-start | bytes 2097152 | tf_op jit(solution)/shard_map/all_to_all | solution.py:27
  83.3 3.5 collective-permute-start.4
  86.8 3.6 %collective-permute-start.5 = (bf16[256,384]{1,0:T(8,128)(2,1)S(1)}, bf16[256,384]{1,0:T(8,128)(2,1)S(1)}, u32[]{:S(2)}, u32[]{:S(2)}) collective-permute-start(bf16[256,384]{1,0:T(8,128)(2,1)S(1)} %copy-done.14), channel_id=1, source_target_pairs={{0,192},{64,128},{128,64},{192,0},{1,193},{65,129},{129,65},{193,1... | collective-permute-start | bytes 589832 | tf_op jit(solution)/shard_map/ppermute | solution.py:39
  93.3 4.2 %collective-permute-done.5.refs_7_ = bf16[256,384]{1,0:T(8,128)(2,1)S(1)} collective-permute-done((bf16[256,384]{1,0:T(8,128)(2,1)S(1)}, bf16[256,384]{1,0:T(8,128)(2,1)S(1)}, u32[]{:S(2)}, u32[]{:S(2)}) %collective-permute-start.5) | collective-permute-done | bytes 196640 | tf_op jit(solution)/shard_map/ppermute | solution.py:39
  102.3 20.7 %all-to-all-start.3 = ((bf16[32,4,256]{2,1,0:T(4,128)(2,1)}), bf16[32,4,256]{2,1,0:T(4,128)(2,1)S(1)}, u32[]{:S(2)}, u32[]{:S(2)}) async-start(bf16[32,4,256]{2,1,0:T(4,128)(2,1)} %bitcast.15), calls=%async_computation.3 | async-start | bytes 131072 | tf_op jit(solution)/shard_map/all_to_all | solution.py:27
  123.1 3.1 collective-permute-start.6
  126.3 4.0 %collective-permute-start.7 = (bf16[384,256]{1,0:T(8,128)(2,1)S(1)}, bf16[384,256]{1,0:T(8,128)(2,1)S(1)}, u32[]{:S(2)}, u32[]{:S(2)}) collective-permute-start(bf16[384,256]{1,0:T(8,128)(2,1)S(1)} %copy-done.17), channel_id=1, source_target_pairs={{0,128},{64,192},{128,0},{192,64},{1,129},{65,193},{129,1},{193,65... | collective-permute-start | bytes 589832 | tf_op jit(solution)/shard_map/ppermute | solution.py:39
  132.4 21.5 %collective-permute-start.9 = (bf16[32,24]{0,1:T(8,128)(2,1)S(1)}, bf16[32,24]{0,1:T(8,128)(2,1)S(1)}, u32[]{:S(2)}, u32[]{:S(2)}) collective-permute-start(bf16[32,24]{0,1:T(8,128)(2,1)S(1)} %pad_maximum_fusion.1), channel_id=1, source_target_pairs={{0,8},{8,0},{1,9},{9,1},{2,10},{10,2},{3,11},{11,3},{4,12},{12,4},... | collective-permute-start | bytes 4616 | tf_op jit(solution)/shard_map/ppermute | solution.py:39
  154.0 8.2 %collective-permute-done.9 = bf16[32,24]{0,1:T(8,128)(2,1)S(1)} collective-permute-done((bf16[32,24]{0,1:T(8,128)(2,1)S(1)}, bf16[32,24]{0,1:T(8,128)(2,1)S(1)}, u32[]{:S(2)}, u32[]{:S(2)}) %collective-permute-start.9) | collective-permute-done | bytes 1568 | tf_op jit(solution)/shard_map/ppermute | solution.py:39
  166.5 5.1 %collective-permute-start.12 = (bf16[64,256]{1,0:T(8,128)(2,1)S(1)}, bf16[64,256]{1,0:T(8,128)(2,1)S(1)}, u32[]{:S(2)}, u32[]{:S(2)}) collective-permute-start(bf16[64,256]{1,0:T(8,128)(2,1)S(1)} %reshape.328), channel_id=1, source_target_pairs={{0,192},{64,128},{128,64},{192,0},{1,193},{65,129},{129,65},{193,1... | collective-permute-start | bytes 98312 | tf_op jit(solution)/shard_map/ppermute | solution.py:39
  174.7 9.7 %all-to-all-start.4 = ((bf16[32,80,128]{2,1,0:T(8,128)(2,1)}), bf16[32,80,128]{2,1,0:T(8,128)(2,1)}, u32[]{:S(2)}, u32[]{:S(2)}) async-start(bf16[32,80,128]{2,1,0:T(8,128)(2,1)} %reshape.329), calls=%async_computation.4 | async-start | bytes 1310720 | tf_op jit(solution)/shard_map/all_to_all | solution.py:27
  185.3 12.0 %all-to-all-done.4 = bf16[32,80,128]{2,1,0:T(8,128)(2,1)} async-done(((bf16[32,80,128]{2,1,0:T(8,128)(2,1)}), bf16[32,80,128]{2,1,0:T(8,128)(2,1)}, u32[]{:S(2)}, u32[]{:S(2)}) %all-to-all-start.4) | async-done | bytes 655392 | tf_op jit(solution)/shard_map/all_to_all | solution.py:27
  204.3 3.5 shard_map.91
  207.9 5.5 %collective-permute-start.13 = (bf16[496,128]{1,0:T(8,128)(2,1)S(1)}, bf16[496,128]{1,0:T(8,128)(2,1)S(1)}, u32[]{:S(2)}, u32[]{:S(2)}) collective-permute-start(bf16[496,128]{1,0:T(8,128)(2,1)S(1)} %get-tuple-element.73), channel_id=1, source_target_pairs={{0,256},{256,0},{512,768},{768,512},{1,257},{257,1},{513,769},{769... | collective-permute-start | bytes 380936 | tf_op jit(solution)/shard_map/ppermute | solution.py:39
  213.4 11.8 %collective-permute-start.14 = (bf16[496,128]{1,0:T(8,128)(2,1)S(1)}, bf16[496,128]{1,0:T(8,128)(2,1)S(1)}, u32[]{:S(2)}, u32[]{:S(2)}) collective-permute-start(bf16[496,128]{1,0:T(8,128)(2,1)S(1)} %get-tuple-element.75), channel_id=1, source_target_pairs={{0,512},{256,768},{512,0},{768,256},{1,513},{257,769},{513,1},{769... | collective-permute-start | bytes 380936 | tf_op jit(solution)/shard_map/ppermute | solution.py:39
  225.2 3.7 %collective-permute-start.15 = (bf16[496,128]{1,0:T(8,128)(2,1)S(1)}, bf16[496,128]{1,0:T(8,128)(2,1)S(1)}, u32[]{:S(2)}, u32[]{:S(2)}) collective-permute-start(bf16[496,128]{1,0:T(8,128)(2,1)S(1)} %get-tuple-element.74), channel_id=1, source_target_pairs={{0,768},{256,512},{512,256},{768,0},{1,769},{257,513},{513,257},{7... | collective-permute-start | bytes 380936 | tf_op jit(solution)/shard_map/ppermute | solution.py:39
  229.5 35.8 %collective-permute-done.14 = bf16[496,128]{1,0:T(8,128)(2,1)S(1)} collective-permute-done((bf16[496,128]{1,0:T(8,128)(2,1)S(1)}, bf16[496,128]{1,0:T(8,128)(2,1)S(1)}, u32[]{:S(2)}, u32[]{:S(2)}) %collective-permute-start.14) | collective-permute-done | bytes 127008 | tf_op jit(solution)/shard_map/ppermute | solution.py:39
  265.6 34.0 %all_to_all.35.activated_ref = bf16[4,3,80,128]{3,2,1,0:T(8,128)(2,1)S(1)} all-to-all(bf16[4,3,80,128]{3,2,1,0:T(8,128)(2,1)S(1)} %broadcast_in_dim.135), channel_id=1, replica_groups=mesh['p'=4,'q'=4,'x'=4,'zh'=2,'y'=4,'core'=2] {'p'}, dimensions={0} | all-to-all | bytes 491520 | tf_op jit(solution)/shard_map/all_to_all | solution.py:27
  303.1 4.1 %all-to-all-start.6 = ((bf16[32,80,128]{2,1,0:T(8,128)(2,1)}), bf16[32,80,128]{2,1,0:T(8,128)(2,1)S(1)}, u32[]{:S(2)}, u32[]{:S(2)}) async-start(bf16[32,80,128]{2,1,0:T(8,128)(2,1)} %reshape.332), calls=%async_computation.6 | async-start | bytes 1310720 | tf_op jit(solution)/shard_map/all_to_all | solution.py:27
  307.7 12.6 %all-to-all-done.6 = bf16[32,80,128]{2,1,0:T(8,128)(2,1)S(1)} async-done(((bf16[32,80,128]{2,1,0:T(8,128)(2,1)}), bf16[32,80,128]{2,1,0:T(8,128)(2,1)S(1)}, u32[]{:S(2)}, u32[]{:S(2)}) %all-to-all-start.6) | async-done | bytes 655392 | tf_op jit(solution)/shard_map/all_to_all | solution.py:27
  323.3 5.5 %collective-permute-start.17 = (bf16[64,256]{1,0:T(8,128)(2,1)S(1)}, bf16[64,256]{1,0:T(8,128)(2,1)S(1)}, u32[]{:S(2)}, u32[]{:S(2)}) collective-permute-start(bf16[64,256]{1,0:T(8,128)(2,1)S(1)} %get-tuple-element.80), channel_id=1, source_target_pairs={{0,128},{64,192},{128,0},{192,64},{1,129},{65,193},{129,1},{193,65... | collective-permute-start | bytes 98312 | tf_op jit(solution)/shard_map/ppermute | solution.py:39
  328.9 3.1 collective-permute-start.18
  332.0 3.3 collective-permute-done.18
  335.4 11.7 %collective-permute-start.19 = (bf16[32,256]{1,0:T(8,128)(2,1)S(1)}, bf16[32,256]{1,0:T(8,128)(2,1)S(1)}, u32[]{:S(2)}, u32[]{:S(2)}) collective-permute-start(bf16[32,256]{1,0:T(8,128)(2,1)S(1)} %fusion.68), channel_id=1, source_target_pairs={{0,8},{8,0},{1,9},{9,1},{2,10},{10,2},{3,11},{11,3},{4,12},{12,4},... | collective-permute-start | bytes 49160 | tf_op jit(solution)/shard_map/ppermute | solution.py:39
  347.2 11.0 %collective-permute-done.19 = bf16[32,256]{1,0:T(8,128)(2,1)S(1)} collective-permute-done((bf16[32,256]{1,0:T(8,128)(2,1)S(1)}, bf16[32,256]{1,0:T(8,128)(2,1)S(1)}, u32[]{:S(2)}, u32[]{:S(2)}) %collective-permute-start.19) | collective-permute-done | bytes 16416 | tf_op jit(solution)/shard_map/ppermute | solution.py:39
  (141 shorter events, 47.6 us)
Async XLA Ops:
  0.0 74.8 %copy-start = (bf16[128,4096]{1,0:T(8,128)(2,1)S(1)}, bf16[128,4096]{1,0:T(8,128)(2,1)}, u32[]{:S(2)}) copy-start(bf16[128,4096]{1,0:T(8,128)(2,1)} %param.13) | copy-start | bytes 3145732
  1.5 48.4 %all-to-all-start = ((bf16[16,16,256]{2,1,0:T(8,128)(2,1)}), bf16[16,16,256]{2,1,0:T(8,128)(2,1)S(1)}, u32[]{:S(2)}, u32[]{:S(2)}) async-start(bf16[16,16,256]{2,1,0:T(8,128)(2,1)} %broadcast_in_dim.118), calls=%async_computation | async-start | bytes 262144 | tf_op jit(solution)/shard_map/all_to_all | solution.py:27
  30.4 9.4 %collective-permute-start = (bf16[256,384]{1,0:T(8,128)(2,1)S(1)}, bf16[256,384]{1,0:T(8,128)(2,1)S(1)}, u32[]{:S(2)}, u32[]{:S(2)}) collective-permute-start(bf16[256,384]{1,0:T(8,128)(2,1)S(1)} %get-tuple-element.67), channel_id=1, source_target_pairs={{0,64},{64,0},{128,192},{192,128},{1,65},{65,1},{129,193},{193,129... | collective-permute-start | bytes 589832 | tf_op jit(solution)/shard_map/ppermute | solution.py:39
  33.6 14.2 %collective-permute-start.1 = (bf16[256,384]{1,0:T(8,128)(2,1)S(1)}, bf16[256,384]{1,0:T(8,128)(2,1)S(1)}, u32[]{:S(2)}, u32[]{:S(2)}) collective-permute-start(bf16[256,384]{1,0:T(8,128)(2,1)S(1)} %get-tuple-element.66), channel_id=1, source_target_pairs={{0,64},{64,0},{128,192},{192,128},{1,65},{65,1},{129,193},{193,129... | collective-permute-start | bytes 589832 | tf_op jit(solution)/shard_map/ppermute | solution.py:39
  35.7 12.2 %collective-permute-start.2 = (bf16[256,384]{1,0:T(8,128)(2,1)S(1)}, bf16[256,384]{1,0:T(8,128)(2,1)S(1)}, u32[]{:S(2)}, u32[]{:S(2)}) collective-permute-start(bf16[256,384]{1,0:T(8,128)(2,1)S(1)} %get-tuple-element.65), channel_id=1, source_target_pairs={{0,128},{64,192},{128,0},{192,64},{1,129},{65,193},{129,1},{193,65... | collective-permute-start | bytes 589832 | tf_op jit(solution)/shard_map/ppermute | solution.py:39
  50.9 22.2 %all-to-all-start.1 = ((bf16[8,16,16,256]{3,2,1,0:T(8,128)(2,1)}), bf16[8,16,16,256]{3,2,1,0:T(8,128)(2,1)S(1)}, u32[]{:S(2)}, u32[]{:S(2)}) async-start(bf16[8,16,16,256]{3,2,1,0:T(8,128)(2,1)} %broadcast_in_dim.119), calls=%async_computation.1 | async-start | bytes 2097152 | tf_op jit(solution)/shard_map/all_to_all | solution.py:27
  58.1 13.5 %collective-permute-start.3 = (bf16[256,384]{1,0:T(8,128)(2,1)S(1)}, bf16[256,384]{1,0:T(8,128)(2,1)S(1)}, u32[]{:S(2)}, u32[]{:S(2)}) collective-permute-start(bf16[256,384]{1,0:T(8,128)(2,1)S(1)} %get-tuple-element.33), channel_id=1, source_target_pairs={{0,128},{64,192},{128,0},{192,64},{1,129},{65,193},{129,1},{193,65... | collective-permute-start | bytes 589832 | tf_op jit(solution)/shard_map/ppermute | solution.py:39
  76.5 23.5 %all-to-all-start.2 = ((bf16[32,4,4096]{2,1,0:T(4,128)(2,1)}), bf16[32,4,4096]{2,1,0:T(4,128)(2,1)}, u32[]{:S(2)}, u32[]{:S(2)}) async-start(bf16[32,4,4096]{2,1,0:T(4,128)(2,1)} %reshape.323), calls=%async_computation.2 | async-start | bytes 2097152 | tf_op jit(solution)/shard_map/all_to_all | solution.py:27
  83.3 10.0 %collective-permute-start.4 = (bf16[256,384]{1,0:T(8,128)(2,1)S(1)}, bf16[256,384]{1,0:T(8,128)(2,1)S(1)}, u32[]{:S(2)}, u32[]{:S(2)}) collective-permute-start(bf16[256,384]{1,0:T(8,128)(2,1)S(1)} %copy-done.15), channel_id=1, source_target_pairs={{0,192},{64,128},{128,64},{192,0},{1,193},{65,129},{129,65},{193,1... | collective-permute-start | bytes 589832 | tf_op jit(solution)/shard_map/ppermute | solution.py:39
  86.8 10.7 %collective-permute-start.5 = (bf16[256,384]{1,0:T(8,128)(2,1)S(1)}, bf16[256,384]{1,0:T(8,128)(2,1)S(1)}, u32[]{:S(2)}, u32[]{:S(2)}) collective-permute-start(bf16[256,384]{1,0:T(8,128)(2,1)S(1)} %copy-done.14), channel_id=1, source_target_pairs={{0,192},{64,128},{128,64},{192,0},{1,193},{65,129},{129,65},{193,1... | collective-permute-start | bytes 589832 | tf_op jit(solution)/shard_map/ppermute | solution.py:39
  91.3 31.8 %copy-start.18 = (bf16[384,256]{1,0:T(8,128)(2,1)S(1)}, bf16[384,256]{1,0:T(8,128)(2,1)}, u32[]{:S(2)}) copy-start(bf16[384,256]{1,0:T(8,128)(2,1)} %get-tuple-element.41) | copy-start | bytes 589828
  91.3 35.0 %copy-start.17 = (bf16[384,256]{1,0:T(8,128)(2,1)S(1)}, bf16[384,256]{1,0:T(8,128)(2,1)}, u32[]{:S(2)}) copy-start(bf16[384,256]{1,0:T(8,128)(2,1)} %get-tuple-element.42) | copy-start | bytes 589828
  91.3 39.0 %copy-start.16 = (bf16[384,256]{1,0:T(8,128)(2,1)S(1)}, bf16[384,256]{1,0:T(8,128)(2,1)}, u32[]{:S(2)}) copy-start(bf16[384,256]{1,0:T(8,128)(2,1)} %get-tuple-element.43) | copy-start | bytes 589828
  93.3 81.3 %copy-start.9 = (bf16[256,384]{1,0:T(8,128)(2,1)}, bf16[256,384]{1,0:T(8,128)(2,1)S(1)}, u32[]{:S(2)}) copy-start(bf16[256,384]{1,0:T(8,128)(2,1)S(1)} %collective-permute-done.4.refs_3_) | copy-start | bytes 589828
  97.5 77.1 %copy-start.11 = (bf16[256,384]{1,0:T(8,128)(2,1)}, bf16[256,384]{1,0:T(8,128)(2,1)S(1)}, u32[]{:S(2)}) copy-start(bf16[256,384]{1,0:T(8,128)(2,1)S(1)} %collective-permute-done.5.refs_7_) | copy-start | bytes 589828
  102.3 51.6 %all-to-all-start.3 = ((bf16[32,4,256]{2,1,0:T(4,128)(2,1)}), bf16[32,4,256]{2,1,0:T(4,128)(2,1)S(1)}, u32[]{:S(2)}, u32[]{:S(2)}) async-start(bf16[32,4,256]{2,1,0:T(4,128)(2,1)} %bitcast.15), calls=%async_computation.3 | async-start | bytes 131072 | tf_op jit(solution)/shard_map/all_to_all | solution.py:27
  123.1 30.8 %collective-permute-start.6 = (bf16[384,256]{1,0:T(8,128)(2,1)S(1)}, bf16[384,256]{1,0:T(8,128)(2,1)S(1)}, u32[]{:S(2)}, u32[]{:S(2)}) collective-permute-start(bf16[384,256]{1,0:T(8,128)(2,1)S(1)} %copy-done.18), channel_id=1, source_target_pairs={{0,64},{64,0},{128,192},{192,128},{1,65},{65,1},{129,193},{193,129... | collective-permute-start | bytes 589832 | tf_op jit(solution)/shard_map/ppermute | solution.py:39
  126.3 27.7 %collective-permute-start.7 = (bf16[384,256]{1,0:T(8,128)(2,1)S(1)}, bf16[384,256]{1,0:T(8,128)(2,1)S(1)}, u32[]{:S(2)}, u32[]{:S(2)}) collective-permute-start(bf16[384,256]{1,0:T(8,128)(2,1)S(1)} %copy-done.17), channel_id=1, source_target_pairs={{0,128},{64,192},{128,0},{192,64},{1,129},{65,193},{129,1},{193,65... | collective-permute-start | bytes 589832 | tf_op jit(solution)/shard_map/ppermute | solution.py:39
  130.3 23.7 %collective-permute-start.8 = (bf16[384,256]{1,0:T(8,128)(2,1)S(1)}, bf16[384,256]{1,0:T(8,128)(2,1)S(1)}, u32[]{:S(2)}, u32[]{:S(2)}) collective-permute-start(bf16[384,256]{1,0:T(8,128)(2,1)S(1)} %copy-done.16), channel_id=1, source_target_pairs={{0,192},{64,128},{128,64},{192,0},{1,193},{65,129},{129,65},{193,1... | collective-permute-start | bytes 589832 | tf_op jit(solution)/shard_map/ppermute | solution.py:39
  132.4 29.8 %collective-permute-start.9 = (bf16[32,24]{0,1:T(8,128)(2,1)S(1)}, bf16[32,24]{0,1:T(8,128)(2,1)S(1)}, u32[]{:S(2)}, u32[]{:S(2)}) collective-permute-start(bf16[32,24]{0,1:T(8,128)(2,1)S(1)} %pad_maximum_fusion.1), channel_id=1, source_target_pairs={{0,8},{8,0},{1,9},{9,1},{2,10},{10,2},{3,11},{11,3},{4,12},{12,4},... | collective-permute-start | bytes 4616 | tf_op jit(solution)/shard_map/ppermute | solution.py:39
  162.3 10.1 %collective-permute-start.10 = (bf16[64,256]{1,0:T(8,128)(2,1)S(1)}, bf16[64,256]{1,0:T(8,128)(2,1)S(1)}, u32[]{:S(2)}, u32[]{:S(2)}) collective-permute-start(bf16[64,256]{1,0:T(8,128)(2,1)S(1)} %reshape.328), channel_id=1, source_target_pairs={{0,64},{64,0},{128,192},{192,128},{1,65},{65,1},{129,193},{193,129... | collective-permute-start | bytes 98312 | tf_op jit(solution)/shard_map/ppermute | solution.py:39
  164.2 8.2 %collective-permute-start.11 = (bf16[64,256]{1,0:T(8,128)(2,1)S(1)}, bf16[64,256]{1,0:T(8,128)(2,1)S(1)}, u32[]{:S(2)}, u32[]{:S(2)}) collective-permute-start(bf16[64,256]{1,0:T(8,128)(2,1)S(1)} %reshape.328), channel_id=1, source_target_pairs={{0,128},{64,192},{128,0},{192,64},{1,129},{65,193},{129,1},{193,65... | collective-permute-start | bytes 98312 | tf_op jit(solution)/shard_map/ppermute | solution.py:39
  166.5 6.5 %collective-permute-start.12 = (bf16[64,256]{1,0:T(8,128)(2,1)S(1)}, bf16[64,256]{1,0:T(8,128)(2,1)S(1)}, u32[]{:S(2)}, u32[]{:S(2)}) collective-permute-start(bf16[64,256]{1,0:T(8,128)(2,1)S(1)} %reshape.328), channel_id=1, source_target_pairs={{0,192},{64,128},{128,64},{192,0},{1,193},{65,129},{129,65},{193,1... | collective-permute-start | bytes 98312 | tf_op jit(solution)/shard_map/ppermute | solution.py:39
  174.7 22.7 %all-to-all-start.4 = ((bf16[32,80,128]{2,1,0:T(8,128)(2,1)}), bf16[32,80,128]{2,1,0:T(8,128)(2,1)}, u32[]{:S(2)}, u32[]{:S(2)}) async-start(bf16[32,80,128]{2,1,0:T(8,128)(2,1)} %reshape.329), calls=%async_computation.4 | async-start | bytes 1310720 | tf_op jit(solution)/shard_map/all_to_all | solution.py:27
  207.9 21.7 %collective-permute-start.13 = (bf16[496,128]{1,0:T(8,128)(2,1)S(1)}, bf16[496,128]{1,0:T(8,128)(2,1)S(1)}, u32[]{:S(2)}, u32[]{:S(2)}) collective-permute-start(bf16[496,128]{1,0:T(8,128)(2,1)S(1)} %get-tuple-element.73), channel_id=1, source_target_pairs={{0,256},{256,0},{512,768},{768,512},{1,257},{257,1},{513,769},{769... | collective-permute-start | bytes 380936 | tf_op jit(solution)/shard_map/ppermute | solution.py:39
  213.4 51.9 %collective-permute-start.14 = (bf16[496,128]{1,0:T(8,128)(2,1)S(1)}, bf16[496,128]{1,0:T(8,128)(2,1)S(1)}, u32[]{:S(2)}, u32[]{:S(2)}) collective-permute-start(bf16[496,128]{1,0:T(8,128)(2,1)S(1)} %get-tuple-element.75), channel_id=1, source_target_pairs={{0,512},{256,768},{512,0},{768,256},{1,513},{257,769},{513,1},{769... | collective-permute-start | bytes 380936 | tf_op jit(solution)/shard_map/ppermute | solution.py:39
  225.2 40.1 %collective-permute-start.15 = (bf16[496,128]{1,0:T(8,128)(2,1)S(1)}, bf16[496,128]{1,0:T(8,128)(2,1)S(1)}, u32[]{:S(2)}, u32[]{:S(2)}) collective-permute-start(bf16[496,128]{1,0:T(8,128)(2,1)S(1)} %get-tuple-element.74), channel_id=1, source_target_pairs={{0,768},{256,512},{512,256},{768,0},{1,769},{257,513},{513,257},{7... | collective-permute-start | bytes 380936 | tf_op jit(solution)/shard_map/ppermute | solution.py:39
  303.1 17.2 %all-to-all-start.6 = ((bf16[32,80,128]{2,1,0:T(8,128)(2,1)}), bf16[32,80,128]{2,1,0:T(8,128)(2,1)S(1)}, u32[]{:S(2)}, u32[]{:S(2)}) async-start(bf16[32,80,128]{2,1,0:T(8,128)(2,1)} %reshape.332), calls=%async_computation.6 | async-start | bytes 1310720 | tf_op jit(solution)/shard_map/all_to_all | solution.py:27
  321.4 10.6 %collective-permute-start.16 = (bf16[64,256]{1,0:T(8,128)(2,1)S(1)}, bf16[64,256]{1,0:T(8,128)(2,1)S(1)}, u32[]{:S(2)}, u32[]{:S(2)}) collective-permute-start(bf16[64,256]{1,0:T(8,128)(2,1)S(1)} %get-tuple-element.78), channel_id=1, source_target_pairs={{0,64},{64,0},{128,192},{192,128},{1,65},{65,1},{129,193},{193,129... | collective-permute-start | bytes 98312 | tf_op jit(solution)/shard_map/ppermute | solution.py:39
  323.3 8.7 %collective-permute-start.17 = (bf16[64,256]{1,0:T(8,128)(2,1)S(1)}, bf16[64,256]{1,0:T(8,128)(2,1)S(1)}, u32[]{:S(2)}, u32[]{:S(2)}) collective-permute-start(bf16[64,256]{1,0:T(8,128)(2,1)S(1)} %get-tuple-element.80), channel_id=1, source_target_pairs={{0,128},{64,192},{128,0},{192,64},{1,129},{65,193},{129,1},{193,65... | collective-permute-start | bytes 98312 | tf_op jit(solution)/shard_map/ppermute | solution.py:39
  328.9 6.5 %collective-permute-start.18 = (bf16[64,256]{1,0:T(8,128)(2,1)S(1)}, bf16[64,256]{1,0:T(8,128)(2,1)S(1)}, u32[]{:S(2)}, u32[]{:S(2)}) collective-permute-start(bf16[64,256]{1,0:T(8,128)(2,1)S(1)} %get-tuple-element.79), channel_id=1, source_target_pairs={{0,192},{64,128},{128,64},{192,0},{1,193},{65,129},{129,65},{193,1... | collective-permute-start | bytes 98312 | tf_op jit(solution)/shard_map/ppermute | solution.py:39
  335.4 22.8 %collective-permute-start.19 = (bf16[32,256]{1,0:T(8,128)(2,1)S(1)}, bf16[32,256]{1,0:T(8,128)(2,1)S(1)}, u32[]{:S(2)}, u32[]{:S(2)}) collective-permute-start(bf16[32,256]{1,0:T(8,128)(2,1)S(1)} %fusion.68), channel_id=1, source_target_pairs={{0,8},{8,0},{1,9},{9,1},{2,10},{10,2},{3,11},{11,3},{4,12},{12,4},... | collective-permute-start | bytes 49160 | tf_op jit(solution)/shard_map/ppermute | solution.py:39
  (17 other events, 100.9 us)

commit v7 on v6

--- a/solution.py
+++ b/solution.py
@@ -103,17 +103,14 @@
 def gate_up_kernel(buffer_ref, gain_ref, *refs):
     *weights, out_ref, held, semaphores = refs
     copies = fetch(weights, held, semaphores)
-    _, feat, units = held.shape
+    units = held.shape[2]
     rows = buffer_ref.shape[0] // NP
     buffer = buffer_ref[...].astype(f32)
     squares = jnp.sum(buffer * buffer, axis=1, keepdims=True)
     scaled = (buffer * gain_ref[...]).astype(bf16)
     for half in range(2):
-        total = jnp.zeros((buffer.shape[0], units), f32)
-        for k in range(NQ):
-            copies[half * NQ + k].wait()
-            total = total + dot(scaled[:, k * feat : (k + 1) * feat], held[half * NQ + k])
-        total = total.astype(bf16)
+        copies[half].wait()
+        total = dot(scaled, held[half]).astype(bf16)
         for p in range(NP):
             for chunk in range(units // HD):
                 start = (half * (units // HD) + chunk) * rows
@@ -239,20 +236,27 @@
     outgoing = partial.astype(bf16).reshape(NZ * share_rows, NCTX, feat).transpose(1, 0, 2)
 
     routing = jnp.concatenate([expert_ids.astype(bf16), *split(gate_values)], axis=1)
-    outgoing, routing = lax.optimization_barrier((outgoing, routing))
-    other = from_peer(routing, "zh", NZ, 1)
-    outgoing, flight = begin(outgoing, ("down", 1), ("down", 2), ("down", 3))
+    fields = routing.shape[1]
+    routing = lax.dynamic_slice_in_dim(routing, ctx_index * share_rows, share_rows, 0)
+    routing = jnp.pad(routing, ((0, 0), (0, HD - fields)))
+    routing = jnp.where(own_group, routing[None], 0).reshape(1, NZ * share_rows, HD)
+    routing = jnp.broadcast_to(routing, (NCTX,) + routing.shape[1:])
+    outgoing = jnp.concatenate([outgoing, routing], axis=2)
+    outgoing, flight = begin(outgoing, ("down", 1), ("down", 2))
+    wide = feat + HD
     outgoing = jnp.broadcast_to(
-        outgoing[:, None], (NCTX, NZ, NZ * share_rows, feat)
-    ).reshape(NCTX * NZ, NZ * share_rows, feat)
-    arrived = swap(outgoing, CTX + ("zh",)).reshape(NCTX, NZ, NZ * share_rows, feat)
-    arrived, other = lax.optimization_barrier((end(arrived, flight), other))
-    hidden = jnp.sum(arrived.astype(f32), axis=1).astype(bf16).reshape(-1, feat)
+        outgoing[:, None], (NCTX, NZ, NZ * share_rows, wide)
+    ).reshape(NCTX * NZ, NZ * share_rows, wide)
+    arrived = swap(outgoing, CTX + ("zh",)).reshape(NCTX, NZ, NZ * share_rows, wide)
+    weight_in = [
+        jnp.concatenate([moved[name, k] for k in range(NQ)], axis=0) for name in ("gate", "up")
+    ]
+    arrived, weight_in = lax.optimization_barrier((end(arrived, flight), weight_in))
+    arrived = jnp.sum(arrived.astype(f32), axis=1)
+    hidden = arrived[:, :, :feat].astype(bf16).reshape(-1, feat)
+    routing = arrived[:, :, feat : feat + fields].reshape(-1, fields)
     choices = expert_ids.shape[1]
     token_count = expert_ids.shape[0]
-    first = zh_index == 0
-    routing = jnp.stack([jnp.where(first, routing, other), jnp.where(first, other, routing)])
-    routing = routing.astype(f32)
 
     hidden = jnp.concatenate(from_peers([hidden] * NQ, "q", NQ), axis=1)
     gain = jnp.concatenate(
@@ -284,16 +288,16 @@
 
     row = jnp.arange(tokens, dtype=jnp.int32)
     group = row // share_rows % NZ
-    table = (
-        routing.reshape(NZ, NCTX, share_rows, -1).transpose(1, 0, 2, 3).reshape(tokens, -1)
-    )
+    table = routing
     slot, _ = slots_of(table, group, row)
     slot = lax.dot_general(owner, slot, (((0,), (1,)), ((), ())), preferred_element_type=f32)
     selector = (slot == slot_value[:, None]) & (slot_group[:, None] == group[None, :])
     selector = selector.astype(bf16)
 
     group = row // token_count
-    table = routing.reshape(tokens, -1)
+    table = (
+        routing.reshape(NCTX, NZ, share_rows, -1).transpose(1, 0, 2, 3).reshape(tokens, -1)
+    )
     slot, picked = slots_of(table, group, row)
     taken = (dot(slot, owner) == slot_value[None, :]) & (slot_group[None, :] == group[:, None])
     combine = []
@@ -303,16 +307,16 @@
         combine.append(jnp.where(taken, dot(gates, owner), 0.0).astype(bf16))
 
     buckets = dot(selector, hidden).astype(bf16).reshape(NPLANE, -1, HD)
-    buffer = swap(buckets, PLANE).reshape(total_slots, width)
+    buckets, flight = begin(buckets, ("down", 3))
+    buffer = end(swap(buckets, PLANE), flight).reshape(total_slots, width)
 
     rows = total_slots // NP
     chunks = 2 * units // HD
-    names = [(name, k) for name in ("gate", "up") for k in range(NQ)]
     body = call(
         gate_up_kernel,
         (NP, chunks * rows + 16, HD),
         (buffer, gain[None]),
-        [moved[name] for name in names],
+        weight_in,
     )
     parts = [
         lax.dynamic_index_in_dim(body, jnp.bitwise_xor(p_index, k), 0, keepdims=False)

time: 360 us -> 344 us (0.956)
  starting transfers between devices: 177 us -> 161 us
  waiting for transfers between devices: 116 us -> 111 us
  other arithmetic: 3.38 us -> 8.33 us
    ppermute x20 -> x19, starting transfers between devices: 102 us -> 80.2 us  [from_peer(): return lax.ppermute(block, axis, [(i, i ^ k) for i in range(count)])]
    all_to_all x6, starting transfers between devices: 74.6 us -> 81.2 us  [swap(): return lax.all_to_all(array, axes, split_axis=0, concat_axis=0, tiled=True)]
    all_to_all x6, waiting for transfers between devices: 30.6 us -> 26.4 us  [swap(): return lax.all_to_all(array, axes, split_axis=0, concat_axis=0, tiled=True)]
    ppermute x20 -> x19, waiting for transfers between devices: 85 us -> 84.6 us  [from_peer(): return lax.ppermute(block, axis, [(i, i ^ k) for i in range(count)])]
  transfers between devices with their start and end apart: 26 -> 25, of which waited for: 15 -> 16; matrix products, arithmetic and copies ran while one was open for 2% -> 3% of each run, Pallas kernels for 0% -> 0%
where the time goes in v7:
time: 344 us; the launch traced here: 342 us
  starting transfers between devices  161 us (47%)
  waiting for transfers between devices  111 us (32%)
  blocking collectives  33.8 us (10%)
  local copies, waits for them, and re-layouts  16.7 us (5%)
  other arithmetic  8.33 us (2%)
  matrix products  5.88 us (2%)
  Pallas kernels  3.74 us (1%)
    ppermute x19, waiting for transfers between devices, from_peer(): return lax.ppermute(block, axis, [(i, i ^ k) for i in range(count)])  84.6 us
    all_to_all x6, starting transfers between devices, swap(): return lax.all_to_all(array, axes, split_axis=0, concat_axis=0, tiled=True)  81.2 us
    ppermute x19, starting transfers between devices, from_peer(): return lax.ppermute(block, axis, [(i, i ^ k) for i in range(count)])  80.2 us
    all_to_all x1, blocking collectives, swap(): return lax.all_to_all(array, axes, split_axis=0, concat_axis=0, tiled=True)  33.8 us
    all_to_all x6, waiting for transfers between devices, swap(): return lax.all_to_all(array, axes, split_axis=0, concat_axis=0, tiled=True)  26.4 us
  transfers between devices with their start and end apart: 25, of which 16 were waited for; matrix products, arithmetic and copies ran while one was open for 3% of the time, Pallas kernels for 0%

profile of v7, /device:TPU:1, one launch (start us, length us, event | category | flops | bytes accessed | tf_op | source)
XLA Modules:
  0.0 341.7 jit_solution(16328855474613677605)
XLA Ops:
  1.5 26.4 %all-to-all-start = ((bf16[16,16,256]{2,1,0:T(8,128)(2,1)}), bf16[16,16,256]{2,1,0:T(8,128)(2,1)S(1)}, u32[]{:S(2)}, u32[]{:S(2)}) async-start(bf16[16,16,256]{2,1,0:T(8,128)(2,1)} %broadcast_in_dim.146), calls=%async_computation | async-start | bytes 262144 | tf_op jit(solution)/shard_map/all_to_all | solution.py:27
  30.4 3.2 collective-permute-start
  35.6 4.1 %collective-permute-start.2 = (bf16[256,384]{1,0:T(8,128)(2,1)S(1)}, bf16[256,384]{1,0:T(8,128)(2,1)S(1)}, u32[]{:S(2)}, u32[]{:S(2)}) collective-permute-start(bf16[256,384]{1,0:T(8,128)(2,1)S(1)} %get-tuple-element.67), channel_id=1, source_target_pairs={{0,128},{64,192},{128,0},{192,64},{1,129},{65,193},{129,1},{193,65... | collective-permute-start | bytes 589832 | tf_op jit(solution)/shard_map/ppermute | solution.py:39
  39.8 8.1 %collective-permute-done.1 = bf16[256,384]{1,0:T(8,128)(2,1)S(1)} collective-permute-done((bf16[256,384]{1,0:T(8,128)(2,1)S(1)}, bf16[256,384]{1,0:T(8,128)(2,1)S(1)}, u32[]{:S(2)}, u32[]{:S(2)}) %collective-permute-start.1) | collective-permute-done | bytes 196640 | tf_op jit(solution)/shard_map/ppermute | solution.py:39
  50.9 7.1 %all-to-all-start.1 = ((bf16[8,16,16,256]{3,2,1,0:T(8,128)(2,1)}), bf16[8,16,16,256]{3,2,1,0:T(8,128)(2,1)S(1)}, u32[]{:S(2)}, u32[]{:S(2)}) async-start(bf16[8,16,16,256]{3,2,1,0:T(8,128)(2,1)} %broadcast_in_dim.147), calls=%async_computation.1 | async-start | bytes 2097152 | tf_op jit(solution)/shard_map/all_to_all | solution.py:27
  60.5 11.1 %collective-permute-done.3 = bf16[256,384]{1,0:T(8,128)(2,1)S(1)} collective-permute-done((bf16[256,384]{1,0:T(8,128)(2,1)S(1)}, bf16[256,384]{1,0:T(8,128)(2,1)S(1)}, u32[]{:S(2)}, u32[]{:S(2)}) %collective-permute-start.3) | collective-permute-done | bytes 196640 | tf_op jit(solution)/shard_map/ppermute | solution.py:39
  76.5 6.4 %all-to-all-start.2 = ((bf16[32,4,4096]{2,1,0:T(4,128)(2,1)}), bf16[32,4,4096]{2,1,0:T(4,128)(2,1)S(1)}, u32[]{:S(2)}, u32[]{:S(2)}) async-start(bf16[32,4,4096]{2,1,0:T(4,128)(2,1)} %reshape.332), calls=%async_computation.2 | async-start | bytes 2097152 | tf_op jit(solution)/shard_map/all_to_all | solution.py:27
  84.3 3.5 %collective-permute-start.4 = (bf16[256,384]{1,0:T(8,128)(2,1)}, bf16[256,384]{1,0:T(8,128)(2,1)S(1)}, u32[]{:S(2)}, u32[]{:S(2)}) collective-permute-start(bf16[256,384]{1,0:T(8,128)(2,1)} %get-tuple-element.37), channel_id=1, source_target_pairs={{0,192},{64,128},{128,64},{192,0},{1,193},{65,129},{129,65},{193,1... | collective-permute-start | bytes 589832 | tf_op jit(solution)/shard_map/ppermute | solution.py:39
  87.8 3.6 %collective-permute-start.5 = (bf16[256,384]{1,0:T(8,128)(2,1)}, bf16[256,384]{1,0:T(8,128)(2,1)S(1)}, u32[]{:S(2)}, u32[]{:S(2)}) collective-permute-start(bf16[256,384]{1,0:T(8,128)(2,1)} %get-tuple-element.38), channel_id=1, source_target_pairs={{0,192},{64,128},{128,64},{192,0},{1,193},{65,129},{129,65},{193,1... | collective-permute-start | bytes 589832 | tf_op jit(solution)/shard_map/ppermute | solution.py:39
  91.5 3.0 collective-permute-done.4
  94.5 4.2 %collective-permute-done.5 = bf16[256,384]{1,0:T(8,128)(2,1)S(1)} collective-permute-done((bf16[256,384]{1,0:T(8,128)(2,1)}, bf16[256,384]{1,0:T(8,128)(2,1)S(1)}, u32[]{:S(2)}, u32[]{:S(2)}) %collective-permute-start.5) | collective-permute-done | bytes 196640 | tf_op jit(solution)/shard_map/ppermute | solution.py:39
  101.0 22.0 %all-to-all-start.3 = ((bf16[32,4,384]{2,1,0:T(4,128)(2,1)}), bf16[32,4,384]{2,1,0:T(4,128)(2,1)S(1)}, u32[]{:S(2)}, u32[]{:S(2)}) async-start(bf16[32,4,384]{2,1,0:T(4,128)(2,1)} %bitcast.15), calls=%async_computation.3 | async-start | bytes 196608 | tf_op jit(solution)/shard_map/all_to_all | solution.py:27
  124.8 3.1 collective-permute-start.6
  127.9 4.0 %collective-permute-start.7 = (bf16[384,256]{1,0:T(8,128)(2,1)}, bf16[384,256]{1,0:T(8,128)(2,1)S(1)}, u32[]{:S(2)}, u32[]{:S(2)}) collective-permute-start(bf16[384,256]{1,0:T(8,128)(2,1)} %get-tuple-element.42), channel_id=1, source_target_pairs={{0,128},{64,192},{128,0},{192,64},{1,129},{65,193},{129,1},{193,65... | collective-permute-start | bytes 589832 | tf_op jit(solution)/shard_map/ppermute | solution.py:39
  134.0 8.4 %collective-permute-done.6.refs_1_ = bf16[384,256]{1,0:T(8,128)(2,1)S(1)} collective-permute-done((bf16[384,256]{1,0:T(8,128)(2,1)}, bf16[384,256]{1,0:T(8,128)(2,1)S(1)}, u32[]{:S(2)}, u32[]{:S(2)}) %collective-permute-start.6) | collective-permute-done | bytes 196640 | tf_op jit(solution)/shard_map/ppermute | solution.py:39
  142.4 7.1 %all-to-all-done.3 = bf16[32,4,384]{2,1,0:T(4,128)(2,1)S(1)} async-done(((bf16[32,4,384]{2,1,0:T(4,128)(2,1)}), bf16[32,4,384]{2,1,0:T(4,128)(2,1)S(1)}, u32[]{:S(2)}, u32[]{:S(2)}) %all-to-all-start.3) | async-done | bytes 98336 | tf_op jit(solution)/shard_map/all_to_all | solution.py:27
  153.8 5.2 %collective-permute-start.8 = (bf16[64,256]{1,0:T(8,128)(2,1)S(1)}, bf16[64,256]{1,0:T(8,128)(2,1)S(1)}, u32[]{:S(2)}, u32[]{:S(2)}) collective-permute-start(bf16[64,256]{1,0:T(8,128)(2,1)S(1)} %reshape.338), channel_id=1, source_target_pairs={{0,64},{64,0},{128,192},{192,128},{1,65},{65,1},{129,193},{193,129... | collective-permute-start | bytes 98312 | tf_op jit(solution)/shard_map/ppermute | solution.py:39
  166.8 13.7 %all-to-all-start.4 = ((bf16[32,80,128]{2,1,0:T(8,128)(2,1)}), bf16[32,80,128]{2,1,0:T(8,128)(2,1)}, u32[]{:S(2)}, u32[]{:S(2)}) async-start(bf16[32,80,128]{2,1,0:T(8,128)(2,1)} %reshape.339), calls=%async_computation.4 | async-start | bytes 1310720 | tf_op jit(solution)/shard_map/all_to_all | solution.py:27
  180.6 3.9 %collective-permute-start.11 = (bf16[384,256]{1,0:T(8,128)(2,1)S(1)}, bf16[384,256]{1,0:T(8,128)(2,1)S(1)}, u32[]{:S(2)}, u32[]{:S(2)}) collective-permute-start(bf16[384,256]{1,0:T(8,128)(2,1)S(1)} %copy-done.9), channel_id=1, source_target_pairs={{0,192},{64,128},{128,64},{192,0},{1,193},{65,129},{129,65},{193,1... | collective-permute-start | bytes 589832 | tf_op jit(solution)/shard_map/ppermute | solution.py:39
  185.5 5.2 %collective-permute-done.11.refs_3_ = bf16[384,256]{1,0:T(8,128)(2,1)S(1)} collective-permute-done((bf16[384,256]{1,0:T(8,128)(2,1)S(1)}, bf16[384,256]{1,0:T(8,128)(2,1)S(1)}, u32[]{:S(2)}, u32[]{:S(2)}) %collective-permute-start.11) | collective-permute-done | bytes 196640 | tf_op jit(solution)/shard_map/ppermute | solution.py:39
  197.2 6.1 %collective-permute-start.14 = (bf16[496,128]{1,0:T(8,128)(2,1)S(1)}, bf16[496,128]{1,0:T(8,128)(2,1)S(1)}, u32[]{:S(2)}, u32[]{:S(2)}) collective-permute-start(bf16[496,128]{1,0:T(8,128)(2,1)S(1)} %get-tuple-element.76), channel_id=1, source_target_pairs={{0,768},{256,512},{512,256},{768,0},{1,769},{257,513},{513,257},{7... | collective-permute-start | bytes 380936 | tf_op jit(solution)/shard_map/ppermute | solution.py:39
  203.2 3.4 %collective-permute-start.13 = (bf16[496,128]{1,0:T(8,128)(2,1)S(1)}, bf16[496,128]{1,0:T(8,128)(2,1)S(1)}, u32[]{:S(2)}, u32[]{:S(2)}) collective-permute-start(bf16[496,128]{1,0:T(8,128)(2,1)S(1)} %get-tuple-element.77), channel_id=1, source_target_pairs={{0,512},{256,768},{512,0},{768,256},{1,513},{257,769},{513,1},{769... | collective-permute-start | bytes 380936 | tf_op jit(solution)/shard_map/ppermute | solution.py:39
  206.7 11.6 %collective-permute-start.12 = (bf16[496,128]{1,0:T(8,128)(2,1)S(1)}, bf16[496,128]{1,0:T(8,128)(2,1)S(1)}, u32[]{:S(2)}, u32[]{:S(2)}) collective-permute-start(bf16[496,128]{1,0:T(8,128)(2,1)S(1)} %get-tuple-element.75), channel_id=1, source_target_pairs={{0,256},{256,0},{512,768},{768,512},{1,257},{257,1},{513,769},{769... | collective-permute-start | bytes 380936 | tf_op jit(solution)/shard_map/ppermute | solution.py:39
  218.3 24.1 %collective-permute-done.14 = bf16[496,128]{1,0:T(8,128)(2,1)S(1)} collective-permute-done((bf16[496,128]{1,0:T(8,128)(2,1)S(1)}, bf16[496,128]{1,0:T(8,128)(2,1)S(1)}, u32[]{:S(2)}, u32[]{:S(2)}) %collective-permute-start.14) | collective-permute-done | bytes 127008 | tf_op jit(solution)/shard_map/ppermute | solution.py:39
  242.5 6.8 %collective-permute-done.13 = bf16[496,128]{1,0:T(8,128)(2,1)S(1)} collective-permute-done((bf16[496,128]{1,0:T(8,128)(2,1)S(1)}, bf16[496,128]{1,0:T(8,128)(2,1)S(1)}, u32[]{:S(2)}, u32[]{:S(2)}) %collective-permute-start.13) | collective-permute-done | bytes 127008 | tf_op jit(solution)/shard_map/ppermute | solution.py:39
  250.5 33.8 %all_to_all.35.activated_ref = bf16[4,3,80,128]{3,2,1,0:T(8,128)(2,1)S(1)} all-to-all(bf16[4,3,80,128]{3,2,1,0:T(8,128)(2,1)S(1)} %broadcast_in_dim.168), channel_id=1, replica_groups=mesh['p'=4,'q'=4,'x'=4,'zh'=2,'y'=4,'core'=2] {'p'}, dimensions={0} | all-to-all | bytes 491520 | tf_op jit(solution)/shard_map/all_to_all | solution.py:27
  287.8 5.5 %all-to-all-start.6 = ((bf16[32,80,128]{2,1,0:T(8,128)(2,1)}), bf16[32,80,128]{2,1,0:T(8,128)(2,1)S(1)}, u32[]{:S(2)}, u32[]{:S(2)}) async-start(bf16[32,80,128]{2,1,0:T(8,128)(2,1)} %reshape.342), calls=%async_computation.6 | async-start | bytes 1310720 | tf_op jit(solution)/shard_map/all_to_all | solution.py:27
  293.8 12.5 %all-to-all-done.6 = bf16[32,80,128]{2,1,0:T(8,128)(2,1)S(1)} async-done(((bf16[32,80,128]{2,1,0:T(8,128)(2,1)}), bf16[32,80,128]{2,1,0:T(8,128)(2,1)S(1)}, u32[]{:S(2)}, u32[]{:S(2)}) %all-to-all-start.6) | async-done | bytes 655392 | tf_op jit(solution)/shard_map/all_to_all | solution.py:27
  309.3 2.6 collective-permute-start.16
  311.9 4.8 %collective-permute-start.15 = (bf16[64,256]{1,0:T(8,128)(2,1)S(1)}, bf16[64,256]{1,0:T(8,128)(2,1)S(1)}, u32[]{:S(2)}, u32[]{:S(2)}) collective-permute-start(bf16[64,256]{1,0:T(8,128)(2,1)S(1)} %get-tuple-element.80), channel_id=1, source_target_pairs={{0,64},{64,0},{128,192},{192,128},{1,65},{65,1},{129,193},{193,129... | collective-permute-start | bytes 98312 | tf_op jit(solution)/shard_map/ppermute | solution.py:39
  318.0 10.6 %collective-permute-start.18 = (bf16[32,256]{1,0:T(8,128)(2,1)S(1)}, bf16[32,256]{1,0:T(8,128)(2,1)S(1)}, u32[]{:S(2)}, u32[]{:S(2)}) collective-permute-start(bf16[32,256]{1,0:T(8,128)(2,1)S(1)} %fusion.68), channel_id=1, source_target_pairs={{0,8},{8,0},{1,9},{9,1},{2,10},{10,2},{3,11},{11,3},{4,12},{12,4},... | collective-permute-start | bytes 49160 | tf_op jit(solution)/shard_map/ppermute | solution.py:39
  328.7 12.4 %collective-permute-done.18 = bf16[32,256]{1,0:T(8,128)(2,1)S(1)} collective-permute-done((bf16[32,256]{1,0:T(8,128)(2,1)S(1)}, bf16[32,256]{1,0:T(8,128)(2,1)S(1)}, u32[]{:S(2)}, u32[]{:S(2)}) %collective-permute-start.18) | collective-permute-done | bytes 16416 | tf_op jit(solution)/shard_map/ppermute | solution.py:39
  (151 shorter events, 53.2 us)
Async XLA Ops:
  0.0 74.8 %copy-start = (bf16[128,4096]{1,0:T(8,128)(2,1)S(1)}, bf16[128,4096]{1,0:T(8,128)(2,1)}, u32[]{:S(2)}) copy-start(bf16[128,4096]{1,0:T(8,128)(2,1)} %param.13) | copy-start | bytes 3145732
  1.5 48.4 %all-to-all-start = ((bf16[16,16,256]{2,1,0:T(8,128)(2,1)}), bf16[16,16,256]{2,1,0:T(8,128)(2,1)S(1)}, u32[]{:S(2)}, u32[]{:S(2)}) async-start(bf16[16,16,256]{2,1,0:T(8,128)(2,1)} %broadcast_in_dim.146), calls=%async_computation | async-start | bytes 262144 | tf_op jit(solution)/shard_map/all_to_all | solution.py:27
  30.4 9.4 %collective-permute-start = (bf16[256,384]{1,0:T(8,128)(2,1)S(1)}, bf16[256,384]{1,0:T(8,128)(2,1)S(1)}, u32[]{:S(2)}, u32[]{:S(2)}) collective-permute-start(bf16[256,384]{1,0:T(8,128)(2,1)S(1)} %get-tuple-element.69), channel_id=1, source_target_pairs={{0,64},{64,0},{128,192},{192,128},{1,65},{65,1},{129,193},{193,129... | collective-permute-start | bytes 589832 | tf_op jit(solution)/shard_map/ppermute | solution.py:39
  33.6 14.3 %collective-permute-start.1 = (bf16[256,384]{1,0:T(8,128)(2,1)S(1)}, bf16[256,384]{1,0:T(8,128)(2,1)S(1)}, u32[]{:S(2)}, u32[]{:S(2)}) collective-permute-start(bf16[256,384]{1,0:T(8,128)(2,1)S(1)} %get-tuple-element.68), channel_id=1, source_target_pairs={{0,64},{64,0},{128,192},{192,128},{1,65},{65,1},{129,193},{193,129... | collective-permute-start | bytes 589832 | tf_op jit(solution)/shard_map/ppermute | solution.py:39
  35.6 12.2 %collective-permute-start.2 = (bf16[256,384]{1,0:T(8,128)(2,1)S(1)}, bf16[256,384]{1,0:T(8,128)(2,1)S(1)}, u32[]{:S(2)}, u32[]{:S(2)}) collective-permute-start(bf16[256,384]{1,0:T(8,128)(2,1)S(1)} %get-tuple-element.67), channel_id=1, source_target_pairs={{0,128},{64,192},{128,0},{192,64},{1,129},{65,193},{129,1},{193,65... | collective-permute-start | bytes 589832 | tf_op jit(solution)/shard_map/ppermute | solution.py:39
  50.9 22.2 %all-to-all-start.1 = ((bf16[8,16,16,256]{3,2,1,0:T(8,128)(2,1)}), bf16[8,16,16,256]{3,2,1,0:T(8,128)(2,1)S(1)}, u32[]{:S(2)}, u32[]{:S(2)}) async-start(bf16[8,16,16,256]{3,2,1,0:T(8,128)(2,1)} %broadcast_in_dim.147), calls=%async_computation.1 | async-start | bytes 2097152 | tf_op jit(solution)/shard_map/all_to_all | solution.py:27
  58.1 13.5 %collective-permute-start.3 = (bf16[256,384]{1,0:T(8,128)(2,1)S(1)}, bf16[256,384]{1,0:T(8,128)(2,1)S(1)}, u32[]{:S(2)}, u32[]{:S(2)}) collective-permute-start(bf16[256,384]{1,0:T(8,128)(2,1)S(1)} %get-tuple-element.34), channel_id=1, source_target_pairs={{0,128},{64,192},{128,0},{192,64},{1,129},{65,193},{129,1},{193,65... | collective-permute-start | bytes 589832 | tf_op jit(solution)/shard_map/ppermute | solution.py:39
  76.5 23.3 %all-to-all-start.2 = ((bf16[32,4,4096]{2,1,0:T(4,128)(2,1)}), bf16[32,4,4096]{2,1,0:T(4,128)(2,1)S(1)}, u32[]{:S(2)}, u32[]{:S(2)}) async-start(bf16[32,4,4096]{2,1,0:T(4,128)(2,1)} %reshape.332), calls=%async_computation.2 | async-start | bytes 2097152 | tf_op jit(solution)/shard_map/all_to_all | solution.py:27
  84.3 10.2 %collective-permute-start.4 = (bf16[256,384]{1,0:T(8,128)(2,1)}, bf16[256,384]{1,0:T(8,128)(2,1)S(1)}, u32[]{:S(2)}, u32[]{:S(2)}) collective-permute-start(bf16[256,384]{1,0:T(8,128)(2,1)} %get-tuple-element.37), channel_id=1, source_target_pairs={{0,192},{64,128},{128,64},{192,0},{1,193},{65,129},{129,65},{193,1... | collective-permute-start | bytes 589832 | tf_op jit(solution)/shard_map/ppermute | solution.py:39
  87.8 10.9 %collective-permute-start.5 = (bf16[256,384]{1,0:T(8,128)(2,1)}, bf16[256,384]{1,0:T(8,128)(2,1)S(1)}, u32[]{:S(2)}, u32[]{:S(2)}) collective-permute-start(bf16[256,384]{1,0:T(8,128)(2,1)} %get-tuple-element.38), channel_id=1, source_target_pairs={{0,192},{64,128},{128,64},{192,0},{1,193},{65,129},{129,65},{193,1... | collective-permute-start | bytes 589832 | tf_op jit(solution)/shard_map/ppermute | solution.py:39
  98.7 33.8 %copy-start.15 = (bf16[256,384]{1,0:T(8,128)(2,1)}, bf16[256,384]{1,0:T(8,128)(2,1)S(1)}, u32[]{:S(2)}) copy-start(bf16[256,384]{1,0:T(8,128)(2,1)S(1)} %collective-permute-done.5) | copy-start | bytes 589828
  101.0 48.5 %all-to-all-start.3 = ((bf16[32,4,384]{2,1,0:T(4,128)(2,1)}), bf16[32,4,384]{2,1,0:T(4,128)(2,1)S(1)}, u32[]{:S(2)}, u32[]{:S(2)}) async-start(bf16[32,4,384]{2,1,0:T(4,128)(2,1)} %bitcast.15), calls=%async_computation.3 | async-start | bytes 196608 | tf_op jit(solution)/shard_map/all_to_all | solution.py:27
  124.8 17.6 %collective-permute-start.6 = (bf16[384,256]{1,0:T(8,128)(2,1)}, bf16[384,256]{1,0:T(8,128)(2,1)S(1)}, u32[]{:S(2)}, u32[]{:S(2)}) collective-permute-start(bf16[384,256]{1,0:T(8,128)(2,1)} %get-tuple-element.41), channel_id=1, source_target_pairs={{0,64},{64,0},{128,192},{192,128},{1,65},{65,1},{129,193},{193,129... | collective-permute-start | bytes 589832 | tf_op jit(solution)/shard_map/ppermute | solution.py:39
  127.9 14.5 %collective-permute-start.7 = (bf16[384,256]{1,0:T(8,128)(2,1)}, bf16[384,256]{1,0:T(8,128)(2,1)S(1)}, u32[]{:S(2)}, u32[]{:S(2)}) collective-permute-start(bf16[384,256]{1,0:T(8,128)(2,1)} %get-tuple-element.42), channel_id=1, source_target_pairs={{0,128},{64,192},{128,0},{192,64},{1,129},{65,193},{129,1},{193,65... | collective-permute-start | bytes 589832 | tf_op jit(solution)/shard_map/ppermute | solution.py:39
  142.4 24.4 %copy-start.2 = (bf16[384,256]{1,0:T(8,128)(2,1)}, bf16[384,256]{1,0:T(8,128)(2,1)S(1)}, u32[]{:S(2)}) copy-start(bf16[384,256]{1,0:T(8,128)(2,1)S(1)} %collective-permute-done.6.refs_1_) | copy-start | bytes 589828
  142.4 24.4 %copy-start.4 = (bf16[384,256]{1,0:T(8,128)(2,1)}, bf16[384,256]{1,0:T(8,128)(2,1)S(1)}, u32[]{:S(2)}) copy-start(bf16[384,256]{1,0:T(8,128)(2,1)S(1)} %collective-permute-done.7.refs_2_) | copy-start | bytes 589828
  149.7 12.1 %collective-permute-start.10 = (bf16[64,256]{1,0:T(8,128)(2,1)S(1)}, bf16[64,256]{1,0:T(8,128)(2,1)S(1)}, u32[]{:S(2)}, u32[]{:S(2)}) collective-permute-start(bf16[64,256]{1,0:T(8,128)(2,1)S(1)} %reshape.338), channel_id=1, source_target_pairs={{0,192},{64,128},{128,64},{192,0},{1,193},{65,129},{129,65},{193,1... | collective-permute-start | bytes 98312 | tf_op jit(solution)/shard_map/ppermute | solution.py:39
  151.6 10.1 %collective-permute-start.9 = (bf16[64,256]{1,0:T(8,128)(2,1)S(1)}, bf16[64,256]{1,0:T(8,128)(2,1)S(1)}, u32[]{:S(2)}, u32[]{:S(2)}) collective-permute-start(bf16[64,256]{1,0:T(8,128)(2,1)S(1)} %reshape.338), channel_id=1, source_target_pairs={{0,128},{64,192},{128,0},{192,64},{1,129},{65,193},{129,1},{193,65... | collective-permute-start | bytes 98312 | tf_op jit(solution)/shard_map/ppermute | solution.py:39
  153.8 8.0 %collective-permute-start.8 = (bf16[64,256]{1,0:T(8,128)(2,1)S(1)}, bf16[64,256]{1,0:T(8,128)(2,1)S(1)}, u32[]{:S(2)}, u32[]{:S(2)}) collective-permute-start(bf16[64,256]{1,0:T(8,128)(2,1)S(1)} %reshape.338), channel_id=1, source_target_pairs={{0,64},{64,0},{128,192},{192,128},{1,65},{65,1},{129,193},{193,129... | collective-permute-start | bytes 98312 | tf_op jit(solution)/shard_map/ppermute | solution.py:39
  166.8 26.7 %all-to-all-start.4 = ((bf16[32,80,128]{2,1,0:T(8,128)(2,1)}), bf16[32,80,128]{2,1,0:T(8,128)(2,1)}, u32[]{:S(2)}, u32[]{:S(2)}) async-start(bf16[32,80,128]{2,1,0:T(8,128)(2,1)} %reshape.339), calls=%async_computation.4 | async-start | bytes 1310720 | tf_op jit(solution)/shard_map/all_to_all | solution.py:27
  180.6 10.0 %collective-permute-start.11 = (bf16[384,256]{1,0:T(8,128)(2,1)S(1)}, bf16[384,256]{1,0:T(8,128)(2,1)S(1)}, u32[]{:S(2)}, u32[]{:S(2)}) collective-permute-start(bf16[384,256]{1,0:T(8,128)(2,1)S(1)} %copy-done.9), channel_id=1, source_target_pairs={{0,192},{64,128},{128,64},{192,0},{1,193},{65,129},{129,65},{193,1... | collective-permute-start | bytes 589832 | tf_op jit(solution)/shard_map/ppermute | solution.py:39
  197.1 87.2 %copy-start.3 = (bf16[384,256]{1,0:T(8,128)(2,1)S(1)}, bf16[384,256]{1,0:T(8,128)(2,1)}, u32[]{:S(2)}) copy-start(bf16[384,256]{1,0:T(8,128)(2,1)} %copy-done.2) | copy-start | bytes 589828
  197.1 87.2 %copy-start.5 = (bf16[384,256]{1,0:T(8,128)(2,1)S(1)}, bf16[384,256]{1,0:T(8,128)(2,1)}, u32[]{:S(2)}) copy-start(bf16[384,256]{1,0:T(8,128)(2,1)} %copy-done.4) | copy-start | bytes 589828
  197.1 87.2 %copy-start.7 = (bf16[384,256]{1,0:T(8,128)(2,1)S(1)}, bf16[384,256]{1,0:T(8,128)(2,1)}, u32[]{:S(2)}) copy-start(bf16[384,256]{1,0:T(8,128)(2,1)} %copy-done.6) | copy-start | bytes 589828
  197.2 45.3 %collective-permute-start.14 = (bf16[496,128]{1,0:T(8,128)(2,1)S(1)}, bf16[496,128]{1,0:T(8,128)(2,1)S(1)}, u32[]{:S(2)}, u32[]{:S(2)}) collective-permute-start(bf16[496,128]{1,0:T(8,128)(2,1)S(1)} %get-tuple-element.76), channel_id=1, source_target_pairs={{0,768},{256,512},{512,256},{768,0},{1,769},{257,513},{513,257},{7... | collective-permute-start | bytes 380936 | tf_op jit(solution)/shard_map/ppermute | solution.py:39
  203.2 46.0 %collective-permute-start.13 = (bf16[496,128]{1,0:T(8,128)(2,1)S(1)}, bf16[496,128]{1,0:T(8,128)(2,1)S(1)}, u32[]{:S(2)}, u32[]{:S(2)}) collective-permute-start(bf16[496,128]{1,0:T(8,128)(2,1)S(1)} %get-tuple-element.77), channel_id=1, source_target_pairs={{0,512},{256,768},{512,0},{768,256},{1,513},{257,769},{513,1},{769... | collective-permute-start | bytes 380936 | tf_op jit(solution)/shard_map/ppermute | solution.py:39
  206.7 42.6 %collective-permute-start.12 = (bf16[496,128]{1,0:T(8,128)(2,1)S(1)}, bf16[496,128]{1,0:T(8,128)(2,1)S(1)}, u32[]{:S(2)}, u32[]{:S(2)}) collective-permute-start(bf16[496,128]{1,0:T(8,128)(2,1)S(1)} %get-tuple-element.75), channel_id=1, source_target_pairs={{0,256},{256,0},{512,768},{768,512},{1,257},{257,1},{513,769},{769... | collective-permute-start | bytes 380936 | tf_op jit(solution)/shard_map/ppermute | solution.py:39
  287.8 18.4 %all-to-all-start.6 = ((bf16[32,80,128]{2,1,0:T(8,128)(2,1)}), bf16[32,80,128]{2,1,0:T(8,128)(2,1)S(1)}, u32[]{:S(2)}, u32[]{:S(2)}) async-start(bf16[32,80,128]{2,1,0:T(8,128)(2,1)} %reshape.342), calls=%async_computation.6 | async-start | bytes 1310720 | tf_op jit(solution)/shard_map/all_to_all | solution.py:27
  307.4 9.3 %collective-permute-start.17 = (bf16[64,256]{1,0:T(8,128)(2,1)S(1)}, bf16[64,256]{1,0:T(8,128)(2,1)S(1)}, u32[]{:S(2)}, u32[]{:S(2)}) collective-permute-start(bf16[64,256]{1,0:T(8,128)(2,1)S(1)} %get-tuple-element.81), channel_id=1, source_target_pairs={{0,192},{64,128},{128,64},{192,0},{1,193},{65,129},{129,65},{193,1... | collective-permute-start | bytes 98312 | tf_op jit(solution)/shard_map/ppermute | solution.py:39
  309.3 7.4 %collective-permute-start.16 = (bf16[64,256]{1,0:T(8,128)(2,1)S(1)}, bf16[64,256]{1,0:T(8,128)(2,1)S(1)}, u32[]{:S(2)}, u32[]{:S(2)}) collective-permute-start(bf16[64,256]{1,0:T(8,128)(2,1)S(1)} %get-tuple-element.82), channel_id=1, source_target_pairs={{0,128},{64,192},{128,0},{192,64},{1,129},{65,193},{129,1},{193,65... | collective-permute-start | bytes 98312 | tf_op jit(solution)/shard_map/ppermute | solution.py:39
  311.9 6.1 %collective-permute-start.15 = (bf16[64,256]{1,0:T(8,128)(2,1)S(1)}, bf16[64,256]{1,0:T(8,128)(2,1)S(1)}, u32[]{:S(2)}, u32[]{:S(2)}) collective-permute-start(bf16[64,256]{1,0:T(8,128)(2,1)S(1)} %get-tuple-element.80), channel_id=1, source_target_pairs={{0,64},{64,0},{128,192},{192,128},{1,65},{65,1},{129,193},{193,129... | collective-permute-start | bytes 98312 | tf_op jit(solution)/shard_map/ppermute | solution.py:39
  318.0 23.1 %collective-permute-start.18 = (bf16[32,256]{1,0:T(8,128)(2,1)S(1)}, bf16[32,256]{1,0:T(8,128)(2,1)S(1)}, u32[]{:S(2)}, u32[]{:S(2)}) collective-permute-start(bf16[32,256]{1,0:T(8,128)(2,1)S(1)} %fusion.68), channel_id=1, source_target_pairs={{0,8},{8,0},{1,9},{9,1},{2,10},{10,2},{3,11},{11,3},{4,12},{12,4},... | collective-permute-start | bytes 49160 | tf_op jit(solution)/shard_map/ppermute | solution.py:39
  (19 other events, 134.3 us)

commit v8 on v7

--- a/solution.py
+++ b/solution.py
@@ -63,16 +63,6 @@
         keys_values, (piece * height, (KV_HEADS + x_index) * HD), (height, HD)
     )
     return share(jnp.concatenate([key_piece, value_piece], axis=1), CTX, NCTX)
-
-
-def key_positions(rows):
-    height = rows // (NY * NC)
-    number = jnp.arange(NCTX * rows, dtype=jnp.int32)
-    return (
-        (number % (NCTX * height)) // height * rows
-        + number // (NCTX * height) * height
-        + number % height
-    )
 
 
 def call(kernel, shape, operands, weights):
@@ -146,18 +136,38 @@
         out_ref[:, k * feat : (k + 1) * feat] = dot(activated, held[k]).astype(bf16)
 
 
-def attend(queries, key_part, value_part, key_pos, ctx_index):
-    rows = queries.shape[0]
+def attend_column(queries, column, ctx_index):
+    heads, rows, _ = queries.shape
+    height = column.shape[1]
+    piece = lax.axis_index(("y", "core"))
+    keys = column.reshape(-1, 2 * HD)
+    number = jnp.arange(keys.shape[0], dtype=jnp.int32)
+    key_pos = number // height * rows + piece * height + number % height
     query_pos = ctx_index * rows + jnp.arange(rows, dtype=jnp.int32)
+    allowed = key_pos[None, None, :] <= query_pos[None, :, None]
     scores = (
-        jnp.einsum("qd,kd->qk", queries, key_part, preferred_element_type=f32) * HD ** (-0.5)
-    )
-    allowed = key_pos[None, :] <= query_pos[:, None]
+        jnp.einsum("hqd,kd->hqk", queries, keys[:, :HD], preferred_element_type=f32)
+        * HD ** (-0.5)
+    )
     scores = jnp.where(allowed, scores, masked_score)
-    top = jnp.max(scores, axis=-1, keepdims=True)
-    weights = jnp.where(allowed, jnp.exp(scores - top), 0.0)
-    total = jnp.sum(weights, axis=-1, keepdims=True)
-    return (dot(weights.astype(bf16), value_part) / total).astype(bf16)
+    shift = lax.reduce_precision(jnp.max(scores, axis=-1), 8, 7)
+    weights = jnp.where(allowed, jnp.exp(scores - shift[:, :, None]), 0.0)
+    total = jnp.sum(weights, axis=-1)
+    sums = jnp.einsum(
+        "hqk,kd->hqd", weights.astype(bf16), keys[:, HD:], preferred_element_type=f32
+    )
+    stats = jnp.stack([shift.astype(bf16), *split(total)], axis=1)
+    stats = jnp.pad(stats, ((0, 0), (0, 16 - stats.shape[1]), (0, HD - rows)))
+    return jnp.concatenate([sums.astype(bf16), stats], axis=1)
+
+
+def merge(parts, rows):
+    parts = parts.astype(f32)
+    shift = parts[:, rows, :rows]
+    total = parts[:, rows + 1, :rows] + parts[:, rows + 2, :rows]
+    scale = jnp.exp(shift - jnp.max(shift, axis=0, keepdims=True))
+    sums = jnp.sum(parts[:, :rows] * scale[:, :, None], axis=0)
+    return (sums / jnp.sum(total * scale, axis=0)[:, None]).astype(bf16)
 
 
 def shards(
@@ -214,12 +224,11 @@
 
     rows = keys_values.shape[0]
     _, flight = begin(None, ("gate", 1), ("up", 1), ("gate", 2))
+    peers = share(queries, ("y", "core"), NY * NC)
     column = end(gather_column(keys_values, x_index), flight)
-    column, flight = begin(column, ("up", 2))
-    segment = end(share(column, ("y", "core"), NY * NC), flight).reshape(NCTX * rows, 2 * HD)
-    attended = attend(
-        queries, segment[:, :HD], segment[:, HD:], key_positions(rows), ctx_index
-    )
+    column, peers = lax.optimization_barrier((column, peers))
+    attended, flight = begin(attend_column(peers, column, ctx_index), ("up", 2))
+    attended = merge(end(swap(attended, ("y", "core")), flight), rows)
     attended, flight = begin(attended, ("gate", 3), ("up", 3))
 
     share_rows = attended.shape[0] // (NPLANE * NZ)

time: 344 us -> 347 us (level)
    all_to_all x6 -> x7, waiting for transfers between devices: 26.4 us -> 39 us  [swap(): return lax.all_to_all(array, axes, split_axis=0, concat_axis=0, tiled=True)]
    ppermute x19, waiting for transfers between devices: 84.6 us -> 74.8 us  [from_peer(): return lax.ppermute(block, axis, [(i, i ^ k) for i in range(count)])]
    all_to_all x6 -> x7, starting transfers between devices: 81.2 us -> 76.8 us  [swap(): return lax.all_to_all(array, axes, split_axis=0, concat_axis=0, tiled=True)]
  transfers between devices with their start and end apart: 25 -> 26, of which waited for: 16 -> 16; matrix products, arithmetic and copies ran while one was open for 3% -> 4% of each run, Pallas kernels for 0% -> 0%
where the time goes in v8:
time: 347 us; the launch traced here: 345 us
  starting transfers between devices  160 us (46%)
  waiting for transfers between devices  114 us (33%)
  blocking collectives  35.1 us (10%)
  local copies, waits for them, and re-layouts  16.6 us (5%)
  other arithmetic  9.44 us (3%)
  matrix products  5.55 us (2%)
  Pallas kernels  3.74 us (1%)
    ppermute x19, starting transfers between devices, from_peer(): return lax.ppermute(block, axis, [(i, i ^ k) for i in range(count)])  83.1 us
    all_to_all x7, starting transfers between devices, swap(): return lax.all_to_all(array, axes, split_axis=0, concat_axis=0, tiled=True)  76.8 us
    ppermute x19, waiting for transfers between devices, from_peer(): return lax.ppermute(block, axis, [(i, i ^ k) for i in range(count)])  74.8 us
    all_to_all x7, waiting for transfers between devices, swap(): return lax.all_to_all(array, axes, split_axis=0, concat_axis=0, tiled=True)  39 us
    all_to_all x1, blocking collectives, swap(): return lax.all_to_all(array, axes, split_axis=0, concat_axis=0, tiled=True)  35.1 us
  transfers between devices with their start and end apart: 26, of which 16 were waited for; matrix products, arithmetic and copies ran while one was open for 4% of the time, Pallas kernels for 0%

profile of v8, /device:TPU:1, one launch (start us, length us, event | category | flops | bytes accessed | tf_op | source)
XLA Modules:
  0.0 345.1 jit_solution(10916186991979226463)
XLA Ops:
  1.5 26.4 %all-to-all-start = ((bf16[16,16,256]{2,1,0:T(8,128)(2,1)}), bf16[16,16,256]{2,1,0:T(8,128)(2,1)S(1)}, u32[]{:S(2)}, u32[]{:S(2)}) async-start(bf16[16,16,256]{2,1,0:T(8,128)(2,1)} %broadcast_in_dim.160), calls=%async_computation | async-start | bytes 262144 | tf_op jit(solution)/shard_map/all_to_all | solution.py:27
  30.4 3.2 collective-permute-start
  35.7 4.1 %collective-permute-start.2 = (bf16[256,384]{1,0:T(8,128)(2,1)S(1)}, bf16[256,384]{1,0:T(8,128)(2,1)S(1)}, u32[]{:S(2)}, u32[]{:S(2)}) collective-permute-start(bf16[256,384]{1,0:T(8,128)(2,1)S(1)} %get-tuple-element.73), channel_id=1, source_target_pairs={{0,128},{64,192},{128,0},{192,64},{1,129},{65,193},{129,1},{193,65... | collective-permute-start | bytes 589832 | tf_op jit(solution)/shard_map/ppermute | solution.py:39
  39.8 10.0 %all-to-all-done = bf16[16,16,256]{2,1,0:T(8,128)(2,1)S(1)} async-done(((bf16[16,16,256]{2,1,0:T(8,128)(2,1)}), bf16[16,16,256]{2,1,0:T(8,128)(2,1)S(1)}, u32[]{:S(2)}, u32[]{:S(2)}) %all-to-all-start) | async-done | bytes 131104 | tf_op jit(solution)/shard_map/all_to_all | solution.py:27
  50.6 7.1 %all-to-all-start.1 = ((bf16[8,128,128]{2,1,0:T(8,128)(2,1)}), bf16[8,128,128]{2,1,0:T(8,128)(2,1)S(1)}, u32[]{:S(2)}, u32[]{:S(2)}) async-start(bf16[8,128,128]{2,1,0:T(8,128)(2,1)} %broadcast_in_dim.161), calls=%async_computation.1 | async-start | bytes 524288 | tf_op jit(solution)/shard_map/all_to_all | solution.py:27
  57.9 6.3 %all-to-all-done.1 = bf16[8,128,128]{2,1,0:T(8,128)(2,1)S(1)} async-done(((bf16[8,128,128]{2,1,0:T(8,128)(2,1)}), bf16[8,128,128]{2,1,0:T(8,128)(2,1)S(1)}, u32[]{:S(2)}, u32[]{:S(2)}) %all-to-all-start.1) | async-done | bytes 262176 | tf_op jit(solution)/shard_map/all_to_all | solution.py:27
  66.2 4.4 %all-to-all-start.2 = ((bf16[8,144,128]{2,1,0:T(8,128)(2,1)}), bf16[8,144,128]{2,1,0:T(8,128)(2,1)S(1)}, u32[]{:S(2)}, u32[]{:S(2)}) async-start(bf16[8,144,128]{2,1,0:T(8,128)(2,1)} %fusion.16), calls=%async_computation.2 | async-start | bytes 589824 | tf_op jit(solution)/shard_map/all_to_all | solution.py:27
  72.9 11.1 %collective-permute-done.3 = bf16[256,384]{1,0:T(8,128)(2,1)S(1)} collective-permute-done((bf16[256,384]{1,0:T(8,128)(2,1)S(1)}, bf16[256,384]{1,0:T(8,128)(2,1)S(1)}, u32[]{:S(2)}, u32[]{:S(2)}) %collective-permute-start.3) | collective-permute-done | bytes 196640 | tf_op jit(solution)/shard_map/ppermute | solution.py:39
  86.3 7.7 %all-to-all-start.3 = ((bf16[32,4,4096]{2,1,0:T(4,128)(2,1)}), bf16[32,4,4096]{2,1,0:T(4,128)(2,1)S(1)}, u32[]{:S(2)}, u32[]{:S(2)}) async-start(bf16[32,4,4096]{2,1,0:T(4,128)(2,1)} %reshape.393), calls=%async_computation.3 | async-start | bytes 2097152 | tf_op jit(solution)/shard_map/all_to_all | solution.py:27
  97.7 4.8 %collective-permute-start.5 = (bf16[256,384]{1,0:T(8,128)(2,1)}, bf16[256,384]{1,0:T(8,128)(2,1)S(1)}, u32[]{:S(2)}, u32[]{:S(2)}) collective-permute-start(bf16[256,384]{1,0:T(8,128)(2,1)} %get-tuple-element.42), channel_id=1, source_target_pairs={{0,192},{64,128},{128,64},{192,0},{1,193},{65,129},{129,65},{193,1... | collective-permute-start | bytes 589832 | tf_op jit(solution)/shard_map/ppermute | solution.py:39
  102.6 3.0 collective-permute-done.4
  105.6 4.2 %collective-permute-done.5 = bf16[256,384]{1,0:T(8,128)(2,1)S(1)} collective-permute-done((bf16[256,384]{1,0:T(8,128)(2,1)}, bf16[256,384]{1,0:T(8,128)(2,1)S(1)}, u32[]{:S(2)}, u32[]{:S(2)}) %collective-permute-start.5) | collective-permute-done | bytes 196640 | tf_op jit(solution)/shard_map/ppermute | solution.py:39
  112.2 14.1 %all-to-all-start.4 = ((bf16[32,4,384]{2,1,0:T(4,128)(2,1)}), bf16[32,4,384]{2,1,0:T(4,128)(2,1)S(1)}, u32[]{:S(2)}, u32[]{:S(2)}) async-start(bf16[32,4,384]{2,1,0:T(4,128)(2,1)} %bitcast.20), calls=%async_computation.4 | async-start | bytes 196608 | tf_op jit(solution)/shard_map/all_to_all | solution.py:27
  128.0 3.1 collective-permute-start.6
  131.2 4.0 %collective-permute-start.7 = (bf16[384,256]{1,0:T(8,128)(2,1)}, bf16[384,256]{1,0:T(8,128)(2,1)S(1)}, u32[]{:S(2)}, u32[]{:S(2)}) collective-permute-start(bf16[384,256]{1,0:T(8,128)(2,1)} %get-tuple-element.46), channel_id=1, source_target_pairs={{0,128},{64,192},{128,0},{192,64},{1,129},{65,193},{129,1},{193,65... | collective-permute-start | bytes 589832 | tf_op jit(solution)/shard_map/ppermute | solution.py:39
  137.3 8.5 %collective-permute-done.6.refs_1_ = bf16[384,256]{1,0:T(8,128)(2,1)S(1)} collective-permute-done((bf16[384,256]{1,0:T(8,128)(2,1)}, bf16[384,256]{1,0:T(8,128)(2,1)S(1)}, u32[]{:S(2)}, u32[]{:S(2)}) %collective-permute-start.6) | collective-permute-done | bytes 196640 | tf_op jit(solution)/shard_map/ppermute | solution.py:39
  145.8 6.7 %all-to-all-done.4 = bf16[32,4,384]{2,1,0:T(4,128)(2,1)S(1)} async-done(((bf16[32,4,384]{2,1,0:T(4,128)(2,1)}), bf16[32,4,384]{2,1,0:T(4,128)(2,1)S(1)}, u32[]{:S(2)}, u32[]{:S(2)}) %all-to-all-start.4) | async-done | bytes 98336 | tf_op jit(solution)/shard_map/all_to_all | solution.py:27
  157.2 4.8 %collective-permute-start.8 = (bf16[64,256]{1,0:T(8,128)(2,1)S(1)}, bf16[64,256]{1,0:T(8,128)(2,1)S(1)}, u32[]{:S(2)}, u32[]{:S(2)}) collective-permute-start(bf16[64,256]{1,0:T(8,128)(2,1)S(1)} %reshape.399), channel_id=1, source_target_pairs={{0,64},{64,0},{128,192},{192,128},{1,65},{65,1},{129,193},{193,129... | collective-permute-start | bytes 98312 | tf_op jit(solution)/shard_map/ppermute | solution.py:39
  169.7 12.8 %all-to-all-start.5 = ((bf16[32,80,128]{2,1,0:T(8,128)(2,1)}), bf16[32,80,128]{2,1,0:T(8,128)(2,1)}, u32[]{:S(2)}, u32[]{:S(2)}) async-start(bf16[32,80,128]{2,1,0:T(8,128)(2,1)} %reshape.400), calls=%async_computation.5 | async-start | bytes 1310720 | tf_op jit(solution)/shard_map/all_to_all | solution.py:27
  182.6 4.9 %collective-permute-start.11 = (bf16[384,256]{1,0:T(8,128)(2,1)S(1)}, bf16[384,256]{1,0:T(8,128)(2,1)S(1)}, u32[]{:S(2)}, u32[]{:S(2)}) collective-permute-start(bf16[384,256]{1,0:T(8,128)(2,1)S(1)} %copy-done.12), channel_id=1, source_target_pairs={{0,192},{64,128},{128,64},{192,0},{1,193},{65,129},{129,65},{193,1... | collective-permute-start | bytes 589832 | tf_op jit(solution)/shard_map/ppermute | solution.py:39
  188.4 4.2 %collective-permute-done.11.refs_3_ = bf16[384,256]{1,0:T(8,128)(2,1)S(1)} collective-permute-done((bf16[384,256]{1,0:T(8,128)(2,1)S(1)}, bf16[384,256]{1,0:T(8,128)(2,1)S(1)}, u32[]{:S(2)}, u32[]{:S(2)}) %collective-permute-start.11) | collective-permute-done | bytes 196640 | tf_op jit(solution)/shard_map/ppermute | solution.py:39
  199.2 7.3 %collective-permute-start.14 = (bf16[496,128]{1,0:T(8,128)(2,1)S(1)}, bf16[496,128]{1,0:T(8,128)(2,1)S(1)}, u32[]{:S(2)}, u32[]{:S(2)}) collective-permute-start(bf16[496,128]{1,0:T(8,128)(2,1)S(1)} %get-tuple-element.82), channel_id=1, source_target_pairs={{0,768},{256,512},{512,256},{768,0},{1,769},{257,513},{513,257},{7... | collective-permute-start | bytes 380936 | tf_op jit(solution)/shard_map/ppermute | solution.py:39
  208.6 11.7 %collective-permute-start.12 = (bf16[496,128]{1,0:T(8,128)(2,1)S(1)}, bf16[496,128]{1,0:T(8,128)(2,1)S(1)}, u32[]{:S(2)}, u32[]{:S(2)}) collective-permute-start(bf16[496,128]{1,0:T(8,128)(2,1)S(1)} %get-tuple-element.81), channel_id=1, source_target_pairs={{0,256},{256,0},{512,768},{768,512},{1,257},{257,1},{513,769},{769... | collective-permute-start | bytes 380936 | tf_op jit(solution)/shard_map/ppermute | solution.py:39
  220.4 24.1 %collective-permute-done.14 = bf16[496,128]{1,0:T(8,128)(2,1)S(1)} collective-permute-done((bf16[496,128]{1,0:T(8,128)(2,1)S(1)}, bf16[496,128]{1,0:T(8,128)(2,1)S(1)}, u32[]{:S(2)}, u32[]{:S(2)}) %collective-permute-start.14) | collective-permute-done | bytes 127008 | tf_op jit(solution)/shard_map/ppermute | solution.py:39
  244.5 6.7 %collective-permute-done.13 = bf16[496,128]{1,0:T(8,128)(2,1)S(1)} collective-permute-done((bf16[496,128]{1,0:T(8,128)(2,1)S(1)}, bf16[496,128]{1,0:T(8,128)(2,1)S(1)}, u32[]{:S(2)}, u32[]{:S(2)}) %collective-permute-start.13) | collective-permute-done | bytes 127008 | tf_op jit(solution)/shard_map/ppermute | solution.py:39
  252.4 35.1 %all_to_all.40.activated_ref = bf16[4,3,80,128]{3,2,1,0:T(8,128)(2,1)S(1)} all-to-all(bf16[4,3,80,128]{3,2,1,0:T(8,128)(2,1)S(1)} %broadcast_in_dim.182), channel_id=1, replica_groups=mesh['p'=4,'q'=4,'x'=4,'zh'=2,'y'=4,'core'=2] {'p'}, dimensions={0} | all-to-all | bytes 491520 | tf_op jit(solution)/shard_map/all_to_all | solution.py:27
  291.0 4.3 %all-to-all-start.7 = ((bf16[32,80,128]{2,1,0:T(8,128)(2,1)}), bf16[32,80,128]{2,1,0:T(8,128)(2,1)S(1)}, u32[]{:S(2)}, u32[]{:S(2)}) async-start(bf16[32,80,128]{2,1,0:T(8,128)(2,1)} %reshape.403), calls=%async_computation.7 | async-start | bytes 1310720 | tf_op jit(solution)/shard_map/all_to_all | solution.py:27
  295.8 12.6 %all-to-all-done.7 = bf16[32,80,128]{2,1,0:T(8,128)(2,1)S(1)} async-done(((bf16[32,80,128]{2,1,0:T(8,128)(2,1)}), bf16[32,80,128]{2,1,0:T(8,128)(2,1)S(1)}, u32[]{:S(2)}, u32[]{:S(2)}) %all-to-all-start.7) | async-done | bytes 655392 | tf_op jit(solution)/shard_map/all_to_all | solution.py:27
  309.5 4.5 %collective-permute-start.17 = (bf16[64,256]{1,0:T(8,128)(2,1)S(1)}, bf16[64,256]{1,0:T(8,128)(2,1)S(1)}, u32[]{:S(2)}, u32[]{:S(2)}) collective-permute-start(bf16[64,256]{1,0:T(8,128)(2,1)S(1)} %get-tuple-element.87), channel_id=1, source_target_pairs={{0,192},{64,128},{128,64},{192,0},{1,193},{65,129},{129,65},{193,1... | collective-permute-start | bytes 98312 | tf_op jit(solution)/shard_map/ppermute | solution.py:39
  314.0 2.6 collective-permute-start.16
  321.3 12.6 %collective-permute-start.18 = (bf16[32,256]{1,0:T(8,128)(2,1)S(1)}, bf16[32,256]{1,0:T(8,128)(2,1)S(1)}, u32[]{:S(2)}, u32[]{:S(2)}) collective-permute-start(bf16[32,256]{1,0:T(8,128)(2,1)S(1)} %fusion.58), channel_id=1, source_target_pairs={{0,8},{8,0},{1,9},{9,1},{2,10},{10,2},{3,11},{11,3},{4,12},{12,4},... | collective-permute-start | bytes 49160 | tf_op jit(solution)/shard_map/ppermute | solution.py:39
  334.0 10.5 %collective-permute-done.18 = bf16[32,256]{1,0:T(8,128)(2,1)S(1)} collective-permute-done((bf16[32,256]{1,0:T(8,128)(2,1)S(1)}, bf16[32,256]{1,0:T(8,128)(2,1)S(1)}, u32[]{:S(2)}, u32[]{:S(2)}) %collective-permute-start.18) | collective-permute-done | bytes 16416 | tf_op jit(solution)/shard_map/ppermute | solution.py:39
  (166 shorter events, 56.7 us)
Async XLA Ops:
  0.0 84.6 %copy-start = (bf16[128,4096]{1,0:T(8,128)(2,1)S(1)}, bf16[128,4096]{1,0:T(8,128)(2,1)}, u32[]{:S(2)}) copy-start(bf16[128,4096]{1,0:T(8,128)(2,1)} %param.13) | copy-start | bytes 3145732
  1.5 48.4 %all-to-all-start = ((bf16[16,16,256]{2,1,0:T(8,128)(2,1)}), bf16[16,16,256]{2,1,0:T(8,128)(2,1)S(1)}, u32[]{:S(2)}, u32[]{:S(2)}) async-start(bf16[16,16,256]{2,1,0:T(8,128)(2,1)} %broadcast_in_dim.160), calls=%async_computation | async-start | bytes 262144 | tf_op jit(solution)/shard_map/all_to_all | solution.py:27
  30.4 27.4 %collective-permute-start = (bf16[256,384]{1,0:T(8,128)(2,1)S(1)}, bf16[256,384]{1,0:T(8,128)(2,1)S(1)}, u32[]{:S(2)}, u32[]{:S(2)}) collective-permute-start(bf16[256,384]{1,0:T(8,128)(2,1)S(1)} %get-tuple-element.75), channel_id=1, source_target_pairs={{0,64},{64,0},{128,192},{192,128},{1,65},{65,1},{129,193},{193,129... | collective-permute-start | bytes 589832 | tf_op jit(solution)/shard_map/ppermute | solution.py:39
  33.6 24.2 %collective-permute-start.1 = (bf16[256,384]{1,0:T(8,128)(2,1)S(1)}, bf16[256,384]{1,0:T(8,128)(2,1)S(1)}, u32[]{:S(2)}, u32[]{:S(2)}) collective-permute-start(bf16[256,384]{1,0:T(8,128)(2,1)S(1)} %get-tuple-element.74), channel_id=1, source_target_pairs={{0,64},{64,0},{128,192},{192,128},{1,65},{65,1},{129,193},{193,129... | collective-permute-start | bytes 589832 | tf_op jit(solution)/shard_map/ppermute | solution.py:39
  35.7 22.2 %collective-permute-start.2 = (bf16[256,384]{1,0:T(8,128)(2,1)S(1)}, bf16[256,384]{1,0:T(8,128)(2,1)S(1)}, u32[]{:S(2)}, u32[]{:S(2)}) collective-permute-start(bf16[256,384]{1,0:T(8,128)(2,1)S(1)} %get-tuple-element.73), channel_id=1, source_target_pairs={{0,128},{64,192},{128,0},{192,64},{1,129},{65,193},{129,1},{193,65... | collective-permute-start | bytes 589832 | tf_op jit(solution)/shard_map/ppermute | solution.py:39
  50.6 13.6 %all-to-all-start.1 = ((bf16[8,128,128]{2,1,0:T(8,128)(2,1)}), bf16[8,128,128]{2,1,0:T(8,128)(2,1)S(1)}, u32[]{:S(2)}, u32[]{:S(2)}) async-start(bf16[8,128,128]{2,1,0:T(8,128)(2,1)} %broadcast_in_dim.161), calls=%async_computation.1 | async-start | bytes 524288 | tf_op jit(solution)/shard_map/all_to_all | solution.py:27
  66.2 17.8 %all-to-all-start.2 = ((bf16[8,144,128]{2,1,0:T(8,128)(2,1)}), bf16[8,144,128]{2,1,0:T(8,128)(2,1)S(1)}, u32[]{:S(2)}, u32[]{:S(2)}) async-start(bf16[8,144,128]{2,1,0:T(8,128)(2,1)} %fusion.16), calls=%async_computation.2 | async-start | bytes 589824 | tf_op jit(solution)/shard_map/all_to_all | solution.py:27
  70.5 13.4 %collective-permute-start.3 = (bf16[256,384]{1,0:T(8,128)(2,1)S(1)}, bf16[256,384]{1,0:T(8,128)(2,1)S(1)}, u32[]{:S(2)}, u32[]{:S(2)}) collective-permute-start(bf16[256,384]{1,0:T(8,128)(2,1)S(1)} %get-tuple-element.38), channel_id=1, source_target_pairs={{0,128},{64,192},{128,0},{192,64},{1,129},{65,193},{129,1},{193,65... | collective-permute-start | bytes 589832 | tf_op jit(solution)/shard_map/ppermute | solution.py:39
  86.3 24.6 %all-to-all-start.3 = ((bf16[32,4,4096]{2,1,0:T(4,128)(2,1)}), bf16[32,4,4096]{2,1,0:T(4,128)(2,1)S(1)}, u32[]{:S(2)}, u32[]{:S(2)}) async-start(bf16[32,4,4096]{2,1,0:T(4,128)(2,1)} %reshape.393), calls=%async_computation.3 | async-start | bytes 2097152 | tf_op jit(solution)/shard_map/all_to_all | solution.py:27
  95.4 10.2 %collective-permute-start.4 = (bf16[256,384]{1,0:T(8,128)(2,1)}, bf16[256,384]{1,0:T(8,128)(2,1)S(1)}, u32[]{:S(2)}, u32[]{:S(2)}) collective-permute-start(bf16[256,384]{1,0:T(8,128)(2,1)} %get-tuple-element.41), channel_id=1, source_target_pairs={{0,192},{64,128},{128,64},{192,0},{1,193},{65,129},{129,65},{193,1... | collective-permute-start | bytes 589832 | tf_op jit(solution)/shard_map/ppermute | solution.py:39
  97.7 12.1 %collective-permute-start.5 = (bf16[256,384]{1,0:T(8,128)(2,1)}, bf16[256,384]{1,0:T(8,128)(2,1)S(1)}, u32[]{:S(2)}, u32[]{:S(2)}) collective-permute-start(bf16[256,384]{1,0:T(8,128)(2,1)} %get-tuple-element.42), channel_id=1, source_target_pairs={{0,192},{64,128},{128,64},{192,0},{1,193},{65,129},{129,65},{193,1... | collective-permute-start | bytes 589832 | tf_op jit(solution)/shard_map/ppermute | solution.py:39
  109.8 25.9 %copy-start.15 = (bf16[256,384]{1,0:T(8,128)(2,1)}, bf16[256,384]{1,0:T(8,128)(2,1)S(1)}, u32[]{:S(2)}) copy-start(bf16[256,384]{1,0:T(8,128)(2,1)S(1)} %collective-permute-done.5) | copy-start | bytes 589828
  112.2 40.3 %all-to-all-start.4 = ((bf16[32,4,384]{2,1,0:T(4,128)(2,1)}), bf16[32,4,384]{2,1,0:T(4,128)(2,1)S(1)}, u32[]{:S(2)}, u32[]{:S(2)}) async-start(bf16[32,4,384]{2,1,0:T(4,128)(2,1)} %bitcast.20), calls=%async_computation.4 | async-start | bytes 196608 | tf_op jit(solution)/shard_map/all_to_all | solution.py:27
  128.0 17.7 %collective-permute-start.6 = (bf16[384,256]{1,0:T(8,128)(2,1)}, bf16[384,256]{1,0:T(8,128)(2,1)S(1)}, u32[]{:S(2)}, u32[]{:S(2)}) collective-permute-start(bf16[384,256]{1,0:T(8,128)(2,1)} %get-tuple-element.45), channel_id=1, source_target_pairs={{0,64},{64,0},{128,192},{192,128},{1,65},{65,1},{129,193},{193,129... | collective-permute-start | bytes 589832 | tf_op jit(solution)/shard_map/ppermute | solution.py:39
  131.2 14.6 %collective-permute-start.7 = (bf16[384,256]{1,0:T(8,128)(2,1)}, bf16[384,256]{1,0:T(8,128)(2,1)S(1)}, u32[]{:S(2)}, u32[]{:S(2)}) collective-permute-start(bf16[384,256]{1,0:T(8,128)(2,1)} %get-tuple-element.46), channel_id=1, source_target_pairs={{0,128},{64,192},{128,0},{192,64},{1,129},{65,193},{129,1},{193,65... | collective-permute-start | bytes 589832 | tf_op jit(solution)/shard_map/ppermute | solution.py:39
  145.8 23.9 %copy-start.2 = (bf16[384,256]{1,0:T(8,128)(2,1)}, bf16[384,256]{1,0:T(8,128)(2,1)S(1)}, u32[]{:S(2)}) copy-start(bf16[384,256]{1,0:T(8,128)(2,1)S(1)} %collective-permute-done.6.refs_1_) | copy-start | bytes 589828
  152.7 12.0 %collective-permute-start.10 = (bf16[64,256]{1,0:T(8,128)(2,1)S(1)}, bf16[64,256]{1,0:T(8,128)(2,1)S(1)}, u32[]{:S(2)}, u32[]{:S(2)}) collective-permute-start(bf16[64,256]{1,0:T(8,128)(2,1)S(1)} %reshape.399), channel_id=1, source_target_pairs={{0,192},{64,128},{128,64},{192,0},{1,193},{65,129},{129,65},{193,1... | collective-permute-start | bytes 98312 | tf_op jit(solution)/shard_map/ppermute | solution.py:39
  154.7 9.9 %collective-permute-start.9 = (bf16[64,256]{1,0:T(8,128)(2,1)S(1)}, bf16[64,256]{1,0:T(8,128)(2,1)S(1)}, u32[]{:S(2)}, u32[]{:S(2)}) collective-permute-start(bf16[64,256]{1,0:T(8,128)(2,1)S(1)} %reshape.399), channel_id=1, source_target_pairs={{0,128},{64,192},{128,0},{192,64},{1,129},{65,193},{129,1},{193,65... | collective-permute-start | bytes 98312 | tf_op jit(solution)/shard_map/ppermute | solution.py:39
  157.2 7.5 %collective-permute-start.8 = (bf16[64,256]{1,0:T(8,128)(2,1)S(1)}, bf16[64,256]{1,0:T(8,128)(2,1)S(1)}, u32[]{:S(2)}, u32[]{:S(2)}) collective-permute-start(bf16[64,256]{1,0:T(8,128)(2,1)S(1)} %reshape.399), channel_id=1, source_target_pairs={{0,64},{64,0},{128,192},{192,128},{1,65},{65,1},{129,193},{193,129... | collective-permute-start | bytes 98312 | tf_op jit(solution)/shard_map/ppermute | solution.py:39
  169.7 25.8 %all-to-all-start.5 = ((bf16[32,80,128]{2,1,0:T(8,128)(2,1)}), bf16[32,80,128]{2,1,0:T(8,128)(2,1)}, u32[]{:S(2)}, u32[]{:S(2)}) async-start(bf16[32,80,128]{2,1,0:T(8,128)(2,1)} %reshape.400), calls=%async_computation.5 | async-start | bytes 1310720 | tf_op jit(solution)/shard_map/all_to_all | solution.py:27
  182.6 10.0 %collective-permute-start.11 = (bf16[384,256]{1,0:T(8,128)(2,1)S(1)}, bf16[384,256]{1,0:T(8,128)(2,1)S(1)}, u32[]{:S(2)}, u32[]{:S(2)}) collective-permute-start(bf16[384,256]{1,0:T(8,128)(2,1)S(1)} %copy-done.12), channel_id=1, source_target_pairs={{0,192},{64,128},{128,64},{192,0},{1,193},{65,129},{129,65},{193,1... | collective-permute-start | bytes 589832 | tf_op jit(solution)/shard_map/ppermute | solution.py:39
  199.2 88.4 %copy-start.3 = (bf16[384,256]{1,0:T(8,128)(2,1)S(1)}, bf16[384,256]{1,0:T(8,128)(2,1)}, u32[]{:S(2)}) copy-start(bf16[384,256]{1,0:T(8,128)(2,1)} %copy-done.2) | copy-start | bytes 589828
  199.2 88.4 %copy-start.5 = (bf16[384,256]{1,0:T(8,128)(2,1)S(1)}, bf16[384,256]{1,0:T(8,128)(2,1)}, u32[]{:S(2)}) copy-start(bf16[384,256]{1,0:T(8,128)(2,1)} %copy-done.4) | copy-start | bytes 589828
  199.2 88.4 %copy-start.7 = (bf16[384,256]{1,0:T(8,128)(2,1)S(1)}, bf16[384,256]{1,0:T(8,128)(2,1)}, u32[]{:S(2)}) copy-start(bf16[384,256]{1,0:T(8,128)(2,1)} %copy-done.6) | copy-start | bytes 589828
  199.2 45.3 %collective-permute-start.14 = (bf16[496,128]{1,0:T(8,128)(2,1)S(1)}, bf16[496,128]{1,0:T(8,128)(2,1)S(1)}, u32[]{:S(2)}, u32[]{:S(2)}) collective-permute-start(bf16[496,128]{1,0:T(8,128)(2,1)S(1)} %get-tuple-element.82), channel_id=1, source_target_pairs={{0,768},{256,512},{512,256},{768,0},{1,769},{257,513},{513,257},{7... | collective-permute-start | bytes 380936 | tf_op jit(solution)/shard_map/ppermute | solution.py:39
  206.5 44.7 %collective-permute-start.13 = (bf16[496,128]{1,0:T(8,128)(2,1)S(1)}, bf16[496,128]{1,0:T(8,128)(2,1)S(1)}, u32[]{:S(2)}, u32[]{:S(2)}) collective-permute-start(bf16[496,128]{1,0:T(8,128)(2,1)S(1)} %get-tuple-element.83), channel_id=1, source_target_pairs={{0,512},{256,768},{512,0},{768,256},{1,513},{257,769},{513,1},{769... | collective-permute-start | bytes 380936 | tf_op jit(solution)/shard_map/ppermute | solution.py:39
  208.6 42.6 %collective-permute-start.12 = (bf16[496,128]{1,0:T(8,128)(2,1)S(1)}, bf16[496,128]{1,0:T(8,128)(2,1)S(1)}, u32[]{:S(2)}, u32[]{:S(2)}) collective-permute-start(bf16[496,128]{1,0:T(8,128)(2,1)S(1)} %get-tuple-element.81), channel_id=1, source_target_pairs={{0,256},{256,0},{512,768},{768,512},{1,257},{257,1},{513,769},{769... | collective-permute-start | bytes 380936 | tf_op jit(solution)/shard_map/ppermute | solution.py:39
  291.0 17.3 %all-to-all-start.7 = ((bf16[32,80,128]{2,1,0:T(8,128)(2,1)}), bf16[32,80,128]{2,1,0:T(8,128)(2,1)S(1)}, u32[]{:S(2)}, u32[]{:S(2)}) async-start(bf16[32,80,128]{2,1,0:T(8,128)(2,1)} %reshape.403), calls=%async_computation.7 | async-start | bytes 1310720 | tf_op jit(solution)/shard_map/all_to_all | solution.py:27
  309.5 9.3 %collective-permute-start.17 = (bf16[64,256]{1,0:T(8,128)(2,1)S(1)}, bf16[64,256]{1,0:T(8,128)(2,1)S(1)}, u32[]{:S(2)}, u32[]{:S(2)}) collective-permute-start(bf16[64,256]{1,0:T(8,128)(2,1)S(1)} %get-tuple-element.87), channel_id=1, source_target_pairs={{0,192},{64,128},{128,64},{192,0},{1,193},{65,129},{129,65},{193,1... | collective-permute-start | bytes 98312 | tf_op jit(solution)/shard_map/ppermute | solution.py:39
  314.0 5.6 %collective-permute-start.16 = (bf16[64,256]{1,0:T(8,128)(2,1)S(1)}, bf16[64,256]{1,0:T(8,128)(2,1)S(1)}, u32[]{:S(2)}, u32[]{:S(2)}) collective-permute-start(bf16[64,256]{1,0:T(8,128)(2,1)S(1)} %get-tuple-element.88), channel_id=1, source_target_pairs={{0,128},{64,192},{128,0},{192,64},{1,129},{65,193},{129,1},{193,65... | collective-permute-start | bytes 98312 | tf_op jit(solution)/shard_map/ppermute | solution.py:39
  316.5 4.7 %collective-permute-start.15 = (bf16[64,256]{1,0:T(8,128)(2,1)S(1)}, bf16[64,256]{1,0:T(8,128)(2,1)S(1)}, u32[]{:S(2)}, u32[]{:S(2)}) collective-permute-start(bf16[64,256]{1,0:T(8,128)(2,1)S(1)} %get-tuple-element.86), channel_id=1, source_target_pairs={{0,64},{64,0},{128,192},{192,128},{1,65},{65,1},{129,193},{193,129... | collective-permute-start | bytes 98312 | tf_op jit(solution)/shard_map/ppermute | solution.py:39
  321.3 23.2 %collective-permute-start.18 = (bf16[32,256]{1,0:T(8,128)(2,1)S(1)}, bf16[32,256]{1,0:T(8,128)(2,1)S(1)}, u32[]{:S(2)}, u32[]{:S(2)}) collective-permute-start(bf16[32,256]{1,0:T(8,128)(2,1)S(1)} %fusion.58), channel_id=1, source_target_pairs={{0,8},{8,0},{1,9},{9,1},{2,10},{10,2},{3,11},{11,3},{4,12},{12,4},... | collective-permute-start | bytes 49160 | tf_op jit(solution)/shard_map/ppermute | solution.py:39
  (20 other events, 157.6 us)

commit v9 on v7

--- a/solution.py
+++ b/solution.py
@@ -220,7 +220,7 @@
     attended = attend(
         queries, segment[:, :HD], segment[:, HD:], key_positions(rows), ctx_index
     )
-    attended, flight = begin(attended, ("gate", 3), ("up", 3))
+    attended, flight = begin(attended, ("gate", 3))
 
     share_rows = attended.shape[0] // (NPLANE * NZ)
     attended = (
@@ -242,16 +242,13 @@
     routing = jnp.where(own_group, routing[None], 0).reshape(1, NZ * share_rows, HD)
     routing = jnp.broadcast_to(routing, (NCTX,) + routing.shape[1:])
     outgoing = jnp.concatenate([outgoing, routing], axis=2)
-    outgoing, flight = begin(outgoing, ("down", 1), ("down", 2))
+    outgoing, flight = begin(outgoing, ("up", 3), ("down", 1), ("down", 2))
     wide = feat + HD
     outgoing = jnp.broadcast_to(
         outgoing[:, None], (NCTX, NZ, NZ * share_rows, wide)
     ).reshape(NCTX * NZ, NZ * share_rows, wide)
     arrived = swap(outgoing, CTX + ("zh",)).reshape(NCTX, NZ, NZ * share_rows, wide)
-    weight_in = [
-        jnp.concatenate([moved[name, k] for k in range(NQ)], axis=0) for name in ("gate", "up")
-    ]
-    arrived, weight_in = lax.optimization_barrier((end(arrived, flight), weight_in))
+    arrived = end(arrived, flight)
     arrived = jnp.sum(arrived.astype(f32), axis=1)
     hidden = arrived[:, :, :feat].astype(bf16).reshape(-1, feat)
     routing = arrived[:, :, feat : feat + fields].reshape(-1, fields)
@@ -259,6 +256,10 @@
     token_count = expert_ids.shape[0]
 
     hidden = jnp.concatenate(from_peers([hidden] * NQ, "q", NQ), axis=1)
+    weight_in = [
+        jnp.concatenate([moved[name, k] for k in range(NQ)], axis=0) for name in ("gate", "up")
+    ]
+    hidden, weight_in = lax.optimization_barrier((hidden, weight_in))
     gain = jnp.concatenate(
         [
             lax.dynamic_slice_in_dim(

time: 344 us -> 346 us (level)
  blocking collectives: 33.8 us -> 45.1 us
  starting transfers between devices: 161 us -> 152 us
    all_to_all x1, blocking collectives: 33.8 us -> 45.1 us  [swap(): return lax.all_to_all(array, axes, split_axis=0, concat_axis=0, tiled=True)]
    all_to_all x6, starting transfers between devices: 81.2 us -> 71.3 us  [swap(): return lax.all_to_all(array, axes, split_axis=0, concat_axis=0, tiled=True)]
    ppermute x19, waiting for transfers between devices: 84.6 us -> 92 us  [from_peer(): return lax.ppermute(block, axis, [(i, i ^ k) for i in range(count)])]
    all_to_all x6, waiting for transfers between devices: 26.4 us -> 22.3 us  [swap(): return lax.all_to_all(array, axes, split_axis=0, concat_axis=0, tiled=True)]
  transfers between devices with their start and end apart: 25 -> 25, of which waited for: 16 -> 17; matrix products, arithmetic and copies ran while one was open for 3% -> 3% of each run, Pallas kernels for 0% -> 0%
where the time goes in v9:
time: 346 us; the launch traced here: 344 us
  starting transfers between devices  152 us (44%)
  waiting for transfers between devices  114 us (33%)
  blocking collectives  45.1 us (13%)
  local copies, waits for them, and re-layouts  17.5 us (5%)
  other arithmetic  6.52 us (2%)
  matrix products  4.38 us (1%)
  Pallas kernels  3.74 us (1%)
    ppermute x19, waiting for transfers between devices, from_peer(): return lax.ppermute(block, axis, [(i, i ^ k) for i in range(count)])  92 us
    ppermute x19, starting transfers between devices, from_peer(): return lax.ppermute(block, axis, [(i, i ^ k) for i in range(count)])  80.4 us
    all_to_all x6, starting transfers between devices, swap(): return lax.all_to_all(array, axes, split_axis=0, concat_axis=0, tiled=True)  71.3 us
    all_to_all x1, blocking collectives, swap(): return lax.all_to_all(array, axes, split_axis=0, concat_axis=0, tiled=True)  45.1 us
    all_to_all x6, waiting for transfers between devices, swap(): return lax.all_to_all(array, axes, split_axis=0, concat_axis=0, tiled=True)  22.3 us
  transfers between devices with their start and end apart: 25, of which 17 were waited for; matrix products, arithmetic and copies ran while one was open for 3% of the time, Pallas kernels for 0%

profile of v9, /device:TPU:1, one launch (start us, length us, event | category | flops | bytes accessed | tf_op | source)
XLA Modules:
  0.0 344.2 jit_solution(18079648463268163877)
XLA Ops:
  1.5 26.4 %all-to-all-start = ((bf16[16,16,256]{2,1,0:T(8,128)(2,1)}), bf16[16,16,256]{2,1,0:T(8,128)(2,1)S(1)}, u32[]{:S(2)}, u32[]{:S(2)}) async-start(bf16[16,16,256]{2,1,0:T(8,128)(2,1)} %broadcast_in_dim.146), calls=%async_computation | async-start | bytes 262144 | tf_op jit(solution)/shard_map/all_to_all | solution.py:27
  30.3 3.2 collective-permute-start
  35.6 4.1 %collective-permute-start.2 = (bf16[256,384]{1,0:T(8,128)(2,1)S(1)}, bf16[256,384]{1,0:T(8,128)(2,1)S(1)}, u32[]{:S(2)}, u32[]{:S(2)}) collective-permute-start(bf16[256,384]{1,0:T(8,128)(2,1)S(1)} %get-tuple-element.67), channel_id=1, source_target_pairs={{0,128},{64,192},{128,0},{192,64},{1,129},{65,193},{129,1},{193,65... | collective-permute-start | bytes 589832 | tf_op jit(solution)/shard_map/ppermute | solution.py:39
  39.7 8.0 %collective-permute-done.1 = bf16[256,384]{1,0:T(8,128)(2,1)S(1)} collective-permute-done((bf16[256,384]{1,0:T(8,128)(2,1)S(1)}, bf16[256,384]{1,0:T(8,128)(2,1)S(1)}, u32[]{:S(2)}, u32[]{:S(2)}) %collective-permute-start.1) | collective-permute-done | bytes 196640 | tf_op jit(solution)/shard_map/ppermute | solution.py:39
  50.9 7.1 %all-to-all-start.1 = ((bf16[8,16,16,256]{3,2,1,0:T(8,128)(2,1)}), bf16[8,16,16,256]{3,2,1,0:T(8,128)(2,1)S(1)}, u32[]{:S(2)}, u32[]{:S(2)}) async-start(bf16[8,16,16,256]{3,2,1,0:T(8,128)(2,1)} %broadcast_in_dim.147), calls=%async_computation.1 | async-start | bytes 2097152 | tf_op jit(solution)/shard_map/all_to_all | solution.py:27
  60.5 11.1 %collective-permute-done.3 = bf16[256,384]{1,0:T(8,128)(2,1)S(1)} collective-permute-done((bf16[256,384]{1,0:T(8,128)(2,1)S(1)}, bf16[256,384]{1,0:T(8,128)(2,1)S(1)}, u32[]{:S(2)}, u32[]{:S(2)}) %collective-permute-start.3) | collective-permute-done | bytes 196640 | tf_op jit(solution)/shard_map/ppermute | solution.py:39
  76.4 6.4 %all-to-all-start.2 = ((bf16[32,4,4096]{2,1,0:T(4,128)(2,1)}), bf16[32,4,4096]{2,1,0:T(4,128)(2,1)S(1)}, u32[]{:S(2)}, u32[]{:S(2)}) async-start(bf16[32,4,4096]{2,1,0:T(4,128)(2,1)} %reshape.335), calls=%async_computation.2 | async-start | bytes 2097152 | tf_op jit(solution)/shard_map/all_to_all | solution.py:27
  85.4 3.4 collective-permute-start.4
  88.9 6.7 %collective-permute-done.4 = bf16[256,384]{1,0:T(8,128)(2,1)S(1)} collective-permute-done((bf16[256,384]{1,0:T(8,128)(2,1)}, bf16[256,384]{1,0:T(8,128)(2,1)S(1)}, u32[]{:S(2)}, u32[]{:S(2)}) %collective-permute-start.4) | collective-permute-done | bytes 196640 | tf_op jit(solution)/shard_map/ppermute | solution.py:39
  95.6 4.1 %all-to-all-done.2 = bf16[32,4,4096]{2,1,0:T(4,128)(2,1)S(1)} async-done(((bf16[32,4,4096]{2,1,0:T(4,128)(2,1)}), bf16[32,4,4096]{2,1,0:T(4,128)(2,1)S(1)}, u32[]{:S(2)}, u32[]{:S(2)}) %all-to-all-start.2) | async-done | bytes 1048608 | tf_op jit(solution)/shard_map/all_to_all | solution.py:27
  101.0 16.3 %all-to-all-start.3 = ((bf16[32,4,384]{2,1,0:T(4,128)(2,1)}), bf16[32,4,384]{2,1,0:T(4,128)(2,1)S(1)}, u32[]{:S(2)}, u32[]{:S(2)}) async-start(bf16[32,4,384]{2,1,0:T(4,128)(2,1)} %bitcast.15), calls=%async_computation.3 | async-start | bytes 196608 | tf_op jit(solution)/shard_map/all_to_all | solution.py:27
  117.9 4.9 %collective-permute-start.5 = (bf16[256,384]{1,0:T(8,128)(2,1)S(1)}, bf16[256,384]{1,0:T(8,128)(2,1)S(1)}, u32[]{:S(2)}, u32[]{:S(2)}) collective-permute-start(bf16[256,384]{1,0:T(8,128)(2,1)S(1)} %get-tuple-element.40), channel_id=1, source_target_pairs={{0,192},{64,128},{128,64},{192,0},{1,193},{65,129},{129,65},{193,1... | collective-permute-start | bytes 589832 | tf_op jit(solution)/shard_map/ppermute | solution.py:39
  127.8 5.6 %collective-permute-done.5 = bf16[256,384]{1,0:T(8,128)(2,1)S(1)} collective-permute-done((bf16[256,384]{1,0:T(8,128)(2,1)S(1)}, bf16[256,384]{1,0:T(8,128)(2,1)S(1)}, u32[]{:S(2)}, u32[]{:S(2)}) %collective-permute-start.5) | collective-permute-done | bytes 196640 | tf_op jit(solution)/shard_map/ppermute | solution.py:39
  133.4 5.2 %collective-permute-done.6.refs_1_ = bf16[384,256]{1,0:T(8,128)(2,1)S(1)} collective-permute-done((bf16[384,256]{1,0:T(8,128)(2,1)}, bf16[384,256]{1,0:T(8,128)(2,1)S(1)}, u32[]{:S(2)}, u32[]{:S(2)}) %collective-permute-start.6) | collective-permute-done | bytes 196640 | tf_op jit(solution)/shard_map/ppermute | solution.py:39
  139.3 6.9 %collective-permute-done.7.refs_2_ = bf16[384,256]{1,0:T(8,128)(2,1)S(1)} collective-permute-done((bf16[384,256]{1,0:T(8,128)(2,1)}, bf16[384,256]{1,0:T(8,128)(2,1)S(1)}, u32[]{:S(2)}, u32[]{:S(2)}) %collective-permute-start.7) | collective-permute-done | bytes 196640 | tf_op jit(solution)/shard_map/ppermute | solution.py:39
  147.1 3.4 collective-permute-start.10
  152.5 3.9 %collective-permute-start.9 = (bf16[64,256]{1,0:T(8,128)(2,1)S(1)}, bf16[64,256]{1,0:T(8,128)(2,1)S(1)}, u32[]{:S(2)}, u32[]{:S(2)}) collective-permute-start(bf16[64,256]{1,0:T(8,128)(2,1)S(1)} %reshape.339), channel_id=1, source_target_pairs={{0,128},{64,192},{128,0},{192,64},{1,129},{65,193},{129,1},{193,65... | collective-permute-start | bytes 98312 | tf_op jit(solution)/shard_map/ppermute | solution.py:39
  162.0 9.5 %all-to-all-start.4 = ((bf16[32,80,128]{2,1,0:T(8,128)(2,1)}), bf16[32,80,128]{2,1,0:T(8,128)(2,1)}, u32[]{:S(2)}, u32[]{:S(2)}) async-start(bf16[32,80,128]{2,1,0:T(8,128)(2,1)} %reshape.343), calls=%async_computation.4 | async-start | bytes 1310720 | tf_op jit(solution)/shard_map/all_to_all | solution.py:27
  171.5 3.5 %collective-permute-start.11 = (bf16[384,256]{1,0:T(8,128)(2,1)}, bf16[384,256]{1,0:T(8,128)(2,1)S(1)}, u32[]{:S(2)}, u32[]{:S(2)}) collective-permute-start(bf16[384,256]{1,0:T(8,128)(2,1)} %get-tuple-element.52), channel_id=1, source_target_pairs={{0,192},{64,128},{128,64},{192,0},{1,193},{65,129},{129,65},{193,1... | collective-permute-start | bytes 589832 | tf_op jit(solution)/shard_map/ppermute | solution.py:39
  176.0 5.8 %collective-permute-done.11.refs_3_ = bf16[384,256]{1,0:T(8,128)(2,1)S(1)} collective-permute-done((bf16[384,256]{1,0:T(8,128)(2,1)}, bf16[384,256]{1,0:T(8,128)(2,1)S(1)}, u32[]{:S(2)}, u32[]{:S(2)}) %collective-permute-start.11) | collective-permute-done | bytes 196640 | tf_op jit(solution)/shard_map/ppermute | solution.py:39
  188.1 5.2 %collective-permute-start.12 = (bf16[496,128]{1,0:T(8,128)(2,1)S(1)}, bf16[496,128]{1,0:T(8,128)(2,1)S(1)}, u32[]{:S(2)}, u32[]{:S(2)}) collective-permute-start(bf16[496,128]{1,0:T(8,128)(2,1)S(1)} %get-tuple-element.75), channel_id=1, source_target_pairs={{0,256},{256,0},{512,768},{768,512},{1,257},{257,1},{513,769},{769... | collective-permute-start | bytes 380936 | tf_op jit(solution)/shard_map/ppermute | solution.py:39
  193.3 11.9 %collective-permute-start.13 = (bf16[496,128]{1,0:T(8,128)(2,1)S(1)}, bf16[496,128]{1,0:T(8,128)(2,1)S(1)}, u32[]{:S(2)}, u32[]{:S(2)}) collective-permute-start(bf16[496,128]{1,0:T(8,128)(2,1)S(1)} %get-tuple-element.77), channel_id=1, source_target_pairs={{0,512},{256,768},{512,0},{768,256},{1,513},{257,769},{513,1},{769... | collective-permute-start | bytes 380936 | tf_op jit(solution)/shard_map/ppermute | solution.py:39
  205.2 4.0 %collective-permute-start.14 = (bf16[496,128]{1,0:T(8,128)(2,1)S(1)}, bf16[496,128]{1,0:T(8,128)(2,1)S(1)}, u32[]{:S(2)}, u32[]{:S(2)}) collective-permute-start(bf16[496,128]{1,0:T(8,128)(2,1)S(1)} %get-tuple-element.76), channel_id=1, source_target_pairs={{0,768},{256,512},{512,256},{768,0},{1,769},{257,513},{513,257},{7... | collective-permute-start | bytes 380936 | tf_op jit(solution)/shard_map/ppermute | solution.py:39
  211.0 12.4 %collective-permute-done.13 = bf16[496,128]{1,0:T(8,128)(2,1)S(1)} collective-permute-done((bf16[496,128]{1,0:T(8,128)(2,1)S(1)}, bf16[496,128]{1,0:T(8,128)(2,1)S(1)}, u32[]{:S(2)}, u32[]{:S(2)}) %collective-permute-start.13) | collective-permute-done | bytes 127008 | tf_op jit(solution)/shard_map/ppermute | solution.py:39
  223.4 13.5 %collective-permute-done.14 = bf16[496,128]{1,0:T(8,128)(2,1)S(1)} collective-permute-done((bf16[496,128]{1,0:T(8,128)(2,1)S(1)}, bf16[496,128]{1,0:T(8,128)(2,1)S(1)}, u32[]{:S(2)}, u32[]{:S(2)}) %collective-permute-start.14) | collective-permute-done | bytes 127008 | tf_op jit(solution)/shard_map/ppermute | solution.py:39
  238.1 45.1 %all_to_all.35.activated_ref = bf16[4,3,80,128]{3,2,1,0:T(8,128)(2,1)S(1)} all-to-all(bf16[4,3,80,128]{3,2,1,0:T(8,128)(2,1)S(1)} %broadcast_in_dim.168), channel_id=1, replica_groups=mesh['p'=4,'q'=4,'x'=4,'zh'=2,'y'=4,'core'=2] {'p'}, dimensions={0} | all-to-all | bytes 491520 | tf_op jit(solution)/shard_map/all_to_all | solution.py:27
  286.7 5.5 %all-to-all-start.6 = ((bf16[32,80,128]{2,1,0:T(8,128)(2,1)}), bf16[32,80,128]{2,1,0:T(8,128)(2,1)S(1)}, u32[]{:S(2)}, u32[]{:S(2)}) async-start(bf16[32,80,128]{2,1,0:T(8,128)(2,1)} %reshape.346), calls=%async_computation.6 | async-start | bytes 1310720 | tf_op jit(solution)/shard_map/all_to_all | solution.py:27
  292.7 12.5 %all-to-all-done.6 = bf16[32,80,128]{2,1,0:T(8,128)(2,1)S(1)} async-done(((bf16[32,80,128]{2,1,0:T(8,128)(2,1)}), bf16[32,80,128]{2,1,0:T(8,128)(2,1)S(1)}, u32[]{:S(2)}, u32[]{:S(2)}) %all-to-all-start.6) | async-done | bytes 655392 | tf_op jit(solution)/shard_map/all_to_all | solution.py:27
  308.2 5.9 %collective-permute-start.16 = (bf16[64,256]{1,0:T(8,128)(2,1)S(1)}, bf16[64,256]{1,0:T(8,128)(2,1)S(1)}, u32[]{:S(2)}, u32[]{:S(2)}) collective-permute-start(bf16[64,256]{1,0:T(8,128)(2,1)S(1)} %get-tuple-element.82), channel_id=1, source_target_pairs={{0,128},{64,192},{128,0},{192,64},{1,129},{65,193},{129,1},{193,65... | collective-permute-start | bytes 98312 | tf_op jit(solution)/shard_map/ppermute | solution.py:39
  317.3 3.3 collective-permute-done.17
  320.7 11.2 %collective-permute-start.18 = (bf16[32,256]{1,0:T(8,128)(2,1)S(1)}, bf16[32,256]{1,0:T(8,128)(2,1)S(1)}, u32[]{:S(2)}, u32[]{:S(2)}) collective-permute-start(bf16[32,256]{1,0:T(8,128)(2,1)S(1)} %fusion.61), channel_id=1, source_target_pairs={{0,8},{8,0},{1,9},{9,1},{2,10},{10,2},{3,11},{11,3},{4,12},{12,4},... | collective-permute-start | bytes 49160 | tf_op jit(solution)/shard_map/ppermute | solution.py:39
  331.9 11.6 %collective-permute-done.18 = bf16[32,256]{1,0:T(8,128)(2,1)S(1)} collective-permute-done((bf16[32,256]{1,0:T(8,128)(2,1)S(1)}, bf16[32,256]{1,0:T(8,128)(2,1)S(1)}, u32[]{:S(2)}, u32[]{:S(2)}) %collective-permute-start.18) | collective-permute-done | bytes 16416 | tf_op jit(solution)/shard_map/ppermute | solution.py:39
  (146 shorter events, 55.3 us)
Async XLA Ops:
  0.0 74.8 %copy-start = (bf16[128,4096]{1,0:T(8,128)(2,1)S(1)}, bf16[128,4096]{1,0:T(8,128)(2,1)}, u32[]{:S(2)}) copy-start(bf16[128,4096]{1,0:T(8,128)(2,1)} %param.13) | copy-start | bytes 3145732
  1.5 48.4 %all-to-all-start = ((bf16[16,16,256]{2,1,0:T(8,128)(2,1)}), bf16[16,16,256]{2,1,0:T(8,128)(2,1)S(1)}, u32[]{:S(2)}, u32[]{:S(2)}) async-start(bf16[16,16,256]{2,1,0:T(8,128)(2,1)} %broadcast_in_dim.146), calls=%async_computation | async-start | bytes 262144 | tf_op jit(solution)/shard_map/all_to_all | solution.py:27
  30.3 9.4 %collective-permute-start = (bf16[256,384]{1,0:T(8,128)(2,1)S(1)}, bf16[256,384]{1,0:T(8,128)(2,1)S(1)}, u32[]{:S(2)}, u32[]{:S(2)}) collective-permute-start(bf16[256,384]{1,0:T(8,128)(2,1)S(1)} %get-tuple-element.69), channel_id=1, source_target_pairs={{0,64},{64,0},{128,192},{192,128},{1,65},{65,1},{129,193},{193,129... | collective-permute-start | bytes 589832 | tf_op jit(solution)/shard_map/ppermute | solution.py:39
  33.5 14.2 %collective-permute-start.1 = (bf16[256,384]{1,0:T(8,128)(2,1)S(1)}, bf16[256,384]{1,0:T(8,128)(2,1)S(1)}, u32[]{:S(2)}, u32[]{:S(2)}) collective-permute-start(bf16[256,384]{1,0:T(8,128)(2,1)S(1)} %get-tuple-element.68), channel_id=1, source_target_pairs={{0,64},{64,0},{128,192},{192,128},{1,65},{65,1},{129,193},{193,129... | collective-permute-start | bytes 589832 | tf_op jit(solution)/shard_map/ppermute | solution.py:39
  35.6 12.2 %collective-permute-start.2 = (bf16[256,384]{1,0:T(8,128)(2,1)S(1)}, bf16[256,384]{1,0:T(8,128)(2,1)S(1)}, u32[]{:S(2)}, u32[]{:S(2)}) collective-permute-start(bf16[256,384]{1,0:T(8,128)(2,1)S(1)} %get-tuple-element.67), channel_id=1, source_target_pairs={{0,128},{64,192},{128,0},{192,64},{1,129},{65,193},{129,1},{193,65... | collective-permute-start | bytes 589832 | tf_op jit(solution)/shard_map/ppermute | solution.py:39
  49.8 23.3 %copy-start.21 = (bf16[128,128]{1,0:T(8,128)(2,1)S(1)}, bf16[128,128]{1,0:T(8,128)(2,1)}, u32[]{:S(2)}) copy-start(bf16[128,128]{1,0:T(8,128)(2,1)} %param.9) | copy-start | bytes 98308
  50.9 22.2 %all-to-all-start.1 = ((bf16[8,16,16,256]{3,2,1,0:T(8,128)(2,1)}), bf16[8,16,16,256]{3,2,1,0:T(8,128)(2,1)S(1)}, u32[]{:S(2)}, u32[]{:S(2)}) async-start(bf16[8,16,16,256]{3,2,1,0:T(8,128)(2,1)} %broadcast_in_dim.147), calls=%async_computation.1 | async-start | bytes 2097152 | tf_op jit(solution)/shard_map/all_to_all | solution.py:27
  58.1 13.5 %collective-permute-start.3 = (bf16[256,384]{1,0:T(8,128)(2,1)S(1)}, bf16[256,384]{1,0:T(8,128)(2,1)S(1)}, u32[]{:S(2)}, u32[]{:S(2)}) collective-permute-start(bf16[256,384]{1,0:T(8,128)(2,1)S(1)} %get-tuple-element.34), channel_id=1, source_target_pairs={{0,128},{64,192},{128,0},{192,64},{1,129},{65,193},{129,1},{193,65... | collective-permute-start | bytes 589832 | tf_op jit(solution)/shard_map/ppermute | solution.py:39
  76.4 23.3 %all-to-all-start.2 = ((bf16[32,4,4096]{2,1,0:T(4,128)(2,1)}), bf16[32,4,4096]{2,1,0:T(4,128)(2,1)S(1)}, u32[]{:S(2)}, u32[]{:S(2)}) async-start(bf16[32,4,4096]{2,1,0:T(4,128)(2,1)} %reshape.335), calls=%async_computation.2 | async-start | bytes 2097152 | tf_op jit(solution)/shard_map/all_to_all | solution.py:27
  85.4 10.2 %collective-permute-start.4 = (bf16[256,384]{1,0:T(8,128)(2,1)}, bf16[256,384]{1,0:T(8,128)(2,1)S(1)}, u32[]{:S(2)}, u32[]{:S(2)}) collective-permute-start(bf16[256,384]{1,0:T(8,128)(2,1)} %get-tuple-element.37), channel_id=1, source_target_pairs={{0,192},{64,128},{128,64},{192,0},{1,193},{65,129},{129,65},{193,1... | collective-permute-start | bytes 589832 | tf_op jit(solution)/shard_map/ppermute | solution.py:39
  95.6 61.5 %copy-start.12 = (bf16[256,384]{1,0:T(8,128)(2,1)}, bf16[256,384]{1,0:T(8,128)(2,1)S(1)}, u32[]{:S(2)}) copy-start(bf16[256,384]{1,0:T(8,128)(2,1)S(1)} %collective-permute-done.4) | copy-start | bytes 589828
  101.0 45.9 %all-to-all-start.3 = ((bf16[32,4,384]{2,1,0:T(4,128)(2,1)}), bf16[32,4,384]{2,1,0:T(4,128)(2,1)S(1)}, u32[]{:S(2)}, u32[]{:S(2)}) async-start(bf16[32,4,384]{2,1,0:T(4,128)(2,1)} %bitcast.15), calls=%async_computation.3 | async-start | bytes 196608 | tf_op jit(solution)/shard_map/all_to_all | solution.py:27
  117.9 15.5 %collective-permute-start.5 = (bf16[256,384]{1,0:T(8,128)(2,1)S(1)}, bf16[256,384]{1,0:T(8,128)(2,1)S(1)}, u32[]{:S(2)}, u32[]{:S(2)}) collective-permute-start(bf16[256,384]{1,0:T(8,128)(2,1)S(1)} %get-tuple-element.40), channel_id=1, source_target_pairs={{0,192},{64,128},{128,64},{192,0},{1,193},{65,129},{129,65},{193,1... | collective-permute-start | bytes 589832 | tf_op jit(solution)/shard_map/ppermute | solution.py:39
  122.8 15.8 %collective-permute-start.6 = (bf16[384,256]{1,0:T(8,128)(2,1)}, bf16[384,256]{1,0:T(8,128)(2,1)S(1)}, u32[]{:S(2)}, u32[]{:S(2)}) collective-permute-start(bf16[384,256]{1,0:T(8,128)(2,1)} %get-tuple-element.41), channel_id=1, source_target_pairs={{0,64},{64,0},{128,192},{192,128},{1,65},{65,1},{129,193},{193,129... | collective-permute-start | bytes 589832 | tf_op jit(solution)/shard_map/ppermute | solution.py:39
  124.8 21.5 %collective-permute-start.7 = (bf16[384,256]{1,0:T(8,128)(2,1)}, bf16[384,256]{1,0:T(8,128)(2,1)S(1)}, u32[]{:S(2)}, u32[]{:S(2)}) collective-permute-start(bf16[384,256]{1,0:T(8,128)(2,1)} %get-tuple-element.42), channel_id=1, source_target_pairs={{0,128},{64,192},{128,0},{192,64},{1,129},{65,193},{129,1},{193,65... | collective-permute-start | bytes 589832 | tf_op jit(solution)/shard_map/ppermute | solution.py:39
  127.2 29.9 %copy-start.20 = (s32[64]{0:T(128)}, s32[64]{0:T(128)S(1)}, u32[]{:S(2)}) copy-start(s32[64]{0:T(128)S(1)} %and_select_fusion) | copy-start | bytes 772
  147.1 11.6 %collective-permute-start.10 = (bf16[64,256]{1,0:T(8,128)(2,1)S(1)}, bf16[64,256]{1,0:T(8,128)(2,1)S(1)}, u32[]{:S(2)}, u32[]{:S(2)}) collective-permute-start(bf16[64,256]{1,0:T(8,128)(2,1)S(1)} %reshape.339), channel_id=1, source_target_pairs={{0,192},{64,128},{128,64},{192,0},{1,193},{65,129},{129,65},{193,1... | collective-permute-start | bytes 98312 | tf_op jit(solution)/shard_map/ppermute | solution.py:39
  150.5 8.1 %collective-permute-start.8 = (bf16[64,256]{1,0:T(8,128)(2,1)S(1)}, bf16[64,256]{1,0:T(8,128)(2,1)S(1)}, u32[]{:S(2)}, u32[]{:S(2)}) collective-permute-start(bf16[64,256]{1,0:T(8,128)(2,1)S(1)} %reshape.339), channel_id=1, source_target_pairs={{0,64},{64,0},{128,192},{192,128},{1,65},{65,1},{129,193},{193,129... | collective-permute-start | bytes 98312 | tf_op jit(solution)/shard_map/ppermute | solution.py:39
  152.5 6.2 %collective-permute-start.9 = (bf16[64,256]{1,0:T(8,128)(2,1)S(1)}, bf16[64,256]{1,0:T(8,128)(2,1)S(1)}, u32[]{:S(2)}, u32[]{:S(2)}) collective-permute-start(bf16[64,256]{1,0:T(8,128)(2,1)S(1)} %reshape.339), channel_id=1, source_target_pairs={{0,128},{64,192},{128,0},{192,64},{1,129},{65,193},{129,1},{193,65... | collective-permute-start | bytes 98312 | tf_op jit(solution)/shard_map/ppermute | solution.py:39
  162.0 22.5 %all-to-all-start.4 = ((bf16[32,80,128]{2,1,0:T(8,128)(2,1)}), bf16[32,80,128]{2,1,0:T(8,128)(2,1)}, u32[]{:S(2)}, u32[]{:S(2)}) async-start(bf16[32,80,128]{2,1,0:T(8,128)(2,1)} %reshape.343), calls=%async_computation.4 | async-start | bytes 1310720 | tf_op jit(solution)/shard_map/all_to_all | solution.py:27
  171.5 10.3 %collective-permute-start.11 = (bf16[384,256]{1,0:T(8,128)(2,1)}, bf16[384,256]{1,0:T(8,128)(2,1)S(1)}, u32[]{:S(2)}, u32[]{:S(2)}) collective-permute-start(bf16[384,256]{1,0:T(8,128)(2,1)} %get-tuple-element.52), channel_id=1, source_target_pairs={{0,192},{64,128},{128,64},{192,0},{1,193},{65,129},{129,65},{193,1... | collective-permute-start | bytes 589832 | tf_op jit(solution)/shard_map/ppermute | solution.py:39
  188.1 95.2 %copy-start.3 = (bf16[384,256]{1,0:T(8,128)(2,1)S(1)}, bf16[384,256]{1,0:T(8,128)(2,1)}, u32[]{:S(2)}) copy-start(bf16[384,256]{1,0:T(8,128)(2,1)} %copy-done.2) | copy-start | bytes 589828
  188.1 95.2 %copy-start.5 = (bf16[384,256]{1,0:T(8,128)(2,1)S(1)}, bf16[384,256]{1,0:T(8,128)(2,1)}, u32[]{:S(2)}) copy-start(bf16[384,256]{1,0:T(8,128)(2,1)} %copy-done.4) | copy-start | bytes 589828
  188.1 95.2 %copy-start.7 = (bf16[384,256]{1,0:T(8,128)(2,1)S(1)}, bf16[384,256]{1,0:T(8,128)(2,1)}, u32[]{:S(2)}) copy-start(bf16[384,256]{1,0:T(8,128)(2,1)} %copy-done.6) | copy-start | bytes 589828
  188.1 22.9 %collective-permute-start.12 = (bf16[496,128]{1,0:T(8,128)(2,1)S(1)}, bf16[496,128]{1,0:T(8,128)(2,1)S(1)}, u32[]{:S(2)}, u32[]{:S(2)}) collective-permute-start(bf16[496,128]{1,0:T(8,128)(2,1)S(1)} %get-tuple-element.75), channel_id=1, source_target_pairs={{0,256},{256,0},{512,768},{768,512},{1,257},{257,1},{513,769},{769... | collective-permute-start | bytes 380936 | tf_op jit(solution)/shard_map/ppermute | solution.py:39
  193.3 30.1 %collective-permute-start.13 = (bf16[496,128]{1,0:T(8,128)(2,1)S(1)}, bf16[496,128]{1,0:T(8,128)(2,1)S(1)}, u32[]{:S(2)}, u32[]{:S(2)}) collective-permute-start(bf16[496,128]{1,0:T(8,128)(2,1)S(1)} %get-tuple-element.77), channel_id=1, source_target_pairs={{0,512},{256,768},{512,0},{768,256},{1,513},{257,769},{513,1},{769... | collective-permute-start | bytes 380936 | tf_op jit(solution)/shard_map/ppermute | solution.py:39
  205.2 31.7 %collective-permute-start.14 = (bf16[496,128]{1,0:T(8,128)(2,1)S(1)}, bf16[496,128]{1,0:T(8,128)(2,1)S(1)}, u32[]{:S(2)}, u32[]{:S(2)}) collective-permute-start(bf16[496,128]{1,0:T(8,128)(2,1)S(1)} %get-tuple-element.76), channel_id=1, source_target_pairs={{0,768},{256,512},{512,256},{768,0},{1,769},{257,513},{513,257},{7... | collective-permute-start | bytes 380936 | tf_op jit(solution)/shard_map/ppermute | solution.py:39
  286.7 18.5 %all-to-all-start.6 = ((bf16[32,80,128]{2,1,0:T(8,128)(2,1)}), bf16[32,80,128]{2,1,0:T(8,128)(2,1)S(1)}, u32[]{:S(2)}, u32[]{:S(2)}) async-start(bf16[32,80,128]{2,1,0:T(8,128)(2,1)} %reshape.346), calls=%async_computation.6 | async-start | bytes 1310720 | tf_op jit(solution)/shard_map/all_to_all | solution.py:27
  306.3 11.0 %collective-permute-start.15 = (bf16[64,256]{1,0:T(8,128)(2,1)S(1)}, bf16[64,256]{1,0:T(8,128)(2,1)S(1)}, u32[]{:S(2)}, u32[]{:S(2)}) collective-permute-start(bf16[64,256]{1,0:T(8,128)(2,1)S(1)} %get-tuple-element.80), channel_id=1, source_target_pairs={{0,64},{64,0},{128,192},{192,128},{1,65},{65,1},{129,193},{193,129... | collective-permute-start | bytes 98312 | tf_op jit(solution)/shard_map/ppermute | solution.py:39
  308.2 9.1 %collective-permute-start.16 = (bf16[64,256]{1,0:T(8,128)(2,1)S(1)}, bf16[64,256]{1,0:T(8,128)(2,1)S(1)}, u32[]{:S(2)}, u32[]{:S(2)}) collective-permute-start(bf16[64,256]{1,0:T(8,128)(2,1)S(1)} %get-tuple-element.82), channel_id=1, source_target_pairs={{0,128},{64,192},{128,0},{192,64},{1,129},{65,193},{129,1},{193,65... | collective-permute-start | bytes 98312 | tf_op jit(solution)/shard_map/ppermute | solution.py:39
  314.1 6.5 %collective-permute-start.17 = (bf16[64,256]{1,0:T(8,128)(2,1)S(1)}, bf16[64,256]{1,0:T(8,128)(2,1)S(1)}, u32[]{:S(2)}, u32[]{:S(2)}) collective-permute-start(bf16[64,256]{1,0:T(8,128)(2,1)S(1)} %get-tuple-element.81), channel_id=1, source_target_pairs={{0,192},{64,128},{128,64},{192,0},{1,193},{65,129},{129,65},{193,1... | collective-permute-start | bytes 98312 | tf_op jit(solution)/shard_map/ppermute | solution.py:39
  320.7 22.9 %collective-permute-start.18 = (bf16[32,256]{1,0:T(8,128)(2,1)S(1)}, bf16[32,256]{1,0:T(8,128)(2,1)S(1)}, u32[]{:S(2)}, u32[]{:S(2)}) collective-permute-start(bf16[32,256]{1,0:T(8,128)(2,1)S(1)} %fusion.61), channel_id=1, source_target_pairs={{0,8},{8,0},{1,9},{9,1},{2,10},{10,2},{3,11},{11,3},{4,12},{12,4},... | collective-permute-start | bytes 49160 | tf_op jit(solution)/shard_map/ppermute | solution.py:39
  (16 other events, 76.2 us)
